TPU v7x, 32 devices: a whole 2x2x4 slice. The times are simulated.
32 devices in a mesh: dp: 16 (over z, x, core), tensor: 2 (over y).
Axes of the slice: x: 2, y: 2, z: 4, core: 2. Of those that a mesh axis runs over, the one named last changes fastest.
Arguments:
- inputs: bfloat16 [16, 1500, 1536], P('dp', 'tensor'), may hold values from -16 to 16
- text_states: bfloat16 [16, 64, 1536], P('dp'), may hold values from -4 to 4
- teacher: bfloat16 [16, 1500, 1536], P('dp', 'tensor'), may hold values from -16 to 16
- valid_frames: int32 [16, 1500], P('dp', 'tensor'), may hold values from 0 to 1, as said below
- self_norm_gain: bfloat16 [1536], P('dp'), may hold values from 0.5 to 1.5
- self_norm_bias: bfloat16 [1536], P('dp'), may hold values from -0.25 to 0.25
- self_query: bfloat16 [1536, 1536], P('dp', 'tensor'), may hold values from -0.15625 to 0.15625
- self_key: bfloat16 [1536, 1536], P('dp', 'tensor'), may hold values from -0.15625 to 0.15625
- self_value: bfloat16 [1536, 1536], P('dp', 'tensor'), may hold values from -0.15625 to 0.15625
- self_out: bfloat16 [1536, 1536], P('tensor', 'dp'), may hold values from -0.875 to 0.875
- cross_norm_gain: bfloat16 [1536], P('dp'), may hold values from 0.5 to 1.5
- cross_norm_bias: bfloat16 [1536], P('dp'), may hold values from -0.25 to 0.25
- cross_query: bfloat16 [1536, 1536], P('dp', 'tensor'), may hold values from -0.15625 to 0.15625
- cross_key: bfloat16 [1536, 1536], P('dp', 'tensor'), may hold values from -0.15625 to 0.15625
- cross_value: bfloat16 [1536, 1536], P('dp', 'tensor'), may hold values from -0.15625 to 0.15625
- cross_out: bfloat16 [1536, 1536], P('tensor', 'dp'), may hold values from -1.25 to 1.25
- feed_norm_gain: bfloat16 [1536], P('dp'), may hold values from 0.5 to 1.5
- feed_norm_bias: bfloat16 [1536], P('dp'), may hold values from -0.25 to 0.25
- feed_in: bfloat16 [1536, 6144], P('dp', 'tensor'), may hold values from -0.15625 to 0.15625
- feed_out: bfloat16 [6144, 1536], P('tensor', 'dp'), may hold values from -0.15625 to 0.15625
Outputs:
- distill_loss: float32 [], replicated
- layer_out: bfloat16 [16, 1500, 1536], P('dp', 'tensor')
- inputs_grad: float32 [16, 1500, 1536], P('dp', 'tensor')
- text_grad: float32 [16, 64, 1536], P('dp', None, 'tensor')
- self_norm_gain_grad: float32 [1536], P(('dp', 'tensor'))
- self_norm_bias_grad: float32 [1536], P(('dp', 'tensor'))
- self_query_grad: float32 [1536, 1536], P('dp', 'tensor')
- self_key_grad: float32 [1536, 1536], P('dp', 'tensor')
- self_value_grad: float32 [1536, 1536], P('dp', 'tensor')
- self_out_grad: float32 [1536, 1536], P('tensor', 'dp')
- cross_norm_gain_grad: float32 [1536], P(('dp', 'tensor'))
- cross_norm_bias_grad: float32 [1536], P(('dp', 'tensor'))
- cross_query_grad: float32 [1536, 1536], P('dp', 'tensor')
- cross_key_grad: float32 [1536, 1536], P('dp', 'tensor')
- cross_value_grad: float32 [1536, 1536], P('dp', 'tensor')
- cross_out_grad: float32 [1536, 1536], P('tensor', 'dp')
- feed_norm_gain_grad: float32 [1536], P(('dp', 'tensor'))
- feed_norm_bias_grad: float32 [1536], P(('dp', 'tensor'))
- feed_in_grad: float32 [1536, 6144], P('dp', 'tensor')
- feed_out_grad: float32 [6144, 1536], P('tensor', 'dp')
Inputs may be any that keep to these rules, and one draw needn't show every extreme that they name: `valid_frames`: in each clip the valid frames form a prefix of at least 250 frames; the last clip is valid throughout.
All inputs are finite; a program needn't handle non-finite values.
Results may differ from a plain program's by a relative error of at most 0.02.
Values may be sent and summed in bfloat16 or wider, within the bound.
A program may use at most 512 MiB of HBM per device.

v0:
```python
import jax
import jax.numpy as jnp
from jax import lax
from jax.sharding import PartitionSpec as P

HEAD_DIM = 64


FLOAT = jnp.float32
BRAIN = jnp.bfloat16
NEGATIVE = -1e30
EPSILON = 1e-05


def normalize(values, gain_vec, bias_vec):
    center = values - jnp.mean(values, -1, keepdims=True)
    spread = jnp.mean(center * center, -1, keepdims=True)
    return center * lax.rsqrt(spread + EPSILON) * gain_vec + bias_vec


def norm_back(values, gain_vec, grads):
    center = values - jnp.mean(values, -1, keepdims=True)
    scale_row = lax.rsqrt(jnp.mean(center * center, -1, keepdims=True) + EPSILON)
    normal = center * scale_row
    scaled = grads * gain_vec.astype(FLOAT)
    inner = jnp.mean(scaled * normal, -1, keepdims=True)
    grad_values = scale_row * (scaled - jnp.mean(scaled, -1, keepdims=True) - normal * inner)
    gain_grad = jnp.sum(grads * normal, axis=(0, 1))
    bias_grad = jnp.sum(grads, axis=(0, 1))
    return (grad_values, gain_grad, bias_grad)


def gelu_exact(values):
    return jax.nn.gelu(values, approximate=False)


def project(left, weight):
    return jnp.dot(left, weight, preferred_element_type=FLOAT)


def project_back(grads, weight):
    return jnp.einsum("cse,de->csd", grads, weight, preferred_element_type=FLOAT)


def weight_grad(left, right):
    return jnp.einsum("csd,cse->de", left, right, preferred_element_type=FLOAT)


def split_heads(values):
    return values.reshape(values.shape[0], values.shape[1], -1, HEAD_DIM)


def merge_heads(values):
    return values.reshape(values.shape[0], values.shape[1], -1)


def gather_frames(values):
    return lax.all_gather(values, "tensor", axis=1, tiled=True)


def scatter_frames(values):
    return lax.psum_scatter(
        values.astype(jnp.bfloat16), "tensor", scatter_dimension=1, tiled=True
    ).astype(jnp.float32)


def gather_grads(values):
    return lax.all_gather(values, "tensor", axis=1, tiled=True)


def scatter_grads(values):
    return lax.psum_scatter(
        values.astype(jnp.bfloat16), "tensor", scatter_dimension=1, tiled=True
    ).astype(jnp.float32)


def scores_of(queries, keys_in, score_scale, start_row):
    scores = (
        jnp.einsum("cqhd,ckhd->chqk", queries, keys_in, preferred_element_type=FLOAT) * score_scale
    )
    if start_row is None:
        return scores
    row_index = start_row + jnp.arange(queries.shape[1])[:, None]
    key_index = jnp.arange(keys_in.shape[1])[None, :]
    return jnp.where(key_index <= row_index, scores, NEGATIVE)


def attend(queries, keys_in, values_in, score_scale, start_row):
    scores = scores_of(queries, keys_in, score_scale, start_row)
    row_max = jnp.max(scores, -1, keepdims=True)
    exponent = jnp.exp(scores - row_max)
    row_total = jnp.sum(exponent, -1, keepdims=True)
    probs = exponent / row_total
    output = jnp.einsum(
        "chqk,ckhd->cqhd", probs.astype(BRAIN), values_in, preferred_element_type=FLOAT
    )
    return (output, (row_max + jnp.log(row_total))[..., 0])


def attend_back(queries, keys_in, values_in, grads_out, logsum, score_scale, start_row):
    scores = scores_of(queries, keys_in, score_scale, start_row)
    probs = jnp.exp(scores - logsum[..., None])
    grad_probs = jnp.einsum("cqhd,ckhd->chqk", grads_out, values_in, preferred_element_type=FLOAT)
    row_inner = jnp.sum(probs * grad_probs, -1, keepdims=True)
    grad_scores = (probs * (grad_probs - row_inner)).astype(BRAIN)
    grad_queries = (
        jnp.einsum("chqk,ckhd->cqhd", grad_scores, keys_in, preferred_element_type=FLOAT)
        * score_scale
    )
    grad_keys = (
        jnp.einsum("chqk,cqhd->ckhd", grad_scores, queries, preferred_element_type=FLOAT)
        * score_scale
    )
    grad_values = jnp.einsum(
        "chqk,cqhd->ckhd", probs.astype(BRAIN), grads_out, preferred_element_type=FLOAT
    )
    return (grad_queries, grad_keys, grad_values)


def self_attend(queries, keys_in, values_in, score_scale):
    rows_block = queries.shape[1] // 2
    outputs = []
    logsums = []
    for number in range(2):
        first_row = number * rows_block
        last_row = first_row + rows_block
        output, logsum = attend(
            queries[:, first_row:last_row],
            keys_in[:, :last_row],
            values_in[:, :last_row],
            score_scale,
            first_row,
        )
        outputs.append(output)
        logsums.append(logsum)
    return (jnp.concatenate(outputs, 1), jnp.concatenate(logsums, 2))


def self_attend_back(queries, keys_in, values_in, grads_out, logsum, score_scale):
    rows_block = queries.shape[1] // 2
    grad_keys = jnp.zeros(keys_in.shape, FLOAT)
    grad_values = jnp.zeros(values_in.shape, FLOAT)
    pieces = []
    for number in range(2):
        first_row = number * rows_block
        last_row = first_row + rows_block
        piece_queries, piece_keys, piece_values = attend_back(
            queries[:, first_row:last_row],
            keys_in[:, :last_row],
            values_in[:, :last_row],
            grads_out[:, first_row:last_row],
            logsum[:, :, first_row:last_row],
            score_scale,
            first_row,
        )
        pieces.append(piece_queries)
        grad_keys = grad_keys.at[:, :last_row].add(piece_keys)
        grad_values = grad_values.at[:, :last_row].add(piece_values)
    return (jnp.concatenate(pieces, 1), grad_keys, grad_values)


def on_device(
    inputs,
    text_states,
    teacher,
    valid_frames,
    self_norm_gain,
    self_norm_bias,
    self_query,
    self_key,
    self_value,
    self_out,
    cross_norm_gain,
    cross_norm_bias,
    cross_query,
    cross_key,
    cross_value,
    cross_out,
    feed_norm_gain,
    feed_norm_bias,
    feed_in,
    feed_out,
):
    (
        gain_self,
        bias_self,
        gain_cross,
        bias_cross,
        gain_feed,
        bias_feed,
        query_self,
        key_self,
        value_self,
        query_cross,
        key_cross,
        value_cross,
        feed_first,
        out_self,
        out_cross,
        feed_second,
    ) = (
        lax.all_gather(self_norm_gain, "dp", axis=0, tiled=True),
        lax.all_gather(self_norm_bias, "dp", axis=0, tiled=True),
        lax.all_gather(cross_norm_gain, "dp", axis=0, tiled=True),
        lax.all_gather(cross_norm_bias, "dp", axis=0, tiled=True),
        lax.all_gather(feed_norm_gain, "dp", axis=0, tiled=True),
        lax.all_gather(feed_norm_bias, "dp", axis=0, tiled=True),
        lax.all_gather(self_query, "dp", axis=0, tiled=True),
        lax.all_gather(self_key, "dp", axis=0, tiled=True),
        lax.all_gather(self_value, "dp", axis=0, tiled=True),
        lax.all_gather(cross_query, "dp", axis=0, tiled=True),
        lax.all_gather(cross_key, "dp", axis=0, tiled=True),
        lax.all_gather(cross_value, "dp", axis=0, tiled=True),
        lax.all_gather(feed_in, "dp", axis=0, tiled=True),
        lax.all_gather(self_out, "dp", axis=1, tiled=True),
        lax.all_gather(cross_out, "dp", axis=1, tiled=True),
        lax.all_gather(feed_out, "dp", axis=1, tiled=True),
    )
    score_scale = HEAD_DIM ** (-0.5)
    token_count = lax.psum(jnp.sum(valid_frames).astype(FLOAT), ("dp", "tensor"))
    residual_in = inputs.astype(FLOAT)
    normed_self = normalize(residual_in, gain_self.astype(FLOAT), bias_self.astype(FLOAT)).astype(
        BRAIN
    )
    frames_self = gather_frames(normed_self)
    self_queries = project(frames_self, query_self).astype(BRAIN)
    self_keys = project(frames_self, key_self).astype(BRAIN)
    self_values = project(frames_self, value_self).astype(BRAIN)
    mixed_self, logsum_self = self_attend(
        split_heads(self_queries), split_heads(self_keys), split_heads(self_values), score_scale
    )
    mixed_self = merge_heads(mixed_self).astype(BRAIN)
    after_self = residual_in + scatter_frames(project(mixed_self, out_self))
    normed_cross = normalize(after_self, gain_cross.astype(FLOAT), bias_cross.astype(FLOAT)).astype(
        BRAIN
    )
    frames_cross = gather_frames(normed_cross)
    cross_queries = project(frames_cross, query_cross).astype(BRAIN)
    cross_keys = project(text_states, key_cross).astype(BRAIN)
    cross_values = project(text_states, value_cross).astype(BRAIN)
    mixed_cross, logsum_cross = attend(
        split_heads(cross_queries),
        split_heads(cross_keys),
        split_heads(cross_values),
        score_scale,
        None,
    )
    mixed_cross = merge_heads(mixed_cross).astype(BRAIN)
    after_cross = after_self + scatter_frames(project(mixed_cross, out_cross))
    normed_feed = normalize(after_cross, gain_feed.astype(FLOAT), bias_feed.astype(FLOAT)).astype(
        BRAIN
    )
    frames_feed = gather_frames(normed_feed)
    hidden_pre = project(frames_feed, feed_first)
    hidden_act = gelu_exact(hidden_pre).astype(BRAIN)
    result = after_cross + scatter_frames(project(hidden_act, feed_second))
    layer_out = result.astype(BRAIN)
    valid_float = valid_frames.astype(FLOAT)[..., None]
    deviation = result - teacher.astype(FLOAT)
    error_total = lax.psum(jnp.sum(valid_float * deviation * deviation), ("dp", "tensor"))
    model_width = inputs.shape[2]
    distill_loss = error_total / (model_width * token_count)
    tokens_all = inputs.shape[0] * inputs.shape[1] * lax.axis_size("dp") * lax.axis_size("tensor")
    grad_result = 2.0 * tokens_all / token_count * valid_float * deviation
    (
        gain_self,
        bias_self,
        gain_cross,
        bias_cross,
        gain_feed,
        bias_feed,
        query_self,
        key_self,
        value_self,
        query_cross,
        key_cross,
        value_cross,
        feed_first,
        out_self,
        out_cross,
        feed_second,
    ) = (
        lax.all_gather(self_norm_gain, "dp", axis=0, tiled=True),
        lax.all_gather(self_norm_bias, "dp", axis=0, tiled=True),
        lax.all_gather(cross_norm_gain, "dp", axis=0, tiled=True),
        lax.all_gather(cross_norm_bias, "dp", axis=0, tiled=True),
        lax.all_gather(feed_norm_gain, "dp", axis=0, tiled=True),
        lax.all_gather(feed_norm_bias, "dp", axis=0, tiled=True),
        lax.all_gather(self_query, "dp", axis=0, tiled=True),
        lax.all_gather(self_key, "dp", axis=0, tiled=True),
        lax.all_gather(self_value, "dp", axis=0, tiled=True),
        lax.all_gather(cross_query, "dp", axis=0, tiled=True),
        lax.all_gather(cross_key, "dp", axis=0, tiled=True),
        lax.all_gather(cross_value, "dp", axis=0, tiled=True),
        lax.all_gather(feed_in, "dp", axis=0, tiled=True),
        lax.all_gather(self_out, "dp", axis=1, tiled=True),
        lax.all_gather(cross_out, "dp", axis=1, tiled=True),
        lax.all_gather(feed_out, "dp", axis=1, tiled=True),
    )
    grad_branch = gather_grads(grad_result.astype(BRAIN))
    feed_second_grad = weight_grad(hidden_act, grad_branch)
    grad_act = project_back(grad_branch, feed_second)
    gelu_pullback = jax.vjp(gelu_exact, hidden_pre)[1]
    grad_pre = gelu_pullback(grad_act)[0].astype(BRAIN)
    feed_first_grad = weight_grad(frames_feed, grad_pre)
    grad_normed = scatter_grads(project_back(grad_pre, feed_first))
    grad_norm_term, feed_gain_grad, feed_bias_grad = norm_back(after_cross, gain_feed, grad_normed)
    grad_after_cross = grad_result + grad_norm_term
    grad_branch = gather_grads(grad_after_cross.astype(BRAIN))
    cross_out_grad = weight_grad(mixed_cross, grad_branch)
    grad_mixed = project_back(grad_branch, out_cross).astype(BRAIN)
    grad_queries, grad_keys, grad_values = attend_back(
        split_heads(cross_queries),
        split_heads(cross_keys),
        split_heads(cross_values),
        split_heads(grad_mixed),
        logsum_cross,
        score_scale,
        None,
    )
    grad_queries = merge_heads(grad_queries).astype(BRAIN)
    grad_keys = merge_heads(grad_keys).astype(BRAIN)
    grad_values = merge_heads(grad_values).astype(BRAIN)
    cross_query_grad = weight_grad(frames_cross, grad_queries)
    cross_key_grad = weight_grad(text_states, grad_keys)
    cross_value_grad = weight_grad(text_states, grad_values)
    text_part = project_back(grad_keys, key_cross) + project_back(grad_values, value_cross)
    text_grad = lax.psum_scatter(
        text_part.astype(jnp.bfloat16), "tensor", scatter_dimension=2, tiled=True
    ).astype(jnp.float32)
    grad_normed = scatter_grads(project_back(grad_queries, query_cross))
    grad_norm_term, cross_gain_grad, cross_bias_grad = norm_back(
        after_self, gain_cross, grad_normed
    )
    grad_after_self = grad_after_cross + grad_norm_term
    grad_branch = gather_grads(grad_after_self.astype(BRAIN))
    self_out_grad = weight_grad(mixed_self, grad_branch)
    grad_mixed = project_back(grad_branch, out_self).astype(BRAIN)
    grad_queries, grad_keys, grad_values = self_attend_back(
        split_heads(self_queries),
        split_heads(self_keys),
        split_heads(self_values),
        split_heads(grad_mixed),
        logsum_self,
        score_scale,
    )
    grad_queries = merge_heads(grad_queries).astype(BRAIN)
    grad_keys = merge_heads(grad_keys).astype(BRAIN)
    grad_values = merge_heads(grad_values).astype(BRAIN)
    self_query_grad = weight_grad(frames_self, grad_queries)
    self_key_grad = weight_grad(frames_self, grad_keys)
    self_value_grad = weight_grad(frames_self, grad_values)
    grad_normed = scatter_grads(
        project_back(grad_queries, query_self)
        + project_back(grad_keys, key_self)
        + project_back(grad_values, value_self)
    )
    grad_norm_term, self_gain_grad, self_bias_grad = norm_back(residual_in, gain_self, grad_normed)
    inputs_grad = grad_after_self + grad_norm_term
    reduced = (
        lax.psum_scatter(self_query_grad, "dp", scatter_dimension=0, tiled=True),
        lax.psum_scatter(self_key_grad, "dp", scatter_dimension=0, tiled=True),
        lax.psum_scatter(self_value_grad, "dp", scatter_dimension=0, tiled=True),
        lax.psum_scatter(cross_query_grad, "dp", scatter_dimension=0, tiled=True),
        lax.psum_scatter(cross_key_grad, "dp", scatter_dimension=0, tiled=True),
        lax.psum_scatter(cross_value_grad, "dp", scatter_dimension=0, tiled=True),
        lax.psum_scatter(feed_first_grad, "dp", scatter_dimension=0, tiled=True),
        lax.psum_scatter(self_out_grad, "dp", scatter_dimension=1, tiled=True),
        lax.psum_scatter(cross_out_grad, "dp", scatter_dimension=1, tiled=True),
        lax.psum_scatter(feed_second_grad, "dp", scatter_dimension=1, tiled=True),
    )
    norm_stack = jnp.stack(
        [
            self_gain_grad,
            self_bias_grad,
            cross_gain_grad,
            cross_bias_grad,
            feed_gain_grad,
            feed_bias_grad,
        ]
    )
    norm_reduced = lax.psum_scatter(norm_stack, ("dp", "tensor"), scatter_dimension=1, tiled=True)
    return (
        distill_loss,
        layer_out,
        inputs_grad,
        text_grad,
        norm_reduced[0],
        norm_reduced[1],
        reduced[0],
        reduced[1],
        reduced[2],
        reduced[7],
        norm_reduced[2],
        norm_reduced[3],
        reduced[3],
        reduced[4],
        reduced[5],
        reduced[8],
        norm_reduced[4],
        norm_reduced[5],
        reduced[6],
        reduced[9],
    )


def solution(mesh):
    placed = (
        P("dp", "tensor", None),
        P("dp", None, None),
        P("dp", "tensor", None),
        P("dp", "tensor"),
        P("dp"),
        P("dp"),
        P("dp", "tensor"),
        P("dp", "tensor"),
        P("dp", "tensor"),
        P("tensor", "dp"),
        P("dp"),
        P("dp"),
        P("dp", "tensor"),
        P("dp", "tensor"),
        P("dp", "tensor"),
        P("tensor", "dp"),
        P("dp"),
        P("dp"),
        P("dp", "tensor"),
        P("tensor", "dp"),
    )
    return jax.shard_map(
        on_device,
        mesh=mesh,
        in_specs=placed,
        out_specs=(
            P(),
            P("dp", "tensor", None),
            P("dp", "tensor", None),
            P("dp", None, "tensor"),
            P(("dp", "tensor")),
            P(("dp", "tensor")),
            P("dp", "tensor"),
            P("dp", "tensor"),
            P("dp", "tensor"),
            P("tensor", "dp"),
            P(("dp", "tensor")),
            P(("dp", "tensor")),
            P("dp", "tensor"),
            P("dp", "tensor"),
            P("dp", "tensor"),
            P("tensor", "dp"),
            P(("dp", "tensor")),
            P(("dp", "tensor")),
            P("dp", "tensor"),
            P("tensor", "dp"),
        ),
        check_vma=False,
    )
```

profile of v0, /device:TPU:1, one launch (start us, length us, event | category | flops | bytes accessed | tf_op | source)
XLA Modules:
  0.0 3500.3 jit_solution(17308623984216620645)
XLA Ops:
  20.4 57.9 %all-reduce.21 = (bf16[1536]{0:T(1024)(128)(2,1)S(1)}, bf16[1536]{0:T(1024)(128)(2,1)S(1)}, bf16[1536]{0:T(1024)(128)(2,1)}, bf16[1536]{0:T(1024)(128)(2,1)}, bf...) all-reduce(bf16[1536]{0:T(1024)(128)(2,1)S(1)} %dynamic-update-slice.11, ...), channel_id=1, replica_groups=mesh['dp'=16,'tensor'=2] {'dp'}, use_global_device_ids=true, to_apply=%add.3 | all-reduce | flops 9216 | bytes 36864
  106.2 111.0 %all-gather.17.cloned.1.call-done = bf16[1,1500,1536]{2,0,1:T(2,128)(2,1)} async-done(((bf16[1,750,1536]{2,0,1:T(2,128)(2,1)}), bf16[1,1500,1536]{2,0,1:T(2,128)(2,1)}) %all-gather.17.cloned.1.call-update) | async-done | bytes 4608016 | tf_op jit(solution)/shard_map/all_gather | solution.py:58
  474.6 56.9 %fusion = bf16[752,1536]{1,0:T(8,128)(2,1)S(1)} fusion(bf16[1,1500,1536]{2,1,0:T(8,128)(2,1)} %fusion.24), kind=kCustom, calls=%all-reduce-scatter | all-reduce-scatter fusion | flops 2310145 | bytes 6918656
  599.4 110.2 %all-gather.29.cloned.1.call-done = bf16[1,1500,1536]{2,0,1:T(2,128)(2,1)} async-done(((bf16[1,750,1536]{2,0,1:T(2,128)(2,1)}), bf16[1,1500,1536]{2,0,1:T(2,128)(2,1)}) %all-gather.29.cloned.1.call-update) | async-done | bytes 4608016 | tf_op jit(solution)/shard_map/all_gather | solution.py:58
  763.1 56.8 %fusion.1 = bf16[752,1536]{1,0:T(8,128)(2,1)S(1)} fusion(bf16[1,1500,1536]{2,1,0:T(8,128)(2,1)} %fusion.25), kind=kCustom, calls=%all-reduce-scatter.1 | all-reduce-scatter fusion | flops 2310145 | bytes 6918656
  876.3 115.3 %all-gather.37.cloned.1.call-done = bf16[1,1500,1536]{2,0,1:T(2,128)(2,1)} async-done(((bf16[1,750,1536]{2,0,1:T(2,128)(2,1)}), bf16[1,1500,1536]{2,0,1:T(2,128)(2,1)}) %all-gather.37.cloned.1.call-update) | async-done | bytes 4608016 | tf_op jit(solution)/shard_map/all_gather | solution.py:58
  991.6 84.0 %all-gather.39.cloned.1.call-done = bf16[1536,3072]{1,0:T(8,128)(2,1)} async-done(((bf16[96,3072]{1,0:T(8,128)(2,1)}), bf16[1536,3072]{1,0:T(8,128)(2,1)}) %all-gather.39.cloned.1.call-update) | async-done | bytes 9437200 | tf_op jit(solution)/shard_map/all_gather | solution.py:214
  1075.6 58.8 %multiply_convert_fusion.2 = (bf16[1500,3072]{1,0:T(8,128)(2,1)}, f32[1500,3072]{1,0:T(8,128)}, f32[1500,3072]{1,0:T(8,128)}) fusion(bf16[1536,3072]{1,0:T(8,128)(2,1)} %all-gather.39.cloned.1.call-done, bf16[1,1500,1536]{2,0,1:T(2,128)(2,1)} %all-gather.37.cloned.1.call-done), kind=kOutput, calls=%fused_computation.22 | convolution fusion | flops 14455296000 | bytes 60125184 | tf_op jit(solution)/shard_map/dot_general | solution.py:38
  1178.8 56.8 %fusion.2 = bf16[752,1536]{1,0:T(8,128)(2,1)S(1)} fusion(bf16[1,1500,1536]{2,1,0:T(8,128)(2,1)} %fusion.26), kind=kCustom, calls=%all-reduce-scatter.2 | all-reduce-scatter fusion | flops 2310145 | bytes 6918656
  1334.3 117.3 %all-gather.43.cloned.1.call-done = bf16[1,1500,1536]{2,0,1:T(2,128)(2,1)} async-done(((bf16[1,750,1536]{2,0,1:T(2,128)(2,1)}), bf16[1,1500,1536]{2,0,1:T(2,128)(2,1)}) %all-gather.43.cloned.1.call-update) | async-done | bytes 4608016 | tf_op jit(solution)/shard_map/all_gather | solution.py:68
  1504.9 55.4 %fusion.3 = bf16[752,1536]{1,0:T(8,128)(2,1)S(1)} fusion(bf16[1,1500,1536]{2,1,0:T(8,128)(2,1)} %fusion.27), kind=kCustom, calls=%all-reduce-scatter.3 | all-reduce-scatter fusion | flops 2310145 | bytes 6918656
  1626.5 118.6 %all-gather.45.cloned.1.call-done = bf16[1,1500,1536]{2,0,1:T(2,128)(2,1)} async-done(((bf16[1,750,1536]{2,0,1:T(2,128)(2,1)}), bf16[1,1500,1536]{2,0,1:T(2,128)(2,1)}) %all-gather.45.cloned.1.call-update) | async-done | bytes 4608016 | tf_op jit(solution)/shard_map/all_gather | solution.py:68
  1772.0 55.5 %fusion.4 = bf16[752,1536]{1,0:T(8,128)(2,1)S(1)} fusion(bf16[1,1500,1536]{2,1,0:T(8,128)(2,1)} %fusion.28), kind=kCustom, calls=%all-reduce-scatter.4 | all-reduce-scatter fusion | flops 2310145 | bytes 6918656
  1903.0 109.2 %all-gather.47.cloned.1.call-done = bf16[1,1500,1536]{2,0,1:T(2,128)(2,1)} async-done(((bf16[1,750,1536]{2,0,1:T(2,128)(2,1)}), bf16[1,1500,1536]{2,0,1:T(2,128)(2,1)}) %all-gather.47.cloned.1.call-update) | async-done | bytes 4608016 | tf_op jit(solution)/shard_map/all_gather | solution.py:68
  2255.3 56.6 %fusion.5 = bf16[752,1536]{1,0:T(8,128)(2,1)} fusion(bf16[1,1500,1536]{2,1,0:T(8,128)(2,1)} %fusion.29), kind=kCustom, calls=%all-reduce-scatter.5 | all-reduce-scatter fusion | flops 2310145 | bytes 6918656
  2539.1 79.3 %reduce-scatter.47.cloned.1.call-done = f32[96,768]{1,0:T(8,128)} async-done(((f32[1536,768]{1,0:T(8,128)}), f32[96,768]{1,0:T(8,128)}) %reduce-scatter.47.cloned.1.call-update) | async-done | bytes 294928 | tf_op jit(solution)/shard_map/reduce_scatter | solution.py:364
  2618.4 79.2 %reduce-scatter.59.cloned.1.call-done = f32[96,768]{1,0:T(8,128)} async-done(((f32[1536,768]{1,0:T(8,128)}), f32[96,768]{1,0:T(8,128)}) %reduce-scatter.59.cloned.1.call-update) | async-done | bytes 294928
  2697.6 79.4 %reduce-scatter.57.cloned.1.call-done = f32[96,768]{1,0:T(8,128)} async-done(((f32[1536,768]{1,0:T(8,128)}), f32[96,768]{1,0:T(8,128)}) %reduce-scatter.57.cloned.1.call-update) | async-done | bytes 294928
  2777.1 79.1 %reduce-scatter.45.cloned.1.call-done = f32[768,96]{0,1:T(8,128)} async-done(((f32[768,1536]{0,1:T(8,128)}), f32[768,96]{0,1:T(8,128)}) %reduce-scatter.45.cloned.1.call-update) | async-done | bytes 294928 | tf_op jit(solution)/shard_map/reduce_scatter | solution.py:368
  2856.1 79.4 %reduce-scatter.43.cloned.1.call-done = f32[96,768]{1,0:T(8,128)} async-done(((f32[1536,768]{1,0:T(8,128)}), f32[96,768]{1,0:T(8,128)}) %reduce-scatter.43.cloned.1.call-update) | async-done | bytes 294928 | tf_op jit(solution)/shard_map/reduce_scatter | solution.py:363
  2935.5 79.2 %reduce-scatter.39.cloned.1.call-done = f32[96,768]{1,0:T(8,128)} async-done(((f32[1536,768]{1,0:T(8,128)}), f32[96,768]{1,0:T(8,128)}) %reduce-scatter.39.cloned.1.call-update) | async-done | bytes 294928 | tf_op jit(solution)/shard_map/reduce_scatter | solution.py:361
  3014.7 79.3 %reduce-scatter.41.cloned.1.call-done = f32[96,768]{1,0:T(8,128)} async-done(((f32[1536,768]{1,0:T(8,128)}), f32[96,768]{1,0:T(8,128)}) %reduce-scatter.41.cloned.1.call-update) | async-done | bytes 294928 | tf_op jit(solution)/shard_map/reduce_scatter | solution.py:362
  3094.0 199.5 %reduce-scatter.51.cloned.1.call-done = f32[96,3072]{1,0:T(8,128)} async-done(((f32[1536,3072]{1,0:T(8,128)}), f32[96,3072]{1,0:T(8,128)}) %reduce-scatter.51.cloned.1.call-update) | async-done | bytes 1179664 | tf_op jit(solution)/shard_map/reduce_scatter | solution.py:367
  3293.5 198.6 %reduce-scatter.53.cloned.1.call-done = f32[3072,96]{0,1:T(8,128)} async-done(((f32[3072,1536]{0,1:T(8,128)}), f32[3072,96]{0,1:T(8,128)}) %reduce-scatter.53.cloned.1.call-update) | async-done | bytes 1179664 | tf_op jit(solution)/shard_map/reduce_scatter | solution.py:370
  (403 shorter events, 1306.1 us)
Async XLA Ops:
  7.2 209.9 %all-gather.17.cloned.1.call-start = ((), (), s32[]{:S(2)}) async-start(), calls=%async_computation.12 | async-start | bytes 13824000 | tf_op jit(solution)/shard_map/all_gather | solution.py:58
  100.5 205.1 %all-gather.23.cloned.1.call-start = ((), (), s32[]{:S(2)}) async-start(), calls=%async_computation.15 | async-start | bytes 2506752 | tf_op jit(solution)/shard_map/all_gather | solution.py:209
  101.3 247.6 %all-gather.19.cloned.1.call-start = ((), (), s32[]{:S(2)}) async-start(), calls=%async_computation.13 | async-start | bytes 2506752 | tf_op jit(solution)/shard_map/all_gather | solution.py:210
  101.8 365.5 %all-gather.25.cloned.1.call-start = ((), (), s32[]{:S(2)}) async-start(), calls=%async_computation.16 | async-start | bytes 2506752 | tf_op jit(solution)/shard_map/all_gather | solution.py:215
  102.4 492.1 %all-gather.33.cloned.1.call-start = ((), (), s32[]{:S(2)}) async-start(), calls=%async_computation.20 | async-start | bytes 2506752 | tf_op jit(solution)/shard_map/all_gather | solution.py:212
  103.0 493.9 %all-gather.27.cloned.1.call-start = ((), (), s32[]{:S(2)}) async-start(), calls=%async_computation.17 | async-start | bytes 2506752 | tf_op jit(solution)/shard_map/all_gather | solution.py:213
  103.8 495.6 %all-gather.31.cloned.1.call-start = ((), (), s32[]{:S(2)}) async-start(), calls=%async_computation.19 | async-start | bytes 2506752 | tf_op jit(solution)/shard_map/all_gather | solution.py:211
  594.0 397.6 %all-gather.37.cloned.1.call-start = ((), (), s32[]{:S(2)}) async-start(), calls=%async_computation.22 | async-start | bytes 13824000 | tf_op jit(solution)/shard_map/all_gather | solution.py:58
  874.7 200.9 %all-gather.39.cloned.1.call-start = ((), (), s32[]{:S(2)}) async-start(), calls=%async_computation.23 | async-start | bytes 10027008 | tf_op jit(solution)/shard_map/all_gather | solution.py:214
  875.3 282.2 %all-gather.41.cloned.1.call-start = ((), (), s32[]{:S(2)}) async-start(), calls=%async_computation.24 | async-start | bytes 10027008 | tf_op jit(solution)/shard_map/all_gather | solution.py:217
  876.1 575.5 %all-gather.43.cloned.1.call-start = ((), (), s32[]{:S(2)}) async-start(), calls=%async_computation.25 | async-start | bytes 13824000 | tf_op jit(solution)/shard_map/all_gather | solution.py:68
  1334.3 410.8 %all-gather.45.cloned.1.call-start = ((), (), s32[]{:S(2)}) async-start(), calls=%async_computation.26 | async-start | bytes 13824000 | tf_op jit(solution)/shard_map/all_gather | solution.py:68
  1625.6 386.6 %all-gather.47.cloned.1.call-start = ((), (), s32[]{:S(2)}) async-start(), calls=%async_computation.27 | async-start | bytes 13824000 | tf_op jit(solution)/shard_map/all_gather | solution.py:68
  1892.7 601.3 %reduce-scatter.37.cloned.1.call-start = ((), (), s32[]{:S(2)}) async-start(), calls=%async_computation.28 | async-start | bytes 294912 | tf_op jit(solution)/shard_map/reduce_scatter | solution.py:328
  2317.2 194.2 %reduce-scatter.55.cloned.1.call-start = ((), (), s32[]{:S(2)}) async-start(), calls=%async_computation.37 | async-start | bytes 811008
  2372.9 245.5 %reduce-scatter.47.cloned.1.call-start = ((), (), s32[]{:S(2)}) async-start(), calls=%async_computation.33 | async-start | bytes 5013504 | tf_op jit(solution)/shard_map/reduce_scatter | solution.py:364
  2383.7 313.9 %reduce-scatter.59.cloned.1.call-start = ((), (), s32[]{:S(2)}) async-start(), calls=%async_computation.39 | async-start | bytes 5013504
  2392.9 384.2 %reduce-scatter.57.cloned.1.call-start = ((), (), s32[]{:S(2)}) async-start(), calls=%async_computation.38 | async-start | bytes 5013504
  2402.8 453.4 %reduce-scatter.45.cloned.1.call-start = ((), (), s32[]{:S(2)}) async-start(), calls=%async_computation.32 | async-start | bytes 5013504 | tf_op jit(solution)/shard_map/reduce_scatter | solution.py:368
  2413.4 522.2 %reduce-scatter.43.cloned.1.call-start = ((), (), s32[]{:S(2)}) async-start(), calls=%async_computation.31 | async-start | bytes 5013504 | tf_op jit(solution)/shard_map/reduce_scatter | solution.py:363
  2422.8 591.9 %reduce-scatter.39.cloned.1.call-start = ((), (), s32[]{:S(2)}) async-start(), calls=%async_computation.29 | async-start | bytes 5013504 | tf_op jit(solution)/shard_map/reduce_scatter | solution.py:361
  2432.7 661.4 %reduce-scatter.41.cloned.1.call-start = ((), (), s32[]{:S(2)}) async-start(), calls=%async_computation.30 | async-start | bytes 5013504 | tf_op jit(solution)/shard_map/reduce_scatter | solution.py:362
  2442.4 851.1 %reduce-scatter.51.cloned.1.call-start = ((), (), s32[]{:S(2)}) async-start(), calls=%async_computation.35 | async-start | bytes 20054016 | tf_op jit(solution)/shard_map/reduce_scatter | solution.py:367
  2465.3 1026.8 %reduce-scatter.53.cloned.1.call-start = ((), (), s32[]{:S(2)}) async-start(), calls=%async_computation.36 | async-start | bytes 20054016 | tf_op jit(solution)/shard_map/reduce_scatter | solution.py:370
  (90 other events, 3354.0 us)
Sparse Core Ops, SparseCore 0:
  99.9 117.2 all-gather.16
  219.4 42.7 all-gather.20
  264.5 41.0 all-gather.22
  437.7 41.0 all-gather.26
  533.9 41.4 all-gather.30
  593.6 115.9 all-gather.28
  711.7 42.7 all-gather.34
  874.9 116.6 all-gather.36
  993.7 81.8 all-gather.38
  1077.9 79.5 all-gather.40
  1334.4 117.1 all-gather.42
  1625.7 119.3 all-gather.44
  1892.8 119.3 all-gather.46
  2362.6 96.7 reduce-scatter.54
  2463.8 75.2 reduce-scatter.48
  2543.9 74.4 reduce-scatter.46
  2622.9 74.6 reduce-scatter.58
  2702.5 74.4 reduce-scatter.56
  2781.5 74.5 reduce-scatter.44
  2860.9 74.5 reduce-scatter.42
  2940.0 74.6 reduce-scatter.38
  3019.5 74.5 reduce-scatter.40
  3098.6 194.8 reduce-scatter.50
  3298.2 193.8 reduce-scatter.52
  (4 shorter events, 135.5 us)
where the time goes:
time: 3510 us; the launch traced here: 3500 us
  waiting for transfers between devices  1900 us (54%)
  matrix products  571 us (16%)
  blocking collectives  435 us (12%)
  other arithmetic  397 us (11%)
  local copies, waits for them, and re-layouts  153 us (4%)
    unnamed x7, blocking collectives  396 us
    all_gather x3, waiting for transfers between devices, gather_grads(): return lax.all_gather(values, 'tensor', axis=1, tiled=True)  345 us
    all_gather x3, waiting for transfers between devices, gather_frames(): return lax.all_gather(values, 'tensor', axis=1, tiled=True)  336 us
    reduce_scatter x1, waiting for transfers between devices, on_device(): lax.psum_scatter(feed_first_grad, 'dp', scatter_dimension=0, tiled=True)  199 us
    reduce_scatter x1, waiting for transfers between devices, on_device(): lax.psum_scatter(feed_second_grad, 'dp', scatter_dimension=1, tiled=True)  199 us
    unnamed x37, waiting for transfers between devices  166 us
    dot_general x10, matrix products, project(): return jnp.dot(left, weight, preferred_element_type=FLOAT)  133 us
    unnamed x203, local copies, waits for them, and re-layouts  131 us
  transfers between devices with their start and end apart: 34, of which 25 were waited for; matrix products, arithmetic and copies ran while one was open for 16% of the time, Pallas kernels for 0%

commit v1 on v0

v1 whole, which is shorter than its diff:
```python
import functools

import jax
import jax.numpy as jnp
import numpy as np
from jax import lax
from jax.experimental import pallas as pl
from jax.experimental.pallas import tpu as pltpu
from jax.sharding import Mesh
from jax.sharding import PartitionSpec as P

HEAD_DIM = 64
LANES = 128
ROWS = 256
FLOAT = jnp.float32
BRAIN = jnp.bfloat16
NEGATIVE = -1e30
EPSILON = 1e-05
SCALE = HEAD_DIM ** (-0.5)
CHIPS = ("z", "x", "y")
MESH = pl.DeviceIdType.MESH


def swap_core(v):
    return lax.ppermute(v, "c", [(0, 1), (1, 0)])


def swap_clip(v):
    return lax.ppermute(v, ("c", "y"), [(0, 0), (1, 2), (2, 1), (3, 3)])


def ring_fit():
    return lax.axis_size("z") == 4 and lax.axis_size("x") == 2 and lax.axis_size("y") == 2


def by_chip(v):
    return v.reshape(4, 2, 2, v.shape[0] // 16, v.shape[1])


def joined(v):
    return v.reshape(-1, v.shape[-1])


def dot_nt(a, b, **kw):
    return lax.dot_general(a, b, (((1,), (1,)), ((), ())), preferred_element_type=FLOAT, **kw)


def dot_nn(a, b):
    return lax.dot_general(a, b, (((1,), (0,)), ((), ())), preferred_element_type=FLOAT)


def dot_tn(a, b):
    return lax.dot_general(a, b, (((0,), (0,)), ((), ())), preferred_element_type=FLOAT)


def attend_kernel(half, real, q_ref, k_ref, v_ref, o_ref, lse_ref):
    core = lax.axis_index("c")
    per_half = half // ROWS
    blocks = 2 * per_half
    lane = lax.broadcasted_iota(jnp.int32, (ROWS, LANES), 1)
    first = lane < HEAD_DIM
    rows_at = lax.broadcasted_iota(jnp.int32, (ROWS, ROWS), 0)
    cols_at = lax.broadcasted_iota(jnp.int32, (ROWS, ROWS), 1)

    def place(i):
        start = jnp.where(core == i // per_half, 0, half) + (i % per_half) * ROWS
        return pl.ds(pl.multiple_of(start, ROWS), ROWS)

    for i in range(blocks):
        queries = q_ref[place(i), :].astype(FLOAT) * SCALE
        outs = []
        logs = []
        for head in range(2):
            mine = first if head == 0 else jnp.logical_not(first)
            masked = jnp.where(mine, queries, 0.0).astype(BRAIN)
            scores = []
            for j in range(i + 1):
                s = dot_nt(masked, k_ref[place(j), :])
                if j == i:
                    s = jnp.where(cols_at <= rows_at, s, NEGATIVE)
                elif j == per_half - 1:
                    s = jnp.where(cols_at < real - (per_half - 1) * ROWS, s, NEGATIVE)
                scores.append(s)
            top = scores[0]
            for s in scores[1:]:
                top = jnp.maximum(top, s)
            top = jnp.max(top, 1, keepdims=True)
            total = None
            out = None
            for j in range(i + 1):
                e = jnp.exp(scores[j] - top)
                total = e if total is None else total + e
                term = dot_nn(e.astype(BRAIN), v_ref[place(j), :])
                out = term if out is None else out + term
            total = jnp.sum(total, 1, keepdims=True)
            outs.append(out / total)
            logs.append(top + jnp.log(total))
        o_ref[place(i), :] = jnp.where(first, outs[0], outs[1]).astype(BRAIN)
        both = jnp.where(lane == 0, logs[0], logs[1])
        lse_ref[0, :, i * ROWS : (i + 1) * ROWS] = both.T[:8, :]


def attend_self(q, k, v, real):
    rows, width = q.shape
    pairs = width // LANES
    spec = pl.BlockSpec((rows, LANES), lambda p: (0, p))
    return pl.pallas_call(
        functools.partial(attend_kernel, rows // 2, real),
        grid=(pairs,),
        in_specs=[spec, spec, spec],
        out_specs=[spec, pl.BlockSpec((1, 8, rows), lambda p: (p, 0, 0))],
        out_shape=[
            jax.ShapeDtypeStruct((rows, width), BRAIN),
            jax.ShapeDtypeStruct((pairs, 8, rows), FLOAT),
        ],
        compiler_params=pltpu.CompilerParams(vmem_limit_bytes=48 * 2**20),
        cost_estimate=pl.CostEstimate(
            flops=10 * rows * rows * width, bytes_accessed=8 * rows * width, transcendentals=0
        ),
        name="attend",
    )(q, k, v)


def attend_back_kernel(
    half, real, q_ref, k_ref, v_ref, do_ref, o_ref, lse_ref, dq_ref, dk_ref, dv_ref,
    dq_sum, dk_sum, dv_sum, inner, hook=None,
):
    core = lax.axis_index("c")
    per_half = half // ROWS
    blocks = 2 * per_half
    first = lax.broadcasted_iota(jnp.int32, (ROWS, LANES), 1) < HEAD_DIM
    key_at = lax.broadcasted_iota(jnp.int32, (ROWS, ROWS), 0)
    query_at = lax.broadcasted_iota(jnp.int32, (ROWS, ROWS), 1)
    pick = lax.broadcasted_iota(jnp.int32, (8, LANES), 1) // HEAD_DIM
    pick = (pick == lax.broadcasted_iota(jnp.int32, (8, LANES), 0)).astype(FLOAT)

    def place(i):
        start = jnp.where(core == i // per_half, 0, half) + (i % per_half) * ROWS
        return pl.ds(pl.multiple_of(start, ROWS), ROWS)

    for i in range(blocks):
        product = do_ref[place(i), :].astype(FLOAT) * o_ref[place(i), :].astype(FLOAT)
        inner[:, i * ROWS : (i + 1) * ROWS] = dot_nt(pick, product, precision=lax.Precision.HIGHEST)
    dq_sum[...] = jnp.zeros_like(dq_sum)

    for j in range(blocks):
        if hook is not None:
            hook(j)
        keys = k_ref[place(j), :]
        values = v_ref[place(j), :]
        dk_sum[...] = jnp.zeros_like(dk_sum)
        dv_sum[...] = jnp.zeros_like(dv_sum)

        def query_step(i, carry, j=j, keys=keys, values=values):
            rows = pl.ds(pl.multiple_of(i * ROWS, ROWS), ROWS)
            queries = q_ref[place(i), :].astype(FLOAT) * SCALE
            grads = do_ref[place(i), :].astype(FLOAT)
            dead = jnp.logical_and(key_at + j * ROWS >= real, key_at + j * ROWS < half)
            keep = jnp.logical_and(key_at + j * ROWS <= query_at + i * ROWS, jnp.logical_not(dead))
            dqs = []
            dk = dk_sum[...]
            dv = dv_sum[...]
            for head in range(2):
                mine = first if head == 0 else jnp.logical_not(first)
                q_m = jnp.where(mine, queries, 0.0).astype(BRAIN)
                do_m = jnp.where(mine, grads, 0.0).astype(BRAIN)
                s = dot_nt(keys, q_m)
                p = jnp.where(keep, jnp.exp(s - lse_ref[0, head : head + 1, rows]), 0.0)
                dp = dot_nt(values, do_m)
                ds = (p * (dp - inner[head : head + 1, rows])).astype(BRAIN)
                dv = dv + dot_nn(p.astype(BRAIN), do_m)
                dk = dk + dot_nn(ds, q_m)
                dqs.append(dot_tn(ds, keys))
            dk_sum[...] = dk
            dv_sum[...] = dv
            dq_sum[rows, :] += jnp.where(first, dqs[0], dqs[1])
            return carry

        lax.fori_loop(j, blocks, query_step, 0)
        dk_ref[place(j), :] = dk_sum[...].astype(BRAIN)
        dv_ref[place(j), :] = dv_sum[...].astype(BRAIN)

    for i in range(blocks):
        dq_ref[place(i), :] = (dq_sum[i * ROWS : (i + 1) * ROWS, :] * SCALE).astype(BRAIN)


def attend_self_back(q, k, v, do, o, lse, real):
    rows, width = q.shape
    pairs = width // LANES
    spec = pl.BlockSpec((rows, LANES), lambda p: (0, p))
    return pl.pallas_call(
        functools.partial(attend_back_kernel, rows // 2, real),
        grid=(pairs,),
        in_specs=[spec] * 5 + [pl.BlockSpec((1, 8, rows), lambda p: (p, 0, 0))],
        out_specs=[spec] * 3,
        scratch_shapes=[
            pltpu.VMEM((rows, LANES), FLOAT),
            pltpu.VMEM((ROWS, LANES), FLOAT),
            pltpu.VMEM((ROWS, LANES), FLOAT),
            pltpu.VMEM((8, rows), FLOAT),
        ],
        out_shape=[jax.ShapeDtypeStruct((rows, width), BRAIN)] * 3,
        compiler_params=pltpu.CompilerParams(vmem_limit_bytes=48 * 2**20),
        cost_estimate=pl.CostEstimate(
            flops=25 * rows * rows * width, bytes_accessed=16 * rows * width, transcendentals=0
        ),
        name="attend_back",
    )(q, k, v, do, o, lse)


ORDERS = ("zxy", "zyx", "xyz")
TICKS = 5


def whereabouts():
    z, x, c, y = (lax.axis_index(name) for name in ("z", "x", "c", "y"))
    return z, x, c, y, lax.rem(z + 1, 4), lax.rem(z + 3, 4), lax.rem(z + 2, 4)


def greet(c, y, up, down, x, cores):
    barrier = pltpu.get_barrier_semaphore()
    partners = [{"z": up}, {"z": down}, {"x": 1 - x}, {"y": 1 - y}]
    if cores:
        partners.append({"c": 1 - c})
    for partner in partners:
        pl.semaphore_signal(barrier, inc=1, device_id=partner, device_id_type=MESH)

    @pl.when(c != y)
    def _():
        pl.semaphore_signal(barrier, inc=1, device_id={"c": y, "y": c}, device_id_type=MESH)
        pl.semaphore_wait(barrier, len(partners) + 1)

    @pl.when(c == y)
    def _():
        pl.semaphore_wait(barrier, len(partners))


def one(i):
    return pl.ds(i, 1)


class Crossing:
    def __init__(self, c, y, send, recv, local):
        self.c, self.y, self.send, self.recv, self.local = c, y, send, recv, local
        self.used = 0

    def begin(self, src, dst):
        start, finish = self.prepare(src, dst)
        start()
        return finish

    def prepare(self, src, dst):
        at = self.used
        self.used += 1
        far = pltpu.make_async_remote_copy(
            src_ref=src, dst_ref=dst, send_sem=self.send.at[at], recv_sem=self.recv.at[at],
            device_id={"c": self.y, "y": self.c}, device_id_type=MESH,
        )
        near = pltpu.make_async_copy(src, dst, self.local.at[at])

        def start():
            @pl.when(self.c != self.y)
            def _():
                far.start()

            @pl.when(self.c == self.y)
            def _():
                near.start()

        def finish():
            @pl.when(self.c != self.y)
            def _():
                far.wait()

            @pl.when(self.c == self.y)
            def _():
                near.wait()

        return start, finish


def gather_events(where, slots, weights, send, recv):
    z, x, c, y, up, down, across = where
    every = slice(None)
    chains = []
    for number, (which, start, sizes) in enumerate(slots):
        ref = weights[which]
        ticks = [[] for _ in range(TICKS)]
        for kind, order in enumerate(ORDERS):
            size = sizes[kind]
            if size == 0:
                continue
            columns = pl.ds(start, size)
            start += size

            def copy(at, region, partner, ref=ref, columns=columns, kind=kind, number=number):
                view = ref.at[(*region, every, columns)]
                return pltpu.make_async_remote_copy(
                    src_ref=view, dst_ref=view, send_sem=send.at[number, kind, at],
                    recv_sem=recv.at[number, kind, at], device_id=partner, device_id_type=MESH,
                )

            if order == "xyz":
                by_x = copy(0, (one(z), one(x), one(y)), {"x": 1 - x})
                by_y = copy(1, (one(z), every, one(y)), {"y": 1 - y})
                rest = (every, every)
            else:
                rest = (one(x), one(y))
            z_up = copy(2, (one(z), *rest), {"z": up})
            z_down = copy(3, (one(z), *rest), {"z": down})
            z_more = copy(4, (one(down), *rest), {"z": up})
            if order == "xyz":
                ticks[0] += [by_x.start]
                ticks[1] += [by_x.wait, by_y.start]
                ticks[2] += [by_y.wait, z_up.start, z_down.start]
                ticks[3] += [z_up.wait, z_more.start]
                ticks[4] += [z_down.wait, z_more.wait]
            else:
                if order == "zxy":
                    near = copy(0, (every, one(x), one(y)), {"x": 1 - x})
                    far = copy(1, (every, every, one(y)), {"y": 1 - y})
                else:
                    near = copy(0, (every, one(x), one(y)), {"y": 1 - y})
                    far = copy(1, (every, one(x), every), {"x": 1 - x})
                ticks[0] += [z_up.start, z_down.start]
                ticks[1] += [z_up.wait, z_more.start]
                ticks[2] += [z_down.wait, z_more.wait, near.start]
                ticks[3] += [near.wait, far.start]
                ticks[4] += [far.wait]
        chains.append(ticks)
    return chains


def run_tick(chains, at):
    for number, ticks in enumerate(chains):
        if 0 <= at - number < TICKS:
            for event in ticks[at - number]:
                event()


def total_ticks(slots):
    return len(slots) + TICKS - 1


def gather_first_kernel(slots, count, *refs):
    blocks, (frames, target, text) = refs[:count], refs[count : count + 3]
    refs = refs[count + 3 :]
    weights, (frames_out, target_out, text_out) = refs[:count], refs[count : count + 3]
    send, recv, cross_send, cross_recv, cross_local, core_send, core_recv = refs[count + 3 :]
    where = whereabouts()
    z, x, c, y, up, down, across = where
    greet(c, y, up, down, x, True)
    crossing = Crossing(c, y, cross_send, cross_recv, cross_local)
    own = [crossing.begin(b, w.at[z, x, c]) for b, w in zip(blocks, weights)]
    frames_in = crossing.begin(frames, frames_out.at[0])
    text_in = crossing.begin(text, text_out)
    target_in = crossing.begin(target, target_out)
    chains = gather_events(where, slots, weights, send, recv)
    sibling = pltpu.make_async_remote_copy(
        src_ref=frames_out.at[0], dst_ref=frames_out.at[1], send_sem=core_send, recv_sem=core_recv,
        device_id={"c": 1 - c}, device_id_type=MESH,
    )
    seen = set()
    for at in range(total_ticks(slots)):
        if at < len(slots) and slots[at][0] not in seen:
            seen.add(slots[at][0])
            own[slots[at][0]]()
        run_tick(chains, at)
        if at == 3:
            frames_in()
            sibling.start()
    sibling.wait()
    text_in()
    target_in()


ANY = pl.BlockSpec(memory_space=pl.ANY)


def gather_first(blocks, frames, target, text, slots):
    count = len(blocks)
    rows = blocks[0].shape[0]
    crossings = count + 3
    shapes = [jax.ShapeDtypeStruct((4, 2, 2, rows, b.shape[1]), BRAIN) for b in blocks]
    shapes += [
        jax.ShapeDtypeStruct((2, *frames.shape), BRAIN),
        jax.ShapeDtypeStruct(target.shape, BRAIN),
        jax.ShapeDtypeStruct(text.shape, BRAIN),
    ]
    dma = pltpu.SemaphoreType.DMA
    return pl.pallas_call(
        functools.partial(gather_first_kernel, slots, count),
        out_shape=shapes,
        in_specs=[ANY] * (count + 3),
        out_specs=[ANY] * (count + 3),
        scratch_shapes=[
            dma((len(slots), 3, 5)), dma((len(slots), 3, 5)),
            dma((crossings,)), dma((crossings,)), dma((crossings,)), dma, dma,
        ],
        compiler_params=pltpu.CompilerParams(collective_id=1, has_side_effects=True),
        name="gather_first",
    )(*blocks, frames, target, text)


def gather_attend_kernel(slots, count, pairs, half, real, q_ref, k_ref, v_ref, *refs):
    blocks, o_ref, lse_ref = refs[:count], refs[count], refs[count + 1]
    weights = refs[count + 2 : 2 * count + 2]
    send, recv, cross_send, cross_recv, cross_local = refs[2 * count + 2 :]
    where = whereabouts()
    z, x, c, y, up, down, across = where
    crossing = Crossing(c, y, cross_send, cross_recv, cross_local)
    chains = gather_events(where, slots, weights, send, recv)
    ticks = total_ticks(slots)
    step = pl.program_id(0)

    @pl.when(step == 0)
    def _():
        greet(c, y, up, down, x, False)
        own = [crossing.begin(b, w.at[z, x, c]) for b, w in zip(blocks, weights)]
        for finish in own:
            finish()
        run_tick(chains, 0)
        run_tick(chains, 1)

    for turn in range(1, pairs):
        @pl.when(step == turn)
        def _(turn=turn):
            for at in range(2 + (turn - 1) * (ticks - 2) // (pairs - 1), 2 + turn * (ticks - 2) // (pairs - 1)):
                if at < ticks - 1:
                    run_tick(chains, at)

    attend_kernel(half, real, q_ref, k_ref, v_ref, o_ref, lse_ref)

    @pl.when(step == pairs - 1)
    def _():
        run_tick(chains, ticks - 1)


def gather_attend(q, k, v, real, blocks, slots):
    rows, width = q.shape
    pairs = width // LANES
    count = len(blocks)
    spec = pl.BlockSpec((rows, LANES), lambda p: (0, p))
    dma = pltpu.SemaphoreType.DMA
    return pl.pallas_call(
        functools.partial(gather_attend_kernel, slots, count, pairs, rows // 2, real),
        grid=(pairs,),
        in_specs=[spec, spec, spec] + [ANY] * count,
        out_specs=[spec, pl.BlockSpec((1, 8, rows), lambda p: (p, 0, 0))] + [ANY] * count,
        out_shape=[
            jax.ShapeDtypeStruct((rows, width), BRAIN),
            jax.ShapeDtypeStruct((pairs, 8, rows), FLOAT),
            *[jax.ShapeDtypeStruct((4, 2, 2, *b.shape), BRAIN) for b in blocks],
        ],
        scratch_shapes=[
            dma((len(slots), 3, 5)), dma((len(slots), 3, 5)), dma((count,)), dma((count,)), dma((count,)),
        ],
        compiler_params=pltpu.CompilerParams(
            collective_id=2, has_side_effects=True, vmem_limit_bytes=48 * 2**20
        ),
        name="gather_attend",
    )(q, k, v, *blocks)


def plus(*terms):
    total = terms[0].astype(FLOAT)
    for term in terms[1:]:
        total = total + term.astype(FLOAT)
    return total.astype(BRAIN)


def sum_scratch(slots, rows):
    shapes = []
    for _, _, sizes in slots:
        for kind, order in enumerate(ORDERS):
            size = sizes[kind]
            if size == 0:
                continue
            if order == "xyz":
                leads = [(2, 2, 2), (2, 2), (2, 2), (2, 2), (2,), ()]
            else:
                leads = [(4, 2), (4, 2), (4,), (), (), (), ()]
            shapes += [pltpu.VMEM((*lead, rows, size), BRAIN) for lead in leads]
    return shapes


def sum_events(where, slots, terms, outs, buffers, crossing, send, recv, local):
    z, x, c, y, up, down, across = where
    every = slice(None)
    chains = []
    taken = 0
    for number, (which, start, sizes) in enumerate(slots):
        ref, out = terms[which], outs[which]
        ticks = [[] for _ in range(TICKS + 1)]
        for kind, order in enumerate(ORDERS):
            size = sizes[kind]
            if size == 0:
                continue
            columns = pl.ds(start, size)
            start += size
            need = 6 if order == "xyz" else 7
            held = buffers[taken : taken + need]
            taken += need

            def copy(at, src, dst, partner, kind=kind, number=number):
                return pltpu.make_async_remote_copy(
                    src_ref=src, dst_ref=dst, send_sem=send.at[number, kind, at],
                    recv_sem=recv.at[number, kind, at], device_id=partner, device_id_type=MESH,
                )

            def view(*region, ref=ref, columns=columns):
                return ref.at[(*region, every, columns)]

            if order == "xyz":
                own, from_two, from_down, from_up, from_y, from_x = held
                load_a = pltpu.make_async_copy(view(z, every, every), own.at[0], local.at[number, kind, 0])
                load_b = pltpu.make_async_copy(view(down, every, every), own.at[1], local.at[number, kind, 1])
                s_three = copy(0, view(up, every, every), from_down, {"z": up})
                s_two = copy(1, view(across, every, every), from_two, {"z": down})
                s_one = copy(2, own.at[1], from_up, {"z": down})
                s_y = copy(3, own.at[0, every, 1 - y], from_y, {"y": 1 - y})
                s_x = copy(4, from_y.at[1 - x], from_x, {"x": 1 - x})

                def add_two(own=own, from_two=from_two):
                    for i in range(2):
                        for j in range(2):
                            own[1, i, j] = plus(own[1, i, j], from_two[i, j])

                def add_z(own=own, a=from_down, b=from_up):
                    for i in range(2):
                        for j in range(2):
                            own[0, i, j] = plus(own[0, i, j], a[i, j], b[i, j])

                def add_y(own=own, from_y=from_y):
                    for i in range(2):
                        from_y[i] = plus(own[0, i, y], from_y[i])

                def add_x(from_y=from_y, from_x=from_x):
                    from_x[...] = plus(from_y[x], from_x[...])

                ticks[0] += [load_a.start, load_b.start, s_three.start, s_two.start]
                ticks[1] += [s_two.wait, load_b.wait, add_two, s_one.start]
                ticks[2] += [s_three.wait, load_a.wait, s_one.wait, add_z, s_y.start]
                ticks[3] += [s_y.wait, add_y, s_x.start]
                ticks[4] += [s_x.wait, add_x]
                final = from_x
            else:
                own, from_first, from_second, from_two, from_down, from_up, total = held
                if order == "zxy":
                    mine, theirs = view(every, every, y), view(every, every, 1 - y)
                    first, second = {"y": 1 - y}, {"x": 1 - x}
                    side = x
                else:
                    mine, theirs = view(every, x, every), view(every, 1 - x, every)
                    first, second = {"x": 1 - x}, {"y": 1 - y}
                    side = y
                load = pltpu.make_async_copy(mine, own, local.at[number, kind, 0])
                s_first = copy(0, theirs, from_first, first)
                s_second = copy(1, own.at[every, 1 - side], from_second, second)
                s_three = copy(2, from_second.at[up], from_down, {"z": up})
                s_two = copy(3, from_second.at[across], from_two, {"z": down})
                s_one = copy(4, from_second.at[down], from_up, {"z": down})

                def add_first(own=own, got=from_first, side=side):
                    for i in range(4):
                        own[i, 1 - side] = plus(own[i, 1 - side], got[i, 1 - side])

                def add_second(own=own, got=from_first, more=from_second, side=side):
                    for i in range(4):
                        more[i] = plus(own[i, side], got[i, side], more[i])

                def add_two(more=from_second, two=from_two):
                    more[down] = plus(more[down], two[...])

                def add_z(more=from_second, a=from_down, b=from_up, total=total):
                    total[...] = plus(more[z], a[...], b[...])

                ticks[0] += [load.start, s_first.start]
                ticks[1] += [s_first.wait, load.wait, add_first, s_second.start]
                ticks[2] += [s_second.wait, add_second, s_three.start, s_two.start]
                ticks[3] += [s_two.wait, add_two, s_one.start]
                ticks[4] += [s_three.wait, s_one.wait, add_z]
                final = total

            leave, left = crossing.prepare(final, out.at[every, columns])
            ticks[4] += [leave]
            ticks[5] += [left]
        chains.append(ticks)
    return chains


def run_sum_tick(chains, at):
    for number, ticks in enumerate(chains):
        if 0 <= at - number < TICKS + 1:
            for event in ticks[at - number]:
                event()


def sum_attend_kernel(slots, count, pairs, half, real, q_ref, k_ref, v_ref, do_ref, o_ref, lse_ref, *refs):
    terms, frames = refs[:count], refs[count]
    refs = refs[count + 1 :]
    dq_ref, dk_ref, dv_ref = refs[:3]
    outs, frames_out = refs[3 : 3 + count], refs[3 + count]
    refs = refs[4 + count :]
    work, refs = refs[:4], refs[4:]
    send, recv, local, cross_send, cross_recv, cross_local = refs[:6]
    where = whereabouts()
    z, x, c, y, up, down, across = where
    crossing = Crossing(c, y, cross_send, cross_recv, cross_local)
    chains = sum_events(where, slots, terms, outs, refs[6:], crossing, send, recv, local)
    frames_start, frames_finish = crossing.prepare(frames, frames_out)
    ticks = len(slots) + TICKS
    step = pl.program_id(0)
    blocks = 2 * half // ROWS
    spots = {}
    for at in range(ticks - 1):
        spot = at * pairs * blocks // ticks
        spots.setdefault(spot, []).append(at)

    def hook(j):
        for turn in range(pairs):
            here = spots.get(turn * blocks + j, [])
            if here:
                @pl.when(step == turn)
                def _(here=here):
                    for at in here:
                        if at == 0:
                            greet(c, y, up, down, x, False)
                            frames_start()
                        run_sum_tick(chains, at)

    attend_back_kernel(
        half, real, q_ref, k_ref, v_ref, do_ref, o_ref, lse_ref, dq_ref, dk_ref, dv_ref, *work, hook=hook
    )

    @pl.when(step == pairs - 1)
    def _():
        run_sum_tick(chains, ticks - 1)
        frames_finish()


def sum_attend(q, k, v, do, o, lse, real, terms, frames, slots):
    rows, width = q.shape
    pairs = width // LANES
    count = len(terms)
    block = terms[0].shape[3]
    spec = pl.BlockSpec((rows, LANES), lambda p: (0, p))
    dma = pltpu.SemaphoreType.DMA
    crossings = 3 * len(slots) + 1
    return pl.pallas_call(
        functools.partial(sum_attend_kernel, slots, count, pairs, rows // 2, real),
        grid=(pairs,),
        in_specs=[spec] * 5
        + [pl.BlockSpec((1, 8, rows), lambda p: (p, 0, 0))] + [ANY] * (count + 1),
        out_specs=[spec] * 3 + [ANY] * (count + 1),
        out_shape=[jax.ShapeDtypeStruct((rows, width), BRAIN)] * 3
        + [jax.ShapeDtypeStruct((block, t.shape[4]), BRAIN) for t in terms]
        + [jax.ShapeDtypeStruct(frames.shape, BRAIN)],
        scratch_shapes=[
            pltpu.VMEM((rows, LANES), FLOAT), pltpu.VMEM((ROWS, LANES), FLOAT),
            pltpu.VMEM((ROWS, LANES), FLOAT), pltpu.VMEM((8, rows), FLOAT),
            dma((len(slots), 3, 5)), dma((len(slots), 3, 5)), dma((len(slots), 3, 2)),
            dma((crossings,)), dma((crossings,)), dma((crossings,)),
            *sum_scratch(slots, block),
        ],
        compiler_params=pltpu.CompilerParams(
            collective_id=3, has_side_effects=True, vmem_limit_bytes=58 * 2**20
        ),
        name="sum_attend",
    )(q, k, v, do, o, lse, *terms, frames)


def sum_last_kernel(slots, count, *refs):
    terms, (frames, vectors) = refs[:count], refs[count : count + 2]
    refs = refs[count + 2 :]
    outs, (frames_out, vectors_out) = refs[:count], refs[count : count + 2]
    refs = refs[count + 2 :]
    send, recv, local, cross_send, cross_recv, cross_local, v_send, v_recv, held, four = refs[:10]
    where = whereabouts()
    z, x, c, y, up, down, across = where
    greet(c, y, up, down, x, True)
    crossing = Crossing(c, y, cross_send, cross_recv, cross_local)
    chains = sum_events(where, slots, terms, outs, refs[10:], crossing, send, recv, local)
    frames_finish = crossing.begin(frames, frames_out)

    def copy(at, src, dst, partner):
        return pltpu.make_async_remote_copy(
            src_ref=src, dst_ref=dst, send_sem=v_send.at[at], recv_sem=v_recv.at[at],
            device_id=partner, device_id_type=MESH,
        )

    run_sum_tick(chains, 0)
    held[0] = vectors[...]
    for at, partner in enumerate(({"c": 1 - c}, {"y": 1 - y}, {"x": 1 - x})):
        hop = copy(at, held.at[2 * at], held.at[2 * at + 1], partner)
        hop.start()
        hop.wait()
        total = held[2 * at] + held[2 * at + 1]
        if at < 2:
            held[2 * at + 2] = total
        else:
            four[z] = total
    run_sum_tick(chains, 1)
    z_up, z_down = copy(3, four.at[z], four.at[z], {"z": up}), copy(4, four.at[z], four.at[z], {"z": down})
    z_more = copy(5, four.at[down], four.at[down], {"z": up})
    z_up.start()
    z_down.start()
    z_up.wait()
    z_more.start()
    for at in range(2, len(slots) + TICKS):
        run_sum_tick(chains, at)
    z_down.wait()
    z_more.wait()
    vectors_out[...] = (four[0] + four[1]) + (four[2] + four[3])
    frames_finish()


def sum_last(terms, frames, vectors, slots):
    count = len(terms)
    block = terms[0].shape[3]
    dma = pltpu.SemaphoreType.DMA
    crossings = 3 * len(slots) + 1
    whole = pl.BlockSpec(memory_space=pltpu.VMEM)
    return pl.pallas_call(
        functools.partial(sum_last_kernel, slots, count),
        in_specs=[ANY] * (count + 1) + [whole],
        out_specs=[ANY] * (count + 1) + [whole],
        out_shape=[jax.ShapeDtypeStruct((block, t.shape[4]), BRAIN) for t in terms]
        + [jax.ShapeDtypeStruct(frames.shape, BRAIN), jax.ShapeDtypeStruct(vectors.shape, FLOAT)],
        scratch_shapes=[
            dma((len(slots), 3, 5)), dma((len(slots), 3, 5)), dma((len(slots), 3, 2)),
            dma((crossings,)), dma((crossings,)), dma((crossings,)), dma((6,)), dma((6,)),
            pltpu.VMEM((6, *vectors.shape), FLOAT), pltpu.VMEM((4, *vectors.shape), FLOAT),
            *sum_scratch(slots, block),
        ],
        compiler_params=pltpu.CompilerParams(
            collective_id=4, has_side_effects=True, vmem_limit_bytes=58 * 2**20
        ),
        name="sum_last",
    )(*terms, frames, vectors)


def slots_of(widths):
    slots = []
    for which, width in enumerate(widths):
        tiles = width // LANES
        if tiles < 6:
            slots.append((which, 0, (width, 0, 0)))
        elif tiles == 6:
            sizes = (3, 2, 1) if len(slots) % 2 else (2, 3, 1)
            slots.append((which, 0, tuple(LANES * s for s in sizes)))
        else:
            for at in range(0, tiles, 8):
                here = min(8, tiles - at)
                many = -(-3 * here // 8)
                sizes = (many, min(many, here - many), max(0, here - 2 * many))
                slots.append((which, at * LANES, tuple(LANES * s for s in sizes)))
    return tuple(slots)


def normalize(values, gain_vec, bias_vec):
    center = values - jnp.mean(values, -1, keepdims=True)
    spread = jnp.mean(center * center, -1, keepdims=True)
    return center * lax.rsqrt(spread + EPSILON) * gain_vec + bias_vec


def norm_back(values, gain_vec, grads):
    center = values - jnp.mean(values, -1, keepdims=True)
    scale_row = lax.rsqrt(jnp.mean(center * center, -1, keepdims=True) + EPSILON)
    normal = center * scale_row
    scaled = grads * gain_vec
    inner = jnp.mean(scaled * normal, -1, keepdims=True)
    grad_values = scale_row * (scaled - jnp.mean(scaled, -1, keepdims=True) - normal * inner)
    return grad_values, jnp.sum(grads * normal, 0), jnp.sum(grads, 0)


def gelu_pair(u):
    half_erf = 0.5 * (1.0 + lax.erf(u * (0.5**0.5)))
    density = jnp.exp(-0.5 * u * u) * ((2.0 * np.pi) ** -0.5)
    return (u * half_erf).astype(BRAIN), (half_erf + u * density).astype(BRAIN)


def split_heads(values):
    return values.reshape(values.shape[0], -1, HEAD_DIM)


def merge_heads(values):
    return values.reshape(values.shape[0], -1)


def attend_cross(q, k, v):
    scores = jnp.einsum("qhd,khd->hqk", q, k, preferred_element_type=FLOAT) * SCALE
    top = jnp.max(scores, -1, keepdims=True)
    e = jnp.exp(scores - top)
    total = jnp.sum(e, -1, keepdims=True)
    probs = e / total
    out = jnp.einsum("hqk,khd->qhd", probs.astype(BRAIN), v, preferred_element_type=FLOAT)
    return merge_heads(out).astype(BRAIN), (top + jnp.log(total))[..., 0]


def attend_cross_back(q, k, v, do, lse):
    scores = jnp.einsum("qhd,khd->hqk", q, k, preferred_element_type=FLOAT) * SCALE
    probs = jnp.exp(scores - lse[..., None])
    dp = jnp.einsum("qhd,khd->hqk", do, v, preferred_element_type=FLOAT)
    inner = jnp.sum(probs * dp, -1, keepdims=True)
    ds = (probs * (dp - inner)).astype(BRAIN)
    dq = jnp.einsum("hqk,khd->qhd", ds, k, preferred_element_type=FLOAT) * SCALE
    dk = jnp.einsum("hqk,qhd->khd", ds, q, preferred_element_type=FLOAT) * SCALE
    dv = jnp.einsum("hqk,qhd->khd", probs.astype(BRAIN), do, preferred_element_type=FLOAT)
    return tuple(merge_heads(t).astype(BRAIN) for t in (dq, dk, dv))


def on_device(
    inputs, text_states, teacher, valid_frames,
    self_norm_gain, self_norm_bias, self_query, self_key, self_value, self_out,
    cross_norm_gain, cross_norm_bias, cross_query, cross_key, cross_value, cross_out,
    feed_norm_gain, feed_norm_bias, feed_in, feed_out,
):
    at_core, at_y = lax.axis_index("c"), lax.axis_index("y")
    real, width = inputs.shape[1], inputs.shape[2]
    half = -(-real // ROWS) * ROWS
    block = self_query.shape[0]

    fits = ring_fit()

    tiny = [self_norm_gain, self_norm_bias, cross_norm_gain, cross_norm_bias, feed_norm_gain, feed_norm_bias]
    count = jnp.sum(valid_frames)
    digits = jnp.stack([count // 64, count % 64]).astype(BRAIN)
    digits = jnp.where((jnp.arange(block) == 0)[:, None], digits[None, :], jnp.zeros((), BRAIN))
    tiny = jnp.pad(jnp.concatenate([jnp.stack(tiny, 1), digits], 1), ((0, 0), (0, LANES - 8)))
    early = [tiny, self_query, self_key, self_value, self_out.T, cross_out.T, cross_query, cross_key, cross_value]
    late = [feed_in, feed_out.T]
    early_slots = slots_of([v.shape[1] for v in early])
    late_slots = slots_of([v.shape[1] for v in late])

    def padded(v):
        return jnp.pad(v, ((0, half - real), (0, 0)))

    frames = padded(inputs[0])
    flags = jnp.pad(valid_frames[0][:, None].astype(BRAIN), ((0, 0), (0, LANES - 1)))
    target = padded(jnp.concatenate([teacher[0], flags], 1))
    if fits:
        *early, x_all, target, text = gather_first(early, frames, target, text_states[0], early_slots)
        early = [joined(v) for v in early]
        x_all = joined(x_all)
    else:
        early = [lax.all_gather(swap_clip(v), CHIPS, axis=0, tiled=True) for v in early]
        x_own = swap_clip(frames)
        x_all = jnp.concatenate([x_own, swap_core(x_own)], 0)
        target, text = swap_clip(target), swap_clip(text_states[0])
    tiny, w_q, w_k, w_v, w_so, w_co, w_cq, w_ck, w_cv = early
    counted = jnp.sum(tiny[:, 6:8].astype(FLOAT), 0)
    counted = counted[0] * 64.0 + counted[1]
    token_count = counted + swap_core(counted)
    gains = tiny.T.astype(FLOAT)
    valid = target[:, width : width + 1].astype(FLOAT)
    target = target[:, :width].astype(FLOAT)

    def both(own):
        return jnp.concatenate([own, swap_core(own)], 0)

    def summed(left, weight):
        far = dot_nt(left[half:], weight).astype(BRAIN)
        got = swap_core(far)
        return dot_nt(left[:half], weight) + got.astype(FLOAT)

    h1 = normalize(x_all.astype(FLOAT), gains[0], gains[1]).astype(BRAIN)
    q1 = dot_nn(h1, w_q).astype(BRAIN)
    k1 = dot_nn(h1, w_k).astype(BRAIN)
    v1 = dot_nn(h1, w_v).astype(BRAIN)
    if fits:
        o1, lse1, *late = gather_attend(q1, k1, v1, real, late, late_slots)
        w_fi, w_fo = (joined(v) for v in late)
    else:
        o1, lse1 = attend_self(q1, k1, v1, real)
        w_fi, w_fo = (lax.all_gather(swap_clip(v), CHIPS, axis=0, tiled=True) for v in late)
    x0 = x_all[:half].astype(FLOAT)
    x1 = x0 + summed(o1, w_so)
    h2 = both(normalize(x1, gains[2], gains[3]).astype(BRAIN))
    q2 = dot_nn(h2, w_cq).astype(BRAIN)
    k2 = dot_nn(text, w_ck).astype(BRAIN)
    v2 = dot_nn(text, w_cv).astype(BRAIN)
    o2, lse2 = attend_cross(split_heads(q2), split_heads(k2), split_heads(v2))
    x2 = x1 + summed(o2, w_co)
    h3 = both(normalize(x2, gains[4], gains[5]).astype(BRAIN))
    g, slope = gelu_pair(dot_nn(h3, w_fi))
    y = x2 + summed(g, w_fo)
    home = y.astype(BRAIN)
    deviation = y - target
    error = jnp.sum(valid * deviation * deviation)
    tokens_all = real * lax.axis_size(("z", "x", "c", "y"))
    dy = (2.0 * tokens_all / token_count) * valid * deviation

    dyb = both(dy.astype(BRAIN))
    fo_grad = dot_tn(dyb, g).astype(BRAIN)
    du = (slope.astype(FLOAT) * dot_nn(dyb, w_fo)).astype(BRAIN)
    fi_grad = dot_tn(h3, du).astype(BRAIN)
    term, gain3, bias3 = norm_back(x2, gains[4], summed(du, w_fi))
    dx2 = dy + term
    dx2b = both(dx2.astype(BRAIN))
    co_grad = dot_tn(dx2b, o2).astype(BRAIN)
    do2 = dot_nn(dx2b, w_co).astype(BRAIN)
    dq2, dk2, dv2 = attend_cross_back(
        split_heads(q2), split_heads(k2), split_heads(v2), split_heads(do2), lse2
    )
    cq_grad = dot_tn(h2, dq2).astype(BRAIN)
    ck_grad = dot_tn(text, dk2).astype(BRAIN)
    cv_grad = dot_tn(text, dv2).astype(BRAIN)
    text_part = (dot_nt(dk2, w_ck) + dot_nt(dv2, w_cv)).astype(BRAIN)
    text_mine = jnp.where(at_core == 0, text_part[:, : width // 2], text_part[:, width // 2 :])
    text_far = jnp.where(at_core == 0, text_part[:, width // 2 :], text_part[:, : width // 2])
    text_sum = text_mine.astype(FLOAT) + swap_core(text_far).astype(FLOAT)
    text_grad = swap_clip(text_sum.astype(BRAIN)).astype(FLOAT)[None]
    term, gain2, bias2 = norm_back(x1, gains[2], summed(dq2, w_cq))
    dx1 = dx2 + term
    dx1b = both(dx1.astype(BRAIN))
    so_grad = dot_tn(dx1b, o1).astype(BRAIN)
    do1 = dot_nn(dx1b, w_so).astype(BRAIN)
    wide = [fi_grad, fo_grad]
    if fits:
        dq1, dk1, dv1, *wide, home = sum_attend(
            q1, k1, v1, do1, o1, lse1, real, [by_chip(v) for v in wide], home, late_slots
        )
    else:
        dq1, dk1, dv1 = attend_self_back(q1, k1, v1, do1, o1, lse1, real)
        wide = [swap_clip(lax.psum_scatter(v, CHIPS, scatter_dimension=0, tiled=True)) for v in wide]
        home = swap_clip(home)
    layer_out = home[:real][None]
    fi_grad, fo_grad = (v.astype(FLOAT) for v in wide)
    dh1_far = dot_nt(dq1[half:], w_q) + dot_nt(dk1[half:], w_k) + dot_nt(dv1[half:], w_v)
    dh1_got = swap_core(dh1_far.astype(BRAIN))
    dh1 = dot_nt(dq1[:half], w_q) + dot_nt(dk1[:half], w_k) + dot_nt(dv1[:half], w_v)
    term, gain1, bias1 = norm_back(x0, gains[0], dh1 + dh1_got.astype(FLOAT))
    frames = (dx1 + term).astype(BRAIN)
    q_grad = dot_tn(h1, dq1).astype(BRAIN)
    k_grad = dot_tn(h1, dk1).astype(BRAIN)
    v_grad = dot_tn(h1, dv1).astype(BRAIN)

    vectors = jnp.stack([gain1, bias1, gain2, bias2, gain3, bias3])
    vectors = jnp.concatenate([vectors, jnp.full((2, width), error)], 0)
    grads = [so_grad, co_grad, cq_grad, ck_grad, cv_grad, q_grad, k_grad, v_grad]
    if fits:
        slots = slots_of([v.shape[1] for v in grads])
        *grads, frames, vectors = sum_last([by_chip(v) for v in grads], frames, vectors, slots)
    else:
        grads = [swap_clip(lax.psum_scatter(v, CHIPS, scatter_dimension=0, tiled=True)) for v in grads]
        frames = swap_clip(frames)
        vectors = lax.psum(vectors, ("z", "x", "c", "y"))
    so_grad, co_grad, cq_grad, ck_grad, cv_grad, q_grad, k_grad, v_grad = (v.astype(FLOAT) for v in grads)
    inputs_grad = frames[:real].astype(FLOAT)[None]
    loss = vectors[6, 0] / (width * token_count)
    mine = block // 2
    place = (lax.axis_index(("z", "x", "c")) * 2 + at_y) * mine
    norms = lax.dynamic_slice(vectors, (0, place), (8, mine))
    return (
        loss, layer_out, inputs_grad, text_grad,
        norms[0], norms[1], q_grad, k_grad, v_grad, so_grad.T,
        norms[2], norms[3], cq_grad, ck_grad, cv_grad, co_grad.T,
        norms[4], norms[5], fi_grad, fo_grad.T,
    )


def solution(mesh):
    outer = mesh.shape["dp"] // 4
    fine = Mesh(np.array(mesh.devices).reshape(outer, 2, 2, 2), ("z", "x", "c", "y"))
    dp = ("z", "x", "c")
    frames = P(dp, "y", None)
    vector, wide, tall = P(dp), P(dp, "y"), P("y", dp)
    small = P(("z", "x", "c", "y"))
    attention = (vector, vector, wide, wide, wide, tall)
    return jax.shard_map(
        on_device,
        mesh=fine,
        in_specs=(frames, P(dp, None, None), frames, P(dp, "y"), *attention, *attention, vector, vector, wide, tall),
        out_specs=(
            P(), frames, frames, P(dp, None, "y"),
            small, small, wide, wide, wide, tall,
            small, small, wide, wide, wide, tall,
            small, small, wide, tall,
        ),
        check_vma=False,
    )
```

time: 3510 us -> 1230 us (0.35)
  waiting for transfers between devices: 1900 us -> 16.1 us
  Pallas kernels: 0 us -> 824 us
  blocking collectives: 435 us -> 0 us
  other arithmetic: 397 us -> 56.9 us
  matrix products: 571 us -> 270 us
  local copies, waits for them, and re-layouts: 153 us -> 31.3 us
    all_gather x16 -> x0, waiting for transfers between devices: 920 us -> none  [the longest x3 345 us: gather_grads(): return lax.all_gather(values, 'tensor', axis=1, tiled=True)]
    pallas_call x0 -> x4, Pallas kernels: none -> 824 us  [the longest x1 243 us: gather_first(): pl.pallas_call(functools.partial(gather_first_kernel, slots, count), out_...]
    reduce_scatter x9 -> x0, waiting for transfers between devices: 818 us -> none  [the longest x1 199 us: on_device(): lax.psum_scatter(feed_first_grad, 'dp', scatter_dimension=0, tiled=True)]
    unnamed x7 -> x0, blocking collectives: 396 us -> none
    dot_general x48 -> x44, matrix products: 571 us -> 270 us  [the longest x18 100 us: dot_nt(): lax.dot_general(a, b, (((1,), (1,)), ((), ())), preferred_element_type=FL...]
    unnamed x37 -> x0, waiting for transfers between devices: 166 us -> none
    reduce_sum x8 -> x4, other arithmetic: 155 us -> 6.7 us  [the longest x1 3.15 us: norm_back(): center = values - jnp.mean(values, -1, keepdims=True)]
    unnamed x203 -> x247, local copies, waits for them, and re-layouts: 131 us -> 18.2 us
  transfers between devices with their start and end apart: 34 -> 14, of which waited for: 25 -> 5; matrix products, arithmetic and copies ran while one was open for 16% -> 10% of each run, Pallas kernels for 0% -> 0%
where the time goes in v1:
time: 1230 us; the launch traced here: 1220 us
  Pallas kernels  824 us (67%)
  matrix products  270 us (22%)
  other arithmetic  56.9 us (5%)
  local copies, waits for them, and re-layouts  31.3 us (3%)
  waiting for transfers between devices  16.1 us (1%)
  starting transfers between devices  13.9 us (1%)
    pallas_call x1, Pallas kernels, gather_first(): pl.pallas_call(functools.partial(gather_first_kernel, slots, count), out_...  243 us
    pallas_call x1, Pallas kernels, sum_last(): pl.pallas_call(functools.partial(sum_last_kernel, slots, count), in_specs...  209 us
    pallas_call x1, Pallas kernels, sum_attend(): pl.pallas_call(functools.partial(sum_attend_kernel, slots, count, pairs,...  204 us
    pallas_call x1, Pallas kernels, gather_attend(): pl.pallas_call(functools.partial(gather_attend_kernel, slots, count, pair...  167 us
    dot_general x18, matrix products, dot_nt(): lax.dot_general(a, b, (((1,), (1,)), ((), ())), preferred_element_type=FL...  100 us
    dot_general x10, matrix products, dot_nn(): lax.dot_general(a, b, (((1,), (0,)), ((), ())), preferred_element_type=FL...  83.4 us
    dot_general x10, matrix products, dot_tn(): lax.dot_general(a, b, (((0,), (0,)), ((), ())), preferred_element_type=FL...  79.9 us
  transfers between devices with their start and end apart: 14, of which 5 were waited for; matrix products, arithmetic and copies ran while one was open for 10% of the time, Pallas kernels for 0%

profile of v1, /device:TPU:1, one launch (start us, length us, event | category | flops | bytes accessed | tf_op | source)
XLA Modules:
  0.0 1220.3 jit_solution(13292433500641168957)
XLA Ops:
  11.8 242.7 %gather_first.1 = (bf16[4,2,2,96,128]{4,3,2,1,0:T(8,128)(2,1)}, bf16[4,2,2,96,768]{4,3,2,1,0:T(8,128)(2,1)}, bf16[4,2,2,96,768]{4,3,2,1,0:T(8,128)(2,1)}, bf16[4...) custom-call(bf16[96,128]{1,0:T(8,128)(2,1)} %pad.16.refs_0_, ...), custom_call_target="tpu_custom_call" | custom-call | tf_op jit(solution)/shard_map/gather_first/pallas_call | solution.py:391
  278.2 167.5 %gather_attend.1 = (bf16[1536,768]{1,0:T(8,128)(2,1)S(1)}, f32[6,8,1536]{2,1,0:T(8,128)S(1)}, bf16[4,2,2,96,3072]{4,3,2,1,0:T(8,128)(2,1)}, bf16[4,2,2,96,3072]{4,3,2,1,0:T(8,128)(2,1)}) custom-call(bf16[1536,768]{1,0:T(8,128)(2,1)S(1)} %convolution_convert_fusion.19.q_ref, bf16[1536,768]{1,0:T(8,128)(2,1)} %convolution_convert_fusion.18.k_ref, ...), custom_call_target="tpu_custom_call" | custom-call | tf_op jit(solution)/shard_map/gather_attend/pallas_call | solution.py:445
  464.5 7.0 convolution_convert_fusion.15
  493.0 21.1 %multiply_convert_fusion.1 = (bf16[1536,3072]{1,0:T(8,128)(2,1)}, f32[1536,3072]{1,0:T(8,128)}) fusion(bf16[1536,3072]{1,0:T(8,128)(2,1)S(1)} %bitcast.257, bf16[768,1536]{1,0:T(8,128)(2,1)S(1)} %collective-permute-done.4, bf16[768,1536]{1,0:T(8,128)(2,1)S(1)} %add_convert_fusion.2), kind=kOutput, calls=%fused_computation.7 | convolution fusion | flops 14528544768 | bytes 42467328 | tf_op jit(solution)/shard_map/dot_general | solution.py:49
  514.1 12.9 %fusion.35 = bf16[768,1536]{1,0:T(8,128)(2,1)} fusion(bf16[1536,3072]{1,0:T(8,128)(2,1)} %bitcast.261, bf16[1536,3072]{1,0:T(8,128)(2,1)} %get-tuple-element.191), kind=kOutput, calls=%fused_computation.102 | convolution fusion | flops 7248936960 | bytes 16515072 | tf_op jit(solution)/shard_map/dot_general | solution.py:45
  532.5 14.5 %fusion.24 = (f32[]{:T(128)}, f32[768,1536]{1,0:T(8,128)S(1)}) fusion(f32[768]{0:T(1024)S(1)} %get-tuple-element.156, bf16[768,1664]{1,0:T(8,128)(2,1)S(1)} %copy-done.11, f32[768,1536]{1,0:T(8,128)} %copy-done.9, bf16[768,1536]{1,0:T(8,128)(2,1)} %collective-permute-done.5, bf16[1536,3072]{1,0:T(8,128)(2,1)} %bitcast.262, ...), kind=kOutput, calls=%fused_computation.38 | convolution fusion | flops 7257194496 | bytes 28314628 | tf_op jit(solution)/shard_map/dot_general | solution.py:45
  554.0 28.0 %multiply_convert_fusion = bf16[1536,3072]{1,0:T(8,128)(2,1)} fusion(bf16[1536,3072]{1,0:T(8,128)(2,1)} %bitcast.263, f32[1536,3072]{1,0:T(8,128)} %get-tuple-element.192, bf16[768,1536]{1,0:T(8,128)(2,1)S(1)} %collective-permute-done.6, bf16[768,1536]{1,0:T(8,128)(2,1)S(1)} %multiply_convert_fusion.4), kind=kOutput, calls=%fused_computation.6 | convolution fusion | flops 14561574912 | bytes 42467328 | tf_op jit(solution)/shard_map/dot_general | solution.py:49
  582.1 10.7 fusion.38
  601.4 15.8 %multiply_reduce_fusion.1 = (f32[1536]{0:T(1024)S(1)}, f32[768]{0:T(1024)S(1)}, f32[768]{0:T(1024)S(1)}, f32[1536]{0:T(1024)S(1)}, f32[768,1536]{1,0:T(8,128)}) fusion(f32[768,1536]{1,0:T(8,128)} %copy-done.9, f32[768]{0:T(1024)S(1)} %copy-done.75, f32[768]{0:T(1024)S(1)} %copy-done.67, bf16[768,1536]{1,0:T(8,128)(2,1)} %collective-permute-done.7, ...), kind=kOutput, calls=%fused_computation.52 | convolution fusion | flops 7260728832 | bytes 25982976 | tf_op jit(solution)/shard_map/dot_general | solution.py:45
  617.3 6.5 fusion.83
  624.1 20.6 %convolution_convert_fusion = bf16[1536,3072]{1,0:T(8,128)(2,1)} fusion(bf16[1536,3072]{1,0:T(8,128)(2,1)} %get-tuple-element.191, bf16[768,1536]{1,0:T(8,128)(2,1)} %copy-done.90, bf16[768,1536]{1,0:T(8,128)(2,1)S(1)} %copy-done.28), kind=kOutput, calls=%fused_computation.9 | convolution fusion | flops 14509670400 | bytes 23592960 | tf_op jit(solution)/shard_map/dot_general | solution.py:53
  644.7 5.4 convolution_convert_fusion.12
  658.8 20.4 %convolution_convert_fusion.1 = bf16[1536,3072]{1,0:T(8,128)(2,1)} fusion(bf16[1536,3072]{1,0:T(8,128)(2,1)} %multiply_convert_fusion, bf16[768,1536]{1,0:T(8,128)(2,1)} %copy-done.89, bf16[768,1536]{1,0:T(8,128)(2,1)S(1)} %copy-done.26), kind=kOutput, calls=%fused_computation.10 | convolution fusion | flops 14509670400 | bytes 23592960 | tf_op jit(solution)/shard_map/dot_general | solution.py:53
  691.8 8.3 convolution_convert_fusion.8
  714.8 6.7 convolution_convert_fusion.5.do_ref
  721.5 204.4 %sum_attend.1 = (bf16[1536,768]{1,0:T(8,128)(2,1)}, bf16[1536,768]{1,0:T(8,128)(2,1)}, bf16[1536,768]{1,0:T(8,128)(2,1)}, bf16[96,3072]{1,0:T(8,128)(2,1)}, bf16...) custom-call(bf16[1536,768]{1,0:T(8,128)(2,1)} %copy-done, bf16[1536,768]{1,0:T(8,128)(2,1)} %convolution_convert_fusion.18.k_ref, ...), custom_call_target="tpu_custom_call" | custom-call | tf_op jit(solution)/shard_map/sum_attend/pallas_call | solution.py:650
  934.4 6.0 add_convert_fusion.1
  942.8 5.2 convolution_convert_fusion.2
  951.7 5.2 convolution_convert_fusion.10
  966.5 5.2 convolution_convert_fusion.3
  971.7 5.2 convolution_convert_fusion.4
  977.0 5.8 fusion.22
  987.2 209.1 %sum_last.1 = (bf16[96,768]{1,0:T(8,128)(2,1)}, bf16[96,768]{1,0:T(8,128)(2,1)}, bf16[96,768]{1,0:T(8,128)(2,1)}, bf16[96,768]{1,0:T(8,128)(2,1)}, bf16[96,768]{...) custom-call(bf16[4,2,2,96,768]{4,3,2,1,0:T(8,128)(2,1)} %bitcast.224, ...), custom_call_target="tpu_custom_call" | custom-call | tf_op jit(solution)/shard_map/sum_last/pallas_call | solution.py:724
  1200.7 9.3 copy.71
  (389 shorter events, 167.9 us)
Async XLA Ops:
  260.1 197.0 %copy-start.60 = (f32[1536]{0:T(1024)}, f32[1536]{0:T(1024)S(1)}, u32[]{:S(2)}) copy-start(f32[1536]{0:T(1024)S(1)} %get-tuple-element.161) | copy-start | bytes 18436
  260.1 226.8 %copy-start.62 = (f32[1536]{0:T(1024)}, f32[1536]{0:T(1024)S(1)}, u32[]{:S(2)}) copy-start(f32[1536]{0:T(1024)S(1)} %get-tuple-element.159) | copy-start | bytes 18436
  278.2 169.6 %copy-start = (bf16[1536,768]{1,0:T(8,128)(2,1)}, bf16[1536,768]{1,0:T(8,128)(2,1)S(1)}, u32[]{:S(2)}) copy-start(bf16[1536,768]{1,0:T(8,128)(2,1)S(1)} %convolution_convert_fusion.19.q_ref) | copy-start | bytes 7077892
  278.2 167.5 %copy-start.83 = (bf16[4,2,2,96,768]{4,3,2,1,0:T(8,128)(2,1)S(1)}, bf16[4,2,2,96,768]{4,3,2,1,0:T(8,128)(2,1)}, u32[]{:S(2)}) copy-start(bf16[4,2,2,96,768]{4,3,2,1,0:T(8,128)(2,1)} %get-tuple-element.59) | copy-start | bytes 7077892
  278.2 175.8 %slice-start = ((s8[4718592]{0:T(1024)(128)(4,1)}), s8[524288]{0:T(1024)(128)(4,1)S(1)}, s32[]{:S(2)}) async-start(s8[4718592]{0:T(1024)(128)(4,1)} %bitcast.190), calls=%async_computation | async-start | bytes 1048576
  447.8 6.3 collective-permute-start.1
  459.6 4.9 collective-permute-start.2
  479.3 4.6 collective-permute-start.3
  488.4 4.5 collective-permute-start.4
  526.9 5.6 collective-permute-start.5
  529.5 2.0 collective-permute-start
  547.1 35.0 %slice-start.19 = ((s8[9437184]{0:T(1024)(128)(4,1)}), s8[4194304]{0:T(1024)(128)(4,1)S(1)}, s32[]{:S(2)}) async-start(s8[9437184]{0:T(1024)(128)(4,1)} %bitcast.258), calls=%async_computation.19 | async-start | bytes 8388608
  549.5 32.6 %copy-start.27 = (bf16[768,1536]{1,0:T(8,128)(2,1)}, bf16[768,1536]{1,0:T(8,128)(2,1)S(1)}, u32[]{:S(2)}) copy-start(bf16[768,1536]{1,0:T(8,128)(2,1)S(1)} %multiply_convert_fusion.4) | copy-start | bytes 7077892
  549.5 4.5 collective-permute-start.6
  554.0 28.0 %slice-start.20 = ((s8[9437184]{0:T(1024)(128)(4,1)}), s8[4194304]{0:T(1024)(128)(4,1)S(1)}, s32[]{:S(2)}) async-start(s8[9437184]{0:T(1024)(128)(4,1)} %bitcast.258), calls=%async_computation.20 | async-start | bytes 8388608
  554.0 28.0 %slice-start.21 = ((s8[9437184]{0:T(1024)(128)(4,1)}), s8[1048576]{0:T(1024)(128)(4,1)S(1)}, s32[]{:S(2)}) async-start(s8[9437184]{0:T(1024)(128)(4,1)} %bitcast.258), calls=%async_computation.21 | async-start | bytes 2097152
  592.8 8.6 collective-permute-start.7
  617.3 32.9 %slice-start.4 = ((s8[4718592]{0:T(1024)(128)(4,1)}), s8[4194304]{0:T(1024)(128)(4,1)S(1)}, s32[]{:S(2)}) async-start(s8[4718592]{0:T(1024)(128)(4,1)} %bitcast.194), calls=%async_computation.4 | async-start | bytes 8388608
  623.8 20.9 %collective-permute-start.8 = (bf16[768,1536]{1,0:T(8,128)(2,1)}, bf16[768,1536]{1,0:T(8,128)(2,1)S(1)}, u32[]{:S(2)}, u32[]{:S(2)}) collective-permute-start(bf16[768,1536]{1,0:T(8,128)(2,1)} %get-tuple-element.168), channel_id=1, source_target_pairs={{0,2},{2,0},{1,3},{3,1},{4,6},{6,4},{5,7},{7,5},{8,10},{10,8},{9,1... | collective-permute-start | bytes 7077896 | tf_op jit(solution)/shard_map/ppermute | solution.py:25
  658.4 25.4 %collective-permute-start.9 = (bf16[768,1536]{1,0:T(8,128)(2,1)}, bf16[768,1536]{1,0:T(8,128)(2,1)S(1)}, u32[]{:S(2)}, u32[]{:S(2)}) collective-permute-start(bf16[768,1536]{1,0:T(8,128)(2,1)} %convolution_convert_fusion.11), channel_id=1, source_target_pairs={{0,2},{2,0},{1,3},{3,1},{4,6},{6,4},{5,7},{7,5},{8,10},{10,8},{9,1... | collective-permute-start | bytes 7077896 | tf_op jit(solution)/shard_map/ppermute | solution.py:25
  683.7 23.9 %collective-permute-start.12 = (bf16[64,768]{1,0:T(8,128)(2,1)S(1)}, bf16[64,768]{1,0:T(8,128)(2,1)S(1)}, u32[]{:S(2)}, u32[]{:S(2)}) collective-permute-start(bf16[64,768]{1,0:T(8,128)(2,1)S(1)} %broadcast_select_fusion), channel_id=1, source_target_pairs={{0,2},{2,0},{1,3},{3,1},{4,6},{6,4},{5,7},{7,5},{8,10},{10,8},{9,1... | collective-permute-start | bytes 294920 | tf_op jit(solution)/shard_map/ppermute | solution.py:25
  691.5 23.2 %collective-permute-start.10 = (bf16[768,1536]{1,0:T(8,128)(2,1)S(1)}, bf16[768,1536]{1,0:T(8,128)(2,1)S(1)}, u32[]{:S(2)}, u32[]{:S(2)}) collective-permute-start(bf16[768,1536]{1,0:T(8,128)(2,1)S(1)} %get-tuple-element.166), channel_id=1, source_target_pairs={{0,2},{2,0},{1,3},{3,1},{4,6},{6,4},{5,7},{7,5},{8,10},{10,8},{9,1... | collective-permute-start | bytes 7077896 | tf_op jit(solution)/shard_map/ppermute | solution.py:25
  707.6 6.4 collective-permute-start.13
  940.4 36.5 %collective-permute-start.11 = (bf16[768,1536]{1,0:T(8,128)(2,1)}, bf16[768,1536]{1,0:T(8,128)(2,1)}, u32[]{:S(2)}, u32[]{:S(2)}) collective-permute-start(bf16[768,1536]{1,0:T(8,128)(2,1)} %add_convert_fusion.1), channel_id=1, source_target_pairs={{0,2},{2,0},{1,3},{3,1},{4,6},{6,4},{5,7},{7,5},{8,10},{10,8},{9,1... | collective-permute-start | bytes 7077896 | tf_op jit(solution)/shard_map/ppermute | solution.py:25
  (113 other events, 871.4 us)

commit v2 on v1

--- a/solution.py
+++ b/solution.py
@@ -210,6 +210,7 @@
 
 ORDERS = ("zxy", "zyx", "xyz")
 TICKS = 5
+SUM_TIME = 1.6
 
 
 def whereabouts():
@@ -342,124 +343,149 @@
     return len(slots) + TICKS - 1
 
 
-def gather_first_kernel(slots, count, *refs):
-    blocks, (frames, target, text) = refs[:count], refs[count : count + 3]
-    refs = refs[count + 3 :]
-    weights, (frames_out, target_out, text_out) = refs[:count], refs[count : count + 3]
-    send, recv, cross_send, cross_recv, cross_local, core_send, core_recv = refs[count + 3 :]
-    where = whereabouts()
-    z, x, c, y, up, down, across = where
-    greet(c, y, up, down, x, True)
-    crossing = Crossing(c, y, cross_send, cross_recv, cross_local)
-    own = [crossing.begin(b, w.at[z, x, c]) for b, w in zip(blocks, weights)]
-    frames_in = crossing.begin(frames, frames_out.at[0])
-    text_in = crossing.begin(text, text_out)
-    target_in = crossing.begin(target, target_out)
-    chains = gather_events(where, slots, weights, send, recv)
-    sibling = pltpu.make_async_remote_copy(
-        src_ref=frames_out.at[0], dst_ref=frames_out.at[1], send_sem=core_send, recv_sem=core_recv,
-        device_id={"c": 1 - c}, device_id_type=MESH,
-    )
-    seen = set()
-    for at in range(total_ticks(slots)):
-        if at < len(slots) and slots[at][0] not in seen:
-            seen.add(slots[at][0])
-            own[slots[at][0]]()
-        run_tick(chains, at)
-        if at == 3:
-            frames_in()
-            sibling.start()
-    sibling.wait()
-    text_in()
-    target_in()
+def bring_own(crossing, where, slots, chains, blocks, weights):
+    z, x, c = where[:3]
+    for which, (block, weight) in enumerate(zip(blocks, weights)):
+        start, finish = crossing.prepare(block, weight.at[z, x, c])
+        number = [slot[0] for slot in slots].index(which)
+        chains[number][0].insert(0, finish)
+        yield start
 
 
 ANY = pl.BlockSpec(memory_space=pl.ANY)
-
-
-def gather_first(blocks, frames, target, text, slots):
-    count = len(blocks)
-    rows = blocks[0].shape[0]
-    crossings = count + 3
-    shapes = [jax.ShapeDtypeStruct((4, 2, 2, rows, b.shape[1]), BRAIN) for b in blocks]
-    shapes += [
-        jax.ShapeDtypeStruct((2, *frames.shape), BRAIN),
-        jax.ShapeDtypeStruct(target.shape, BRAIN),
-        jax.ShapeDtypeStruct(text.shape, BRAIN),
-    ]
-    dma = pltpu.SemaphoreType.DMA
-    return pl.pallas_call(
-        functools.partial(gather_first_kernel, slots, count),
-        out_shape=shapes,
-        in_specs=[ANY] * (count + 3),
-        out_specs=[ANY] * (count + 3),
-        scratch_shapes=[
-            dma((len(slots), 3, 5)), dma((len(slots), 3, 5)),
-            dma((crossings,)), dma((crossings,)), dma((crossings,)), dma, dma,
-        ],
-        compiler_params=pltpu.CompilerParams(collective_id=1, has_side_effects=True),
-        name="gather_first",
-    )(*blocks, frames, target, text)
-
-
-def gather_attend_kernel(slots, count, pairs, half, real, q_ref, k_ref, v_ref, *refs):
-    blocks, o_ref, lse_ref = refs[:count], refs[count], refs[count + 1]
-    weights = refs[count + 2 : 2 * count + 2]
-    send, recv, cross_send, cross_recv, cross_local = refs[2 * count + 2 :]
+NEEDED_FIRST = 4
+
+
+def gather_kernel(slots, count, real, *refs):
+    blocks, (frames, text, target, block) = refs[:count], refs[count : count + 4]
+    refs = refs[count + 4 :]
+    weights, (own_out, text_out, target_out, block_out) = refs[:count], refs[count : count + 4]
+    gains_ref, h_ref, q_ref, k_ref, v_ref, o_ref, lse_ref = refs[count + 4 : count + 11]
+    send, recv, cross_send, cross_recv, cross_local, core_send, core_recv, loads, tiny, both, held = refs[count + 11 :]
+    rows, width = h_ref.shape
+    half = rows // 2
+    pairs = q_ref.shape[1] // LANES
     where = whereabouts()
     z, x, c, y, up, down, across = where
     crossing = Crossing(c, y, cross_send, cross_recv, cross_local)
     chains = gather_events(where, slots, weights, send, recv)
-    ticks = total_ticks(slots)
-    step = pl.program_id(0)
-
-    @pl.when(step == 0)
-    def _():
-        greet(c, y, up, down, x, False)
-        own = [crossing.begin(b, w.at[z, x, c]) for b, w in zip(blocks, weights)]
-        for finish in own:
-            finish()
-        run_tick(chains, 0)
-        run_tick(chains, 1)
-
-    for turn in range(1, pairs):
-        @pl.when(step == turn)
-        def _(turn=turn):
-            for at in range(2 + (turn - 1) * (ticks - 2) // (pairs - 1), 2 + turn * (ticks - 2) // (pairs - 1)):
-                if at < ticks - 1:
-                    run_tick(chains, at)
-
-    attend_kernel(half, real, q_ref, k_ref, v_ref, o_ref, lse_ref)
-
-    @pl.when(step == pairs - 1)
-    def _():
-        run_tick(chains, ticks - 1)
-
-
-def gather_attend(q, k, v, real, blocks, slots):
-    rows, width = q.shape
-    pairs = width // LANES
+    starts = list(bring_own(crossing, where, slots, chains, blocks, weights))
+    frames_start, frames_finish = crossing.prepare(frames, both.at[0])
+    moves = [crossing.prepare(*pair) for pair in ((text, text_out), (block, block_out), (target, target_out))]
+    sibling = pltpu.make_async_remote_copy(
+        src_ref=both.at[0], dst_ref=both.at[1], send_sem=core_send, recv_sem=core_recv,
+        device_id={"c": 1 - c}, device_id_type=MESH,
+    )
+    keep = pltpu.make_async_copy(both.at[0], own_out, loads.at[4])
+    fetch = [pltpu.make_async_copy(weights[0], tiny, loads.at[0])]
+    fetch += [pltpu.make_async_copy(weights[i + 1], held.at[i], loads.at[i + 1]) for i in range(3)]
+
+    def tick(at):
+        for number in reversed(range(len(slots))):
+            stage = at - number
+            last = TICKS if number < NEEDED_FIRST else TICKS - 1
+            if 0 <= stage < last:
+                run_events(chains[number][stage])
+
+    greet(c, y, up, down, x, True)
+    for start in starts[:NEEDED_FIRST]:
+        start()
+    frames_start()
+    for start in starts[NEEDED_FIRST:]:
+        start()
+    for start, _ in moves:
+        start()
+    ready = NEEDED_FIRST + TICKS - 1
+    for at in range(ready):
+        tick(at)
+        if at == 3:
+            frames_finish()
+            sibling.start()
+            keep.start()
+        if at == ready - 4:
+            fetch[0].start()
+    for copy in fetch[1:]:
+        copy.start()
+    sibling.wait()
+    fetch[0].wait()
+    gains_ref[...] = tiny[...].reshape(width, LANES).astype(FLOAT).T[:8, :]
+
+    def norm_step(i, carry):
+        here = pl.ds(pl.multiple_of(i * LANES, LANES), LANES)
+        for side in range(2):
+            there = pl.ds(pl.multiple_of(side * half + i * LANES, LANES), LANES)
+            h_ref[there, :] = normalize(both[side, here, :].astype(FLOAT), gains_ref[0:1, :], gains_ref[1:2, :]).astype(BRAIN)
+        return carry
+
+    lax.fori_loop(0, half // LANES, norm_step, 0)
+    later = list(range(ready, len(slots) + TICKS - 2))
+    tick(later.pop(0))
+    for i, out in enumerate((q_ref, k_ref, v_ref)):
+        fetch[i + 1].wait()
+
+        def project_step(r, carry, i=i, out=out):
+            here = pl.ds(pl.multiple_of(r * ROWS, ROWS), ROWS)
+            out[here, :] = dot_nn(h_ref[here, :], held[i].reshape(width, -1)).astype(BRAIN)
+            return carry
+
+        lax.fori_loop(0, rows // ROWS, project_step, 0)
+        if later:
+            tick(later.pop(0))
+
+    def pair_step(p, carry):
+        for turn in range(pairs):
+            if turn < len(later):
+                @pl.when(p == turn)
+                def _(turn=turn):
+                    tick(later[turn])
+
+        lanes = pl.ds(pl.multiple_of(p * LANES, LANES), LANES)
+        every = slice(None)
+        q, k, v, o = (ref.at[every, lanes] for ref in (q_ref, k_ref, v_ref, o_ref))
+        attend_kernel(half, real, q, k, v, o, lse_ref.at[pl.ds(p, 1)])
+        return carry
+
+    lax.fori_loop(0, pairs, pair_step, 0)
+    for at in later[pairs:]:
+        tick(at)
+    for ticks in chains[NEEDED_FIRST:]:
+        run_events(ticks[TICKS - 1])
+    keep.wait()
+    for _, finish in moves:
+        finish()
+
+
+def gather(blocks, frames, text, target, block, real, slots):
     count = len(blocks)
-    spec = pl.BlockSpec((rows, LANES), lambda p: (0, p))
+    rows, width = 2 * frames.shape[0], frames.shape[1]
+    share = blocks[1].shape[1]
+    pairs = share // LANES
+    crossings = count + 4
     dma = pltpu.SemaphoreType.DMA
+    vmem = pl.BlockSpec(memory_space=pltpu.VMEM)
+    heads = jax.ShapeDtypeStruct((rows, share), BRAIN)
+    gathered = [jax.ShapeDtypeStruct((4, 2, 2, *b.shape), BRAIN) for b in blocks]
     return pl.pallas_call(
-        functools.partial(gather_attend_kernel, slots, count, pairs, rows // 2, real),
-        grid=(pairs,),
-        in_specs=[spec, spec, spec] + [ANY] * count,
-        out_specs=[spec, pl.BlockSpec((1, 8, rows), lambda p: (p, 0, 0))] + [ANY] * count,
+        functools.partial(gather_kernel, slots, count, real),
         out_shape=[
-            jax.ShapeDtypeStruct((rows, width), BRAIN),
-            jax.ShapeDtypeStruct((pairs, 8, rows), FLOAT),
-            *[jax.ShapeDtypeStruct((4, 2, 2, *b.shape), BRAIN) for b in blocks],
+            *gathered,
+            *[jax.ShapeDtypeStruct(v.shape, v.dtype) for v in (frames, text, target, block)],
+            jax.ShapeDtypeStruct((8, width), FLOAT), jax.ShapeDtypeStruct((rows, width), BRAIN),
+            heads, heads, heads, heads, jax.ShapeDtypeStruct((pairs, 8, rows), FLOAT),
         ],
+        in_specs=[ANY] * (count + 4),
+        out_specs=[ANY] * (count + 4) + [vmem] * 7,
         scratch_shapes=[
-            dma((len(slots), 3, 5)), dma((len(slots), 3, 5)), dma((count,)), dma((count,)), dma((count,)),
+            dma((len(slots), 3, 5)), dma((len(slots), 3, 5)),
+            dma((crossings,)), dma((crossings,)), dma((crossings,)), dma, dma, dma((5,)),
+            pltpu.VMEM(gathered[0].shape, BRAIN), pltpu.VMEM((2, *frames.shape), BRAIN),
+            pltpu.VMEM((3, *gathered[1].shape), BRAIN),
         ],
         compiler_params=pltpu.CompilerParams(
-            collective_id=2, has_side_effects=True, vmem_limit_bytes=48 * 2**20
+            collective_id=1, has_side_effects=True, vmem_limit_bytes=56 * 2**20
         ),
-        name="gather_attend",
-    )(q, k, v, *blocks)
+        name="gather",
+    )(*blocks, frames, text, target, block)
 
 
 def plus(*terms):
@@ -479,26 +505,36 @@
             if order == "xyz":
                 leads = [(2, 2, 2), (2, 2), (2, 2), (2, 2), (2,), ()]
             else:
-                leads = [(4, 2), (4, 2), (4,), (), (), (), ()]
+                leads = [(4,), (4,), (), (), (), ()]
             shapes += [pltpu.VMEM((*lead, rows, size), BRAIN) for lead in leads]
     return shapes
 
 
-def sum_events(where, slots, terms, outs, buffers, crossing, send, recv, local):
+def sum_landings(slots, rows):
+    return [
+        jax.ShapeDtypeStruct((4, 2, rows, sizes[kind]), BRAIN)
+        for _, _, sizes in slots
+        for kind, order in enumerate(ORDERS)
+        if sizes[kind] and order != "xyz"
+    ]
+
+
+def sum_events(where, slots, terms, outs, landings, buffers, pads, crossing, send, recv, local):
     z, x, c, y, up, down, across = where
     every = slice(None)
     chains = []
-    taken = 0
+    taken = landed = 0
     for number, (which, start, sizes) in enumerate(slots):
         ref, out = terms[which], outs[which]
         ticks = [[] for _ in range(TICKS + 1)]
+        after, later = [], []
         for kind, order in enumerate(ORDERS):
             size = sizes[kind]
             if size == 0:
                 continue
             columns = pl.ds(start, size)
             start += size
-            need = 6 if order == "xyz" else 7
+            need = 6
             held = buffers[taken : taken + need]
             taken += need
 
@@ -545,29 +581,36 @@
                 ticks[4] += [s_x.wait, add_x]
                 final = from_x
             else:
-                own, from_first, from_second, from_two, from_down, from_up, total = held
+                from_second, far, from_two, from_down, from_up, total = held
+                landing = landings[landed]
+                landed += 1
+                mine_at, got_at = (pad.at[every, every, pl.ds(0, size)] for pad in pads[kind])
+                mine_pad, got_pad = pads[kind]
                 if order == "zxy":
-                    mine, theirs = view(every, every, y), view(every, every, 1 - y)
+                    mine, theirs = view(every, 1 - x, y), view(every, every, 1 - y)
                     first, second = {"y": 1 - y}, {"x": 1 - x}
                     side = x
                 else:
-                    mine, theirs = view(every, x, every), view(every, 1 - x, every)
+                    mine, theirs = view(every, x, 1 - y), view(every, 1 - x, every)
                     first, second = {"x": 1 - x}, {"y": 1 - y}
                     side = y
-                load = pltpu.make_async_copy(mine, own, local.at[number, kind, 0])
-                s_first = copy(0, theirs, from_first, first)
-                s_second = copy(1, own.at[every, 1 - side], from_second, second)
+                load_mine = pltpu.make_async_copy(mine, mine_at, local.at[number, kind, 0])
+                load_got = pltpu.make_async_copy(landing.at[every, 1 - side], got_at, local.at[number, kind, 1])
+                load_near = pltpu.make_async_copy(view(every, x, y), mine_at, local.at[number, kind, 2])
+                load_rest = pltpu.make_async_copy(landing.at[every, side], got_at, local.at[number, kind, 3])
+                s_first = copy(0, theirs, landing, first)
+                s_second = copy(1, far, from_second, second)
                 s_three = copy(2, from_second.at[up], from_down, {"z": up})
                 s_two = copy(3, from_second.at[across], from_two, {"z": down})
                 s_one = copy(4, from_second.at[down], from_up, {"z": down})
 
-                def add_first(own=own, got=from_first, side=side):
+                def add_first(mine=mine_pad, got=got_pad, size=size, far=far):
                     for i in range(4):
-                        own[i, 1 - side] = plus(own[i, 1 - side], got[i, 1 - side])
-
-                def add_second(own=own, got=from_first, more=from_second, side=side):
+                        far[i] = plus(mine[i, :, :size], got[i, :, :size])
+
+                def add_second(mine=mine_pad, got=got_pad, size=size, more=from_second):
                     for i in range(4):
-                        more[i] = plus(own[i, side], got[i, side], more[i])
+                        more[i] = plus(mine[i, :, :size], got[i, :, :size], more[i])
 
                 def add_two(more=from_second, two=from_two):
                     more[down] = plus(more[down], two[...])
@@ -575,9 +618,11 @@
                 def add_z(more=from_second, a=from_down, b=from_up, total=total):
                     total[...] = plus(more[z], a[...], b[...])
 
-                ticks[0] += [load.start, s_first.start]
-                ticks[1] += [s_first.wait, load.wait, add_first, s_second.start]
-                ticks[2] += [s_second.wait, add_second, s_three.start, s_two.start]
+                ticks[0] += [s_first.start]
+                ticks[1] += [s_first.wait, load_mine.start, load_got.start]
+                after += [load_mine.wait, load_got.wait, add_first, s_second.start]
+                ticks[2] += [s_second.wait, load_near.start, load_rest.start]
+                later += [load_near.wait, load_rest.wait, add_second, s_three.start, s_two.start]
                 ticks[3] += [s_two.wait, add_two, s_one.start]
                 ticks[4] += [s_three.wait, s_one.wait, add_z]
                 final = total
@@ -585,176 +630,291 @@
             leave, left = crossing.prepare(final, out.at[every, columns])
             ticks[4] += [leave]
             ticks[5] += [left]
+        ticks[1] += after
+        ticks[2] += later
         chains.append(ticks)
     return chains
 
 
-def run_sum_tick(chains, at):
-    for number, ticks in enumerate(chains):
-        if 0 <= at - number < TICKS + 1:
-            for event in ticks[at - number]:
-                event()
-
-
-def sum_attend_kernel(slots, count, pairs, half, real, q_ref, k_ref, v_ref, do_ref, o_ref, lse_ref, *refs):
-    terms, frames = refs[:count], refs[count]
-    refs = refs[count + 1 :]
-    dq_ref, dk_ref, dv_ref = refs[:3]
-    outs, frames_out = refs[3 : 3 + count], refs[3 + count]
-    refs = refs[4 + count :]
-    work, refs = refs[:4], refs[4:]
-    send, recv, local, cross_send, cross_recv, cross_local = refs[:6]
+def sum_order(count):
+    shares = ((1, 0.5), (2, 0.27), (3, 0.08), (4, 0.1), (5, 0.05))
+    order = []
+    passed = 0.0
+    for tick, part in shares:
+        order += [(n, tick, passed + part * (n + 1) / count) for n in range(count)]
+        passed += part
+    return order
+
+
+def run_events(events):
+    for event in events:
+        event()
+
+
+def sum_kernel(slots, count, real, *refs):
+    terms, refs = refs[:count], refs[count:]
+    home, block, q, k, v, do, o, h, w_q, w_k, w_v, x0, dx1, lse, gains, vectors = refs[:16]
+    refs = refs[16:]
+    outs, (home_out, frames_out, block_out, vectors_out) = refs[: count + 3], refs[count + 3 : count + 7]
+    refs = refs[count + 7 :]
+    lands = len([1 for _, _, sizes in slots for kind, order in enumerate(ORDERS) if sizes[kind] and order != "xyz"])
+    landings, refs = refs[:lands], refs[lands:]
+    send, recv, local, cross_send, cross_recv, cross_local, v_send, v_recv, h_send, h_recv, loads = refs[:11]
+    four, ring, pad_a, pad_b, pad_c, pad_d, grads, grad_terms, far, got, near = refs[11:22]
+    half, width = x0.shape
+    rows, share = q.shape
+    pairs = share // LANES
+    tiles = rows // ROWS
+    quarter = width // 4
     where = whereabouts()
     z, x, c, y, up, down, across = where
+    every = slice(None)
     crossing = Crossing(c, y, cross_send, cross_recv, cross_local)
-    chains = sum_events(where, slots, terms, outs, refs[6:], crossing, send, recv, local)
-    frames_start, frames_finish = crossing.prepare(frames, frames_out)
-    ticks = len(slots) + TICKS
-    step = pl.program_id(0)
-    blocks = 2 * half // ROWS
+    all_terms = [*terms, *(grad_terms.at[i] for i in range(3))]
+    pads = ((pad_a, pad_b), (pad_c, pad_d))
+    chains = sum_events(where, slots, all_terms, outs, landings, refs[22:], pads, crossing, send, recv, local)
+    early = [n for n, slot in enumerate(slots) if slot[0] < count]
+    late = [n for n, slot in enumerate(slots) if slot[0] >= count]
+    home_start, home_finish = crossing.prepare(home, home_out)
+    block_start, block_finish = crossing.prepare(block, block_out)
+    frames_start, frames_finish = crossing.prepare(far, frames_out)
+    greet(c, y, up, down, x, True)
+    for n in early:
+        run_events(chains[n][0])
+    block_start()
+    home_start()
+
+    work = tiles * (tiles + 1) // 2
+    times = [p + sum(tiles - i for i in range(j)) / work for p in range(pairs) for j in range(tiles)]
+    times += [pairs + 0.5 * i for i in range(1, 5)]
     spots = {}
-    for at in range(ticks - 1):
-        spot = at * pairs * blocks // ticks
-        spots.setdefault(spot, []).append(at)
-
-    def hook(j):
-        for turn in range(pairs):
-            here = spots.get(turn * blocks + j, [])
-            if here:
-                @pl.when(step == turn)
-                def _(here=here):
-                    for at in here:
-                        if at == 0:
-                            greet(c, y, up, down, x, False)
-                            frames_start()
-                        run_sum_tick(chains, at)
-
-    attend_back_kernel(
-        half, real, q_ref, k_ref, v_ref, do_ref, o_ref, lse_ref, dq_ref, dk_ref, dv_ref, *work, hook=hook
+    for number, tick, part in sum_order(len(early)):
+        due = part * SUM_TIME * pairs
+        later = [i for i, time in enumerate(times) if time >= due]
+        spots.setdefault(later[0] if later else len(times), []).append((early[number], tick))
+
+    def at_spot(spot):
+        for number, tick in spots.get(spot, []):
+            run_events(chains[number][tick])
+
+    def attention(pair_in, dq_sum, dk_sum, dv_sum, inner):
+        def load(p, i):
+            lanes = pl.ds(pl.multiple_of(p * LANES, LANES), LANES)
+            slot = lax.rem(p, 2)
+            source = (q, k, v, do, o)[i]
+            return pltpu.make_async_copy(source.at[every, lanes], pair_in.at[slot, i], loads.at[slot, i])
+
+        for i in range(5):
+            load(0, i).start()
+
+        def pair_step(p, carry):
+            @pl.when(p + 1 < pairs)
+            def _():
+                for i in range(5):
+                    load(p + 1, i).start()
+
+            for i in range(5):
+                load(p, i).wait()
+
+            def hook(j):
+                for turn in range(pairs):
+                    if turn * tiles + j in spots:
+                        @pl.when(p == turn)
+                        def _(turn=turn):
+                            at_spot(turn * tiles + j)
+
+            lanes = pl.ds(pl.multiple_of(p * LANES, LANES), LANES)
+            slot = lax.rem(p, 2)
+            attend_back_kernel(
+                half, real, *(pair_in.at[slot, i] for i in range(5)), lse.at[pl.ds(p, 1)],
+                *(grads.at[i, every, lanes] for i in range(3)), dq_sum, dk_sum, dv_sum, inner, hook=hook,
+            )
+            return carry
+
+        lax.fori_loop(0, pairs, pair_step, 0)
+
+    pl.run_scoped(
+        attention,
+        pltpu.VMEM((2, 5, rows, LANES), BRAIN), pltpu.VMEM((rows, LANES), FLOAT),
+        pltpu.VMEM((ROWS, LANES), FLOAT), pltpu.VMEM((ROWS, LANES), FLOAT), pltpu.VMEM((8, rows), FLOAT),
     )
 
-    @pl.when(step == pairs - 1)
-    def _():
-        run_sum_tick(chains, ticks - 1)
-        frames_finish()
-
-
-def sum_attend(q, k, v, do, o, lse, real, terms, frames, slots):
-    rows, width = q.shape
-    pairs = width // LANES
+    def exchange(part):
+        columns = pl.ds(part * quarter, quarter)
+        return pltpu.make_async_remote_copy(
+            src_ref=far.at[every, columns], dst_ref=got.at[every, columns], send_sem=h_send.at[part],
+            recv_sem=h_recv.at[part], device_id={"c": 1 - c}, device_id_type=MESH,
+        )
+
+    def projections(h_in, w_in):
+        def load(part, i):
+            slot = part % 2
+            if i == 3:
+                return pltpu.make_async_copy(h.at[every, pl.ds(part * quarter, quarter)], h_in.at[slot], loads.at[slot, 3])
+            return pltpu.make_async_copy((w_q, w_k, w_v)[i].at[part], w_in.at[slot, i], loads.at[slot, i])
+
+        for i in range(4):
+            load(0, i).start()
+        for part in range(4):
+            if part < 3:
+                for i in range(4):
+                    load(part + 1, i).start()
+            for i in range(4):
+                load(part, i).wait()
+            slot = part % 2
+            columns = pl.ds(part * quarter, quarter)
+
+            def grad_step(i, carry, part=part, slot=slot):
+                product = dot_tn(h_in[slot], grads[i]).astype(BRAIN)
+                grad_terms[i, part] = product.reshape(grad_terms.shape[2:])
+                return carry
+
+            def back_step(r, carry, slot=slot, columns=columns, out=None, base=0):
+                here = pl.ds(pl.multiple_of(r * ROWS, ROWS), ROWS)
+                there = pl.ds(pl.multiple_of(base + r * ROWS, ROWS), ROWS)
+                total = dot_nt(grads[0, there, :], w_in[slot, 0].reshape(quarter, share))
+                for i in (1, 2):
+                    total = total + dot_nt(grads[i, there, :], w_in[slot, i].reshape(quarter, share))
+                out[here, columns] = total.astype(out.dtype)
+                return carry
+
+            lax.fori_loop(0, half // ROWS, functools.partial(back_step, out=far, base=half), 0)
+            exchange(part).start()
+            lax.fori_loop(0, half // ROWS, functools.partial(back_step, out=near), 0)
+            lax.fori_loop(0, 3, grad_step, 0)
+            at_spot(pairs * tiles + part)
+
+    pl.run_scoped(
+        projections, pltpu.VMEM((2, rows, quarter), BRAIN), pltpu.VMEM((2, 3, *w_q.shape[1:]), BRAIN)
+    )
+    for n in late:
+        run_events(chains[n][0])
+    for part in range(4):
+        exchange(part).wait()
+    four[...] = vectors[...]
+
+    def norm(x_in, dx_in):
+        size = x_in.shape[1]
+
+        def load(i):
+            slot = lax.rem(i, 2)
+            here = pl.ds(pl.multiple_of(i * size, size), size)
+            return (
+                pltpu.make_async_copy(x0.at[here], x_in.at[slot], loads.at[slot, 0]),
+                pltpu.make_async_copy(dx1.at[here], dx_in.at[slot], loads.at[slot, 1]),
+            )
+
+        for copy in load(0):
+            copy.start()
+
+        def step(i, carry):
+            @pl.when(i + 1 < half // size)
+            def _():
+                for copy in load(i + 1):
+                    copy.start()
+
+            for copy in load(i):
+                copy.wait()
+            slot = lax.rem(i, 2)
+            here = pl.ds(pl.multiple_of(i * size, size), size)
+            flow = near[here, :].astype(FLOAT) + got[here, :].astype(FLOAT)
+            values, gain_sum, bias_sum = norm_back(x_in[slot].astype(FLOAT), gains[0:1, :], flow)
+            far[here, :] = (dx_in[slot] + values).astype(BRAIN)
+            four[0:1, :] += gain_sum[None, :]
+            four[1:2, :] += bias_sum[None, :]
+            return carry
+
+        lax.fori_loop(0, half // size, step, 0)
+
+    pl.run_scoped(norm, pltpu.VMEM((2, 96, width), BRAIN), pltpu.VMEM((2, 96, width), FLOAT))
+    frames_start()
+
+    def hop(at, src, dst, partner):
+        return pltpu.make_async_remote_copy(
+            src_ref=src, dst_ref=dst, send_sem=v_send.at[at], recv_sem=v_recv.at[at],
+            device_id=partner, device_id_type=MESH,
+        )
+
+    held = ring
+    held[0] = four[...]
+    for at, partner in enumerate(({"c": 1 - c}, {"y": 1 - y}, {"x": 1 - x})):
+        turn = hop(at, held.at[2 * at], held.at[2 * at + 1], partner)
+        turn.start()
+        turn.wait()
+        total = held[2 * at] + held[2 * at + 1]
+        if at < 2:
+            held[2 * at + 2] = total
+        else:
+            held[6 + z] = total
+    z_up = hop(3, held.at[6 + z], held.at[6 + z], {"z": up})
+    z_down = hop(4, held.at[6 + z], held.at[6 + z], {"z": down})
+    z_more = hop(5, held.at[6 + down], held.at[6 + down], {"z": up})
+    z_up.start()
+    z_down.start()
+    z_up.wait()
+    z_more.start()
+    for number, tick in spots.get(len(times), []):
+        run_events(chains[number][tick])
+    for tick in range(1, TICKS + 1):
+        for n in late:
+            run_events(chains[n][tick])
+    z_down.wait()
+    z_more.wait()
+    vectors_out[...] = (held[6] + held[7]) + (held[8] + held[9])
+    home_finish()
+    block_finish()
+    frames_finish()
+
+
+def sum_gradients(terms, home, block, attention, h, weights, x0, dx1, lse, gains, vectors, real, slots):
     count = len(terms)
-    block = terms[0].shape[3]
-    spec = pl.BlockSpec((rows, LANES), lambda p: (0, p))
+    rows, share = attention[0].shape
+    half, width = x0.shape
+    size = terms[0].shape[3]
+    crossings = 3 * len(slots) + 3
     dma = pltpu.SemaphoreType.DMA
-    crossings = 3 * len(slots) + 1
-    return pl.pallas_call(
-        functools.partial(sum_attend_kernel, slots, count, pairs, rows // 2, real),
-        grid=(pairs,),
-        in_specs=[spec] * 5
-        + [pl.BlockSpec((1, 8, rows), lambda p: (p, 0, 0))] + [ANY] * (count + 1),
-        out_specs=[spec] * 3 + [ANY] * (count + 1),
-        out_shape=[jax.ShapeDtypeStruct((rows, width), BRAIN)] * 3
-        + [jax.ShapeDtypeStruct((block, t.shape[4]), BRAIN) for t in terms]
-        + [jax.ShapeDtypeStruct(frames.shape, BRAIN)],
+    vmem = pl.BlockSpec(memory_space=pltpu.VMEM)
+    landings = sum_landings(slots, size)
+    widths = [t.shape[4] for t in terms] + [share] * 3
+    most = [max(sizes[kind] for _, _, sizes in slots) for kind in range(2)]
+    results = pl.pallas_call(
+        functools.partial(sum_kernel, slots, count, real),
+        in_specs=[ANY] * (count + 13) + [vmem] * 3,
+        out_specs=[ANY] * (count + 6) + [vmem] + [ANY] * len(landings),
+        out_shape=[jax.ShapeDtypeStruct((size, n), BRAIN) for n in widths]
+        + [jax.ShapeDtypeStruct(home.shape, BRAIN), jax.ShapeDtypeStruct(x0.shape, BRAIN)]
+        + [jax.ShapeDtypeStruct(block.shape, BRAIN), jax.ShapeDtypeStruct(vectors.shape, FLOAT)]
+        + landings,
         scratch_shapes=[
-            pltpu.VMEM((rows, LANES), FLOAT), pltpu.VMEM((ROWS, LANES), FLOAT),
-            pltpu.VMEM((ROWS, LANES), FLOAT), pltpu.VMEM((8, rows), FLOAT),
-            dma((len(slots), 3, 5)), dma((len(slots), 3, 5)), dma((len(slots), 3, 2)),
-            dma((crossings,)), dma((crossings,)), dma((crossings,)),
-            *sum_scratch(slots, block),
+            dma((len(slots), 3, 5)), dma((len(slots), 3, 5)), dma((len(slots), 3, 4)),
+            dma((crossings,)), dma((crossings,)), dma((crossings,)), dma((6,)), dma((6,)),
+            dma((4,)), dma((4,)), dma((2, 5)),
+            pltpu.VMEM(vectors.shape, FLOAT), pltpu.VMEM((10, *vectors.shape), FLOAT),
+            *[pltpu.VMEM((4, size, most[kind]), BRAIN) for kind in (0, 0, 1, 1)],
+            pltpu.VMEM((3, rows, share), BRAIN), pltpu.VMEM((3, 4, 2, 2, size, share), BRAIN),
+            pltpu.VMEM((half, width), BRAIN), pltpu.VMEM((half, width), BRAIN), pltpu.VMEM((half, width), BRAIN),
+            *sum_scratch(slots, size),
         ],
         compiler_params=pltpu.CompilerParams(
             collective_id=3, has_side_effects=True, vmem_limit_bytes=58 * 2**20
         ),
-        name="sum_attend",
-    )(q, k, v, do, o, lse, *terms, frames)
-
-
-def sum_last_kernel(slots, count, *refs):
-    terms, (frames, vectors) = refs[:count], refs[count : count + 2]
-    refs = refs[count + 2 :]
-    outs, (frames_out, vectors_out) = refs[:count], refs[count : count + 2]
-    refs = refs[count + 2 :]
-    send, recv, local, cross_send, cross_recv, cross_local, v_send, v_recv, held, four = refs[:10]
-    where = whereabouts()
-    z, x, c, y, up, down, across = where
-    greet(c, y, up, down, x, True)
-    crossing = Crossing(c, y, cross_send, cross_recv, cross_local)
-    chains = sum_events(where, slots, terms, outs, refs[10:], crossing, send, recv, local)
-    frames_finish = crossing.begin(frames, frames_out)
-
-    def copy(at, src, dst, partner):
-        return pltpu.make_async_remote_copy(
-            src_ref=src, dst_ref=dst, send_sem=v_send.at[at], recv_sem=v_recv.at[at],
-            device_id=partner, device_id_type=MESH,
-        )
-
-    run_sum_tick(chains, 0)
-    held[0] = vectors[...]
-    for at, partner in enumerate(({"c": 1 - c}, {"y": 1 - y}, {"x": 1 - x})):
-        hop = copy(at, held.at[2 * at], held.at[2 * at + 1], partner)
-        hop.start()
-        hop.wait()
-        total = held[2 * at] + held[2 * at + 1]
-        if at < 2:
-            held[2 * at + 2] = total
-        else:
-            four[z] = total
-    run_sum_tick(chains, 1)
-    z_up, z_down = copy(3, four.at[z], four.at[z], {"z": up}), copy(4, four.at[z], four.at[z], {"z": down})
-    z_more = copy(5, four.at[down], four.at[down], {"z": up})
-    z_up.start()
-    z_down.start()
-    z_up.wait()
-    z_more.start()
-    for at in range(2, len(slots) + TICKS):
-        run_sum_tick(chains, at)
-    z_down.wait()
-    z_more.wait()
-    vectors_out[...] = (four[0] + four[1]) + (four[2] + four[3])
-    frames_finish()
-
-
-def sum_last(terms, frames, vectors, slots):
-    count = len(terms)
-    block = terms[0].shape[3]
-    dma = pltpu.SemaphoreType.DMA
-    crossings = 3 * len(slots) + 1
-    whole = pl.BlockSpec(memory_space=pltpu.VMEM)
-    return pl.pallas_call(
-        functools.partial(sum_last_kernel, slots, count),
-        in_specs=[ANY] * (count + 1) + [whole],
-        out_specs=[ANY] * (count + 1) + [whole],
-        out_shape=[jax.ShapeDtypeStruct((block, t.shape[4]), BRAIN) for t in terms]
-        + [jax.ShapeDtypeStruct(frames.shape, BRAIN), jax.ShapeDtypeStruct(vectors.shape, FLOAT)],
-        scratch_shapes=[
-            dma((len(slots), 3, 5)), dma((len(slots), 3, 5)), dma((len(slots), 3, 2)),
-            dma((crossings,)), dma((crossings,)), dma((crossings,)), dma((6,)), dma((6,)),
-            pltpu.VMEM((6, *vectors.shape), FLOAT), pltpu.VMEM((4, *vectors.shape), FLOAT),
-            *sum_scratch(slots, block),
-        ],
-        compiler_params=pltpu.CompilerParams(
-            collective_id=4, has_side_effects=True, vmem_limit_bytes=58 * 2**20
-        ),
-        name="sum_last",
-    )(*terms, frames, vectors)
-
-
-def slots_of(widths):
+        name="sum_gradients",
+    )(*terms, home, block, *attention, h, *weights, x0, dx1, lse, gains, vectors)
+    return results[: count + 7]
+
+
+def slots_of(widths, six=((1, 4, 1), (0, 4, 2), (1, 4, 1)), eight=(1, 5, 2), last=None):
     slots = []
     for which, width in enumerate(widths):
         tiles = width // LANES
-        if tiles < 6:
+        ways = last if last and which >= len(widths) - 3 else six
+        if tiles == 6:
+            slots.append((which, 0, tuple(LANES * n for n in ways[len(slots) % len(ways)])))
+        elif tiles % 8 == 0:
+            for at in range(0, tiles, 8):
+                slots.append((which, at * LANES, tuple(LANES * n for n in eight)))
+        else:
             slots.append((which, 0, (width, 0, 0)))
-        elif tiles == 6:
-            sizes = (3, 2, 1) if len(slots) % 2 else (2, 3, 1)
-            slots.append((which, 0, tuple(LANES * s for s in sizes)))
-        else:
-            for at in range(0, tiles, 8):
-                here = min(8, tiles - at)
-                many = -(-3 * here // 8)
-                sizes = (many, min(many, here - many), max(0, here - 2 * many))
-                slots.append((which, at * LANES, tuple(LANES * s for s in sizes)))
     return tuple(slots)
 
 
@@ -819,7 +979,8 @@
     at_core, at_y = lax.axis_index("c"), lax.axis_index("y")
     real, width = inputs.shape[1], inputs.shape[2]
     half = -(-real // ROWS) * ROWS
-    block = self_query.shape[0]
+    block, share = self_query.shape
+    hidden = feed_in.shape[1]
 
     fits = ring_fit()
 
@@ -828,10 +989,18 @@
     digits = jnp.stack([count // 64, count % 64]).astype(BRAIN)
     digits = jnp.where((jnp.arange(block) == 0)[:, None], digits[None, :], jnp.zeros((), BRAIN))
     tiny = jnp.pad(jnp.concatenate([jnp.stack(tiny, 1), digits], 1), ((0, 0), (0, LANES - 8)))
-    early = [tiny, self_query, self_key, self_value, self_out.T, cross_out.T, cross_query, cross_key, cross_value]
-    late = [feed_in, feed_out.T]
-    early_slots = slots_of([v.shape[1] for v in early])
-    late_slots = slots_of([v.shape[1] for v in late])
+    weights = [
+        tiny, self_query, self_key, self_value, self_out.T, cross_query, cross_key, cross_value, cross_out.T, feed_in
+    ]
+    feed_rows = feed_out.T
+
+    def both(own):
+        return jnp.concatenate([own, swap_core(own)], 0)
+
+    def summed(left, weight):
+        far = dot_nt(left[half:], weight).astype(BRAIN)
+        got = swap_core(far)
+        return dot_nt(left[:half], weight) + got.astype(FLOAT)
 
     def padded(v):
         return jnp.pad(v, ((0, half - real), (0, 0)))
@@ -840,41 +1009,27 @@
     flags = jnp.pad(valid_frames[0][:, None].astype(BRAIN), ((0, 0), (0, LANES - 1)))
     target = padded(jnp.concatenate([teacher[0], flags], 1))
     if fits:
-        *early, x_all, target, text = gather_first(early, frames, target, text_states[0], early_slots)
-        early = [joined(v) for v in early]
-        x_all = joined(x_all)
+        slots = slots_of([v.shape[1] for v in weights])
+        *weights, x_own, text, target, feed_rows, gains, h1, q1, k1, v1, o1, lse1 = gather(
+            weights, frames, text_states[0], target, feed_rows, real, slots
+        )
+        weights = [joined(v) for v in weights]
     else:
-        early = [lax.all_gather(swap_clip(v), CHIPS, axis=0, tiled=True) for v in early]
-        x_own = swap_clip(frames)
+        weights = [lax.all_gather(swap_clip(v), CHIPS, axis=0, tiled=True) for v in weights]
+        x_own, text, target, feed_rows = (swap_clip(v) for v in (frames, text_states[0], target, feed_rows))
+        gains = weights[0].T.astype(FLOAT)
         x_all = jnp.concatenate([x_own, swap_core(x_own)], 0)
-        target, text = swap_clip(target), swap_clip(text_states[0])
-    tiny, w_q, w_k, w_v, w_so, w_co, w_cq, w_ck, w_cv = early
+        h1 = normalize(x_all.astype(FLOAT), gains[0], gains[1]).astype(BRAIN)
+        q1, k1, v1 = (dot_nn(h1, w).astype(BRAIN) for w in weights[1:4])
+        o1, lse1 = attend_self(q1, k1, v1, real)
+    tiny, w_q, w_k, w_v, w_so, w_cq, w_ck, w_cv, w_co, w_fi = weights
     counted = jnp.sum(tiny[:, 6:8].astype(FLOAT), 0)
     counted = counted[0] * 64.0 + counted[1]
     token_count = counted + swap_core(counted)
-    gains = tiny.T.astype(FLOAT)
+    w_fo = lax.all_gather(feed_rows, CHIPS, axis=0, tiled=True)
     valid = target[:, width : width + 1].astype(FLOAT)
     target = target[:, :width].astype(FLOAT)
-
-    def both(own):
-        return jnp.concatenate([own, swap_core(own)], 0)
-
-    def summed(left, weight):
-        far = dot_nt(left[half:], weight).astype(BRAIN)
-        got = swap_core(far)
-        return dot_nt(left[:half], weight) + got.astype(FLOAT)
-
-    h1 = normalize(x_all.astype(FLOAT), gains[0], gains[1]).astype(BRAIN)
-    q1 = dot_nn(h1, w_q).astype(BRAIN)
-    k1 = dot_nn(h1, w_k).astype(BRAIN)
-    v1 = dot_nn(h1, w_v).astype(BRAIN)
-    if fits:
-        o1, lse1, *late = gather_attend(q1, k1, v1, real, late, late_slots)
-        w_fi, w_fo = (joined(v) for v in late)
-    else:
-        o1, lse1 = attend_self(q1, k1, v1, real)
-        w_fi, w_fo = (lax.all_gather(swap_clip(v), CHIPS, axis=0, tiled=True) for v in late)
-    x0 = x_all[:half].astype(FLOAT)
+    x0 = x_own.astype(FLOAT)
     x1 = x0 + summed(o1, w_so)
     h2 = both(normalize(x1, gains[2], gains[3]).astype(BRAIN))
     q2 = dot_nn(h2, w_cq).astype(BRAIN)
@@ -892,7 +1047,11 @@
     dy = (2.0 * tokens_all / token_count) * valid * deviation
 
     dyb = both(dy.astype(BRAIN))
-    fo_grad = dot_tn(dyb, g).astype(BRAIN)
+    cut = hidden - share
+    fo_grad = dot_tn(dyb, g[:, :cut]).astype(BRAIN)
+    dyb, fo_grad = lax.optimization_barrier((dyb, fo_grad))
+    fo_grad = lax.psum_scatter(fo_grad, CHIPS, scatter_dimension=0, tiled=True)
+    fo_rest = dot_tn(dyb, g[:, cut:]).astype(BRAIN)
     du = (slope.astype(FLOAT) * dot_nn(dyb, w_fo)).astype(BRAIN)
     fi_grad = dot_tn(h3, du).astype(BRAIN)
     term, gain3, bias3 = norm_back(x2, gains[4], summed(du, w_fi))
@@ -916,38 +1075,33 @@
     dx1b = both(dx1.astype(BRAIN))
     so_grad = dot_tn(dx1b, o1).astype(BRAIN)
     do1 = dot_nn(dx1b, w_so).astype(BRAIN)
-    wide = [fi_grad, fo_grad]
+    zero = jnp.zeros((width,), FLOAT)
+    vectors = jnp.stack([zero, zero, gain2, bias2, gain3, bias3])
+    vectors = jnp.concatenate([vectors, jnp.full((2, width), error)], 0)
+    grads = [fi_grad, fo_rest, co_grad, cq_grad, ck_grad, cv_grad, so_grad]
     if fits:
-        dq1, dk1, dv1, *wide, home = sum_attend(
-            q1, k1, v1, do1, o1, lse1, real, [by_chip(v) for v in wide], home, late_slots
+        slots = slots_of(
+            [v.shape[1] for v in grads] + [w_q.shape[1]] * 3, six=((1, 4, 1), (1, 3, 2)), eight=(1, 5, 2), last=((0, 4, 2),)
+        )
+        *grads, home, frames, fo_grad, vectors = sum_gradients(
+            [by_chip(v) for v in grads], home, fo_grad, (q1, k1, v1, do1, o1), h1,
+            [by_chip(v) for v in (w_q, w_k, w_v)], x_own, dx1, lse1, gains, vectors, real, slots,
         )
     else:
         dq1, dk1, dv1 = attend_self_back(q1, k1, v1, do1, o1, lse1, real)
-        wide = [swap_clip(lax.psum_scatter(v, CHIPS, scatter_dimension=0, tiled=True)) for v in wide]
-        home = swap_clip(home)
+        dh1 = dot_nt(dq1, w_q) + dot_nt(dk1, w_k) + dot_nt(dv1, w_v)
+        dh1 = dh1[:half] + swap_core(dh1[half:].astype(BRAIN)).astype(FLOAT)
+        term, gain1, bias1 = norm_back(x0, gains[0], dh1)
+        frames = swap_clip((dx1 + term).astype(BRAIN))
+        grads += [dot_tn(h1, d).astype(BRAIN) for d in (dq1, dk1, dv1)]
+        grads = [swap_clip(lax.psum_scatter(v, CHIPS, scatter_dimension=0, tiled=True)) for v in grads]
+        home, fo_grad = swap_clip(home), swap_clip(fo_grad)
+        vectors = lax.psum(vectors.at[:2].set(jnp.stack([gain1, bias1])), ("z", "x", "c", "y"))
     layer_out = home[:real][None]
-    fi_grad, fo_grad = (v.astype(FLOAT) for v in wide)
-    dh1_far = dot_nt(dq1[half:], w_q) + dot_nt(dk1[half:], w_k) + dot_nt(dv1[half:], w_v)
-    dh1_got = swap_core(dh1_far.astype(BRAIN))
-    dh1 = dot_nt(dq1[:half], w_q) + dot_nt(dk1[:half], w_k) + dot_nt(dv1[:half], w_v)
-    term, gain1, bias1 = norm_back(x0, gains[0], dh1 + dh1_got.astype(FLOAT))
-    frames = (dx1 + term).astype(BRAIN)
-    q_grad = dot_tn(h1, dq1).astype(BRAIN)
-    k_grad = dot_tn(h1, dk1).astype(BRAIN)
-    v_grad = dot_tn(h1, dv1).astype(BRAIN)
-
-    vectors = jnp.stack([gain1, bias1, gain2, bias2, gain3, bias3])
-    vectors = jnp.concatenate([vectors, jnp.full((2, width), error)], 0)
-    grads = [so_grad, co_grad, cq_grad, ck_grad, cv_grad, q_grad, k_grad, v_grad]
-    if fits:
-        slots = slots_of([v.shape[1] for v in grads])
-        *grads, frames, vectors = sum_last([by_chip(v) for v in grads], frames, vectors, slots)
-    else:
-        grads = [swap_clip(lax.psum_scatter(v, CHIPS, scatter_dimension=0, tiled=True)) for v in grads]
-        frames = swap_clip(frames)
-        vectors = lax.psum(vectors, ("z", "x", "c", "y"))
-    so_grad, co_grad, cq_grad, ck_grad, cv_grad, q_grad, k_grad, v_grad = (v.astype(FLOAT) for v in grads)
-    inputs_grad = frames[:real].astype(FLOAT)[None]
+    inputs_grad = frames[None].astype(FLOAT)[:, :real]
+    fo_grad, *grads = (v.astype(FLOAT) for v in (fo_grad, *grads))
+    fi_grad, fo_rest, co_grad, cq_grad, ck_grad, cv_grad, so_grad, q_grad, k_grad, v_grad = grads
+    fo_grad = jnp.concatenate([fo_grad.T, fo_rest.T], 0)
     loss = vectors[6, 0] / (width * token_count)
     mine = block // 2
     place = (lax.axis_index(("z", "x", "c")) * 2 + at_y) * mine
@@ -956,7 +1110,7 @@
         loss, layer_out, inputs_grad, text_grad,
         norms[0], norms[1], q_grad, k_grad, v_grad, so_grad.T,
         norms[2], norms[3], cq_grad, ck_grad, cv_grad, co_grad.T,
-        norms[4], norms[5], fi_grad, fo_grad.T,
+        norms[4], norms[5], fi_grad, fo_grad,
     )
 
 

time: 1230 us -> 1120 us (0.911)
  Pallas kernels: 824 us -> 678 us
  waiting for transfers between devices: 16.1 us -> 91.3 us
  matrix products: 270 us -> 236 us
  other arithmetic: 56.9 us -> 38.2 us
  between operations: 8.92 us -> 21.9 us
    pallas_call x4 -> x2, Pallas kernels: 824 us -> 678 us  [the longest x1 357 us: sum_gradients(): pl.pallas_call(functools.partial(sum_kernel, slots, count, real), in_spec...]
    all_gather x0 -> x1, waiting for transfers between devices: none -> 43.3 us  [on_device(): w_fo = lax.all_gather(feed_rows, CHIPS, axis=0, tiled=True)]
    reduce_scatter x0 -> x1, waiting for transfers between devices: none -> 21.8 us  [on_device(): fo_grad = lax.psum_scatter(fo_grad, CHIPS, scatter_dimension=0, tiled=True)]
    dot_general x10 -> x7, matrix products: 83.4 us -> 68.4 us  [dot_nn(): lax.dot_general(a, b, (((1,), (0,)), ((), ())), preferred_element_type=FL...]
    dot_general x10 -> x8, matrix products: 79.9 us -> 70.3 us  [dot_tn(): lax.dot_general(a, b, (((0,), (0,)), ((), ())), preferred_element_type=FL...]
    dot_general x18 -> x12, matrix products: 100 us -> 91.8 us  [dot_nt(): lax.dot_general(a, b, (((1,), (1,)), ((), ())), preferred_element_type=FL...]
  transfers between devices with their start and end apart: 14 -> 15, of which waited for: 5 -> 9; matrix products, arithmetic and copies ran while one was open for 10% -> 15% of each run, Pallas kernels for 0% -> 0%
where the time goes in v2:
time: 1120 us; the launch traced here: 1110 us
  Pallas kernels  678 us (61%)
  matrix products  236 us (21%)
  waiting for transfers between devices  91.3 us (8%)
  other arithmetic  38.2 us (3%)
  local copies, waits for them, and re-layouts  32.3 us (3%)
  between operations  21.9 us (2%)
  starting transfers between devices  16.3 us (1%)
    pallas_call x1, Pallas kernels, sum_gradients(): pl.pallas_call(functools.partial(sum_kernel, slots, count, real), in_spec...  357 us
    pallas_call x1, Pallas kernels, gather(): pl.pallas_call(functools.partial(gather_kernel, slots, count, real), out_...  321 us
    dot_general x12, matrix products, dot_nt(): lax.dot_general(a, b, (((1,), (1,)), ((), ())), preferred_element_type=FL...  91.8 us
    dot_general x8, matrix products, dot_tn(): lax.dot_general(a, b, (((0,), (0,)), ((), ())), preferred_element_type=FL...  70.3 us
    dot_general x7, matrix products, dot_nn(): lax.dot_general(a, b, (((1,), (0,)), ((), ())), preferred_element_type=FL...  68.4 us
    all_gather x1, waiting for transfers between devices, on_device(): w_fo = lax.all_gather(feed_rows, CHIPS, axis=0, tiled=True)  43.3 us
    ppermute x12, waiting for transfers between devices, swap_core(): return lax.ppermute(v, 'c', [(0, 1), (1, 0)])  23.7 us
  transfers between devices with their start and end apart: 15, of which 9 were waited for; matrix products, arithmetic and copies ran while one was open for 15% of the time, Pallas kernels for 0%

profile of v2, /device:TPU:1, one launch (start us, length us, event | category | flops | bytes accessed | tf_op | source)
XLA Modules:
  0.0 1114.0 jit_solution(6765668073896950726)
XLA Ops:
  18.3 321.4 %gather.1 = (bf16[4,2,2,96,128]{4,3,2,1,0:T(8,128)(2,1)}, bf16[4,2,2,96,768]{4,3,2,1,0:T(8,128)(2,1)}, bf16[4,2,2,96,768]{4,3,2,1,0:T(8,128)(2,1)}, bf16[4,2,2,9...) custom-call(bf16[96,128]{1,0:T(8,128)(2,1)} %pad.16.refs_0_, ...), custom_call_target="tpu_custom_call" | custom-call | tf_op jit(solution)/shard_map/gather/pallas_call | solution.py:468
  339.7 5.6 convolution_convert_fusion.14
  345.3 6.5 collective-permute-start
  369.6 7.0 convolution_convert_fusion.13
  382.2 12.6 %convolution_convert_fusion.11 = bf16[768,1536]{1,0:T(8,128)(2,1)S(1)} fusion(bf16[768,768]{0,1:T(8,128)(2,1)S(1)} %bitcast.158, bf16[1536,768]{1,0:T(8,128)(2,1)S(1)} %bitcast.186), kind=kOutput, calls=%fused_computation.68 | convolution fusion | flops 1813118976 | bytes 5898240 | tf_op jit(solution)/shard_map/dot_general | solution.py:45
  409.9 21.2 %multiply_convert_fusion.1 = (bf16[1536,3072]{1,0:T(8,128)(2,1)}, f32[1536,3072]{1,0:T(8,128)}) fusion(bf16[1536,3072]{1,0:T(8,128)(2,1)S(1)} %bitcast.179, bf16[768,1536]{1,0:T(8,128)(2,1)S(1)} %collective-permute-done.3, bf16[768,1536]{1,0:T(8,128)(2,1)S(1)} %add_convert_fusion), kind=kOutput, calls=%fused_computation.7 | convolution fusion | flops 14528544768 | bytes 42467328 | tf_op jit(solution)/shard_map/dot_general | solution.py:49
  431.2 43.3 %all-gather.2.cloned.1.call-done = bf16[1536,3072]{1,0:T(8,128)(2,1)} async-done(((bf16[96,3072]{1,0:T(8,128)(2,1)}), bf16[1536,3072]{1,0:T(8,128)(2,1)}) %all-gather.2.cloned.1.call-update) | async-done | bytes 9437200 | tf_op jit(solution)/shard_map/all_gather | solution.py:1029
  474.4 12.7 %fusion.18 = bf16[768,1536]{1,0:T(8,128)(2,1)} fusion(bf16[1536,3072]{1,0:T(8,128)(2,1)} %all-gather.2.cloned.1.call-done, bf16[1536,3072]{1,0:T(8,128)(2,1)} %get-tuple-element.195), kind=kOutput, calls=%fused_computation.72 | convolution fusion | flops 7248936960 | bytes 16515072 | tf_op jit(solution)/shard_map/dot_general | solution.py:45
  493.4 14.6 %fusion.7 = (f32[]{:T(128)}, f32[768,1536]{1,0:T(8,128)S(1)}) fusion(f32[768]{0:T(1024)S(1)} %get-tuple-element.162, bf16[768,1664]{1,0:T(8,128)(2,1)S(1)} %copy-done.4, f32[768,1536]{1,0:T(8,128)} %copy-done.2, bf16[768,1536]{1,0:T(8,128)(2,1)} %collective-permute-done.5, bf16[1536,3072]{1,0:T(8,128)(2,1)} %all-gather.2.cloned.1.call-done, ...), kind=kOutput, calls=%fused_computation.15 | convolution fusion | flops 7257194496 | bytes 28314628 | tf_op jit(solution)/shard_map/dot_general | solution.py:45
  517.2 16.3 %convolution_convert_fusion.1 = bf16[1536,2304]{1,0:T(8,128)(2,1)} fusion(bf16[1536,3072]{1,0:T(8,128)(2,1)} %get-tuple-element.195, bf16[768,1536]{1,0:T(8,128)(2,1)S(1)} %collective-permute-done.6, bf16[768,1536]{1,0:T(8,128)(2,1)S(1)} %multiply_convert_fusion.4), kind=kOutput, calls=%fused_computation.10 | convolution fusion | flops 10884612096 | bytes 18874368 | tf_op jit(solution)/shard_map/dot_general | solution.py:53
  533.6 25.2 %multiply_convert_fusion = bf16[1536,3072]{1,0:T(8,128)(2,1)S(1)} fusion(f32[1536,3072]{1,0:T(8,128)} %get-tuple-element.196, bf16[1536,1536]{1,0:T(8,128)(2,1)} %pad_maximum_fusion.2, bf16[1536,3072]{1,0:T(8,128)(2,1)} %all-gather.2.cloned.1.call-done), kind=kOutput, calls=%fused_computation.6 | convolution fusion | flops 14552137728 | bytes 42467328 | tf_op jit(solution)/shard_map/dot_general | solution.py:49
  558.8 14.7 %fusion.21 = bf16[768,1536]{1,0:T(8,128)(2,1)} fusion(bf16[1536,3072]{1,0:T(8,128)(2,1)} %bitcast.175, bf16[1536,3072]{1,0:T(8,128)(2,1)S(1)} %multiply_convert_fusion), kind=kOutput, calls=%fused_computation.73 | convolution fusion | flops 7248936960 | bytes 16515072 | tf_op jit(solution)/shard_map/dot_general | solution.py:45
  578.5 15.1 %multiply_reduce_fusion = (f32[1536]{0:T(1024)S(1)}, f32[768]{0:T(1024)S(1)}, f32[768]{0:T(1024)S(1)}, f32[1536]{0:T(1024)S(1)}, f32[768,1536]{1,0:T(8,128)S(1)}) fusion(f32[768,1536]{1,0:T(8,128)} %copy-done.2, f32[768]{0:T(1024)S(1)} %copy-done.53, f32[768]{0:T(1024)S(1)} %copy-done.49, bf16[768,1536]{1,0:T(8,128)(2,1)} %collective-permute-done.7, ...), kind=kOutput, calls=%fused_computation.29 | convolution fusion | flops 7260728832 | bytes 25982976 | tf_op jit(solution)/shard_map/dot_general | solution.py:45
  593.7 9.0 fusion.55
  603.1 21.1 %convolution_convert_fusion = bf16[1536,3072]{1,0:T(8,128)(2,1)} fusion(bf16[1536,3072]{1,0:T(8,128)(2,1)} %copy-done.61, bf16[768,1536]{1,0:T(8,128)(2,1)} %copy-done.58, bf16[768,1536]{1,0:T(8,128)(2,1)} %copy-done.17), kind=kOutput, calls=%fused_computation.9 | convolution fusion | flops 14509670400 | bytes 23592960 | tf_op jit(solution)/shard_map/dot_general | solution.py:53
  624.2 5.4 convolution_convert_fusion.8
  637.5 7.3 convolution_convert_fusion.10
  658.0 5.5 convolution_convert_fusion.9
  663.6 7.8 convolution_convert_fusion.7
  684.0 8.5 convolution_convert_fusion.2.refs_12_
  692.5 7.8 convolution_convert_fusion.3
  700.3 21.8 %reduce-scatter.2.cloned.1.call-done.refs_8_ = bf16[96,2304]{1,0:T(8,128)(2,1)} async-done(((bf16[1536,2304]{1,0:T(8,128)(2,1)}), bf16[96,2304]{1,0:T(8,128)(2,1)}) %reduce-scatter.2.cloned.1.call-update) | async-done | bytes 442384 | tf_op jit(solution)/shard_map/reduce_scatter | solution.py:1053
  722.1 356.6 %sum_gradients.1 = (bf16[96,3072]{1,0:T(8,128)(2,1)}, bf16[96,768]{1,0:T(8,128)(2,1)}, bf16[96,768]{1,0:T(8,128)(2,1)}, bf16[96,768]{1,0:T(8,128)(2,1)}, bf16[96...) custom-call(bf16[4,2,2,96,3072]{4,3,2,1,0:T(8,128)(2,1)} %bitcast.13, ...), custom_call_target="tpu_custom_call" | custom-call | tf_op jit(solution)/shard_map/sum_gradients/pallas_call | solution.py:880
  1094.6 9.3 copy.69
  (262 shorter events, 115.7 us)
Async XLA Ops:
  7.2 467.2 %all-gather.2.cloned.1.call-start = ((), (), s32[]{:S(2)}) async-start(), calls=%async_computation.1 | async-start | bytes 10027008 | tf_op jit(solution)/shard_map/all_gather | solution.py:1029
  345.3 11.0 collective-permute-start
  351.8 370.3 %reduce-scatter.2.cloned.1.call-start = ((), (), s32[]{:S(2)}) async-start(), calls=%async_computation.2 | async-start | bytes 7520256 | tf_op jit(solution)/shard_map/reduce_scatter | solution.py:1053
  352.2 50.3 %copy-start.44 = (f32[1536]{0:T(1024)}, f32[1536]{0:T(1024)S(1)}, u32[]{:S(2)}) copy-start(f32[1536]{0:T(1024)S(1)} %get-tuple-element.164) | copy-start | bytes 18436
  364.7 4.9 collective-permute-start.1
  381.1 18.4 %slice-start.2 = ((s8[4718592]{0:T(1024)(128)(4,1)}), s8[4194304]{0:T(1024)(128)(4,1)S(1)}, s32[]{:S(2)}) async-start(s8[4718592]{0:T(1024)(128)(4,1)} %bitcast.122), calls=%async_computation.5 | async-start | bytes 8388608
  394.9 4.6 collective-permute-start.2
  404.0 4.5 collective-permute-start.3
  474.4 18.8 %copy-start.4 = (bf16[768,1664]{1,0:T(8,128)(2,1)S(1)}, bf16[768,1664]{1,0:T(8,128)(2,1)}, u32[]{:S(2)}) copy-start(bf16[768,1664]{1,0:T(8,128)(2,1)} %get-tuple-element.68) | copy-start | bytes 7667716
  487.1 6.3 collective-permute-start.5
  490.5 2.0 collective-permute-start.4
  510.3 4.5 collective-permute-start.6
  573.6 4.9 collective-permute-start.7
  574.0 19.7 %slice-start.6 = ((s8[4718592]{0:T(1024)(128)(4,1)}), s8[524288]{0:T(1024)(128)(4,1)S(1)}, s32[]{:S(2)}) async-start(s8[4718592]{0:T(1024)(128)(4,1)} %bitcast.126), calls=%async_computation.9 | async-start | bytes 1048576
  574.0 19.7 %slice-start.7 = ((s8[4718592]{0:T(1024)(128)(4,1)}), s8[4194304]{0:T(1024)(128)(4,1)S(1)}, s32[]{:S(2)}) async-start(s8[4718592]{0:T(1024)(128)(4,1)} %bitcast.126), calls=%async_computation.10 | async-start | bytes 8388608
  593.7 35.9 %slice-start = ((s8[4718592]{0:T(1024)(128)(4,1)}), s8[4194304]{0:T(1024)(128)(4,1)S(1)}, s32[]{:S(2)}) async-start(s8[4718592]{0:T(1024)(128)(4,1)} %bitcast.120), calls=%async_computation.3 | async-start | bytes 8388608
  602.7 21.5 %copy-start.18 = (bf16[768,1536]{1,0:T(8,128)(2,1)S(1)}, bf16[768,1536]{1,0:T(8,128)(2,1)}, u32[]{:S(2)}) copy-start(bf16[768,1536]{1,0:T(8,128)(2,1)} %get-tuple-element.172) | copy-start | bytes 7077892
  602.7 21.5 %copy-start.57 = (bf16[4,2,2,96,768]{4,3,2,1,0:T(8,128)(2,1)S(1)}, bf16[4,2,2,96,768]{4,3,2,1,0:T(8,128)(2,1)}, u32[]{:S(2)}) copy-start(bf16[4,2,2,96,768]{4,3,2,1,0:T(8,128)(2,1)} %get-tuple-element.65) | copy-start | bytes 7077892
  602.7 26.9 %slice-start.1 = ((s8[4718592]{0:T(1024)(128)(4,1)}), s8[524288]{0:T(1024)(128)(4,1)S(1)}, s32[]{:S(2)}) async-start(s8[4718592]{0:T(1024)(128)(4,1)} %bitcast.120), calls=%async_computation.4 | async-start | bytes 1048576
  602.7 21.4 %collective-permute-start.8 = (bf16[768,1536]{1,0:T(8,128)(2,1)}, bf16[768,1536]{1,0:T(8,128)(2,1)S(1)}, u32[]{:S(2)}, u32[]{:S(2)}) collective-permute-start(bf16[768,1536]{1,0:T(8,128)(2,1)} %get-tuple-element.172), channel_id=1, source_target_pairs={{0,2},{2,0},{1,3},{3,1},{4,6},{6,4},{5,7},{7,5},{8,10},{10,8},{9,1... | collective-permute-start | bytes 7077896 | tf_op jit(solution)/shard_map/ppermute | solution.py:25
  637.4 12.5 %collective-permute-start.9 = (bf16[768,1536]{1,0:T(8,128)(2,1)}, bf16[768,1536]{1,0:T(8,128)(2,1)S(1)}, u32[]{:S(2)}, u32[]{:S(2)}) collective-permute-start(bf16[768,1536]{1,0:T(8,128)(2,1)} %convolution_convert_fusion.4), channel_id=1, source_target_pairs={{0,2},{2,0},{1,3},{3,1},{4,6},{6,4},{5,7},{7,5},{8,10},{10,8},{9,1... | collective-permute-start | bytes 7077896 | tf_op jit(solution)/shard_map/ppermute | solution.py:25
  649.4 24.2 %collective-permute-start.11 = (bf16[64,768]{1,0:T(8,128)(2,1)S(1)}, bf16[64,768]{1,0:T(8,128)(2,1)S(1)}, u32[]{:S(2)}, u32[]{:S(2)}) collective-permute-start(bf16[64,768]{1,0:T(8,128)(2,1)S(1)} %broadcast_select_fusion), channel_id=1, source_target_pairs={{0,2},{2,0},{1,3},{3,1},{4,6},{6,4},{5,7},{7,5},{8,10},{10,8},{9,1... | collective-permute-start | bytes 294920 | tf_op jit(solution)/shard_map/ppermute | solution.py:25
  657.9 26.1 %collective-permute-start.10 = (bf16[768,1536]{1,0:T(8,128)(2,1)}, bf16[768,1536]{1,0:T(8,128)(2,1)}, u32[]{:S(2)}, u32[]{:S(2)}) collective-permute-start(bf16[768,1536]{1,0:T(8,128)(2,1)} %get-tuple-element.170), channel_id=1, source_target_pairs={{0,2},{2,0},{1,3},{3,1},{4,6},{6,4},{5,7},{7,5},{8,10},{10,8},{9,1... | collective-permute-start | bytes 7077896 | tf_op jit(solution)/shard_map/ppermute | solution.py:25
  673.7 8.2 collective-permute-start.12
  (66 other events, 423.4 us)
Sparse Core Ops, SparseCore 0:
  351.9 122.4 all-gather.1
  574.1 147.9 reduce-scatter.1

commit v3 on v2

--- a/solution.py
+++ b/solution.py
@@ -27,6 +27,10 @@
 
 def swap_clip(v):
     return lax.ppermute(v, ("c", "y"), [(0, 0), (1, 2), (2, 1), (3, 3)])
+
+
+def swap_others(v):
+    return lax.ppermute(v, ("c", "y"), [(1, 2), (2, 1)])
 
 
 def ring_fit():
@@ -123,14 +127,14 @@
 
 def attend_back_kernel(
     half, real, q_ref, k_ref, v_ref, do_ref, o_ref, lse_ref, dq_ref, dk_ref, dv_ref,
-    dq_sum, dk_sum, dv_sum, inner, hook=None,
+    dq_sum, inner, q_two, do_two, hook=None,
 ):
     core = lax.axis_index("c")
     per_half = half // ROWS
     blocks = 2 * per_half
     first = lax.broadcasted_iota(jnp.int32, (ROWS, LANES), 1) < HEAD_DIM
-    key_at = lax.broadcasted_iota(jnp.int32, (ROWS, ROWS), 0)
-    query_at = lax.broadcasted_iota(jnp.int32, (ROWS, ROWS), 1)
+    key_at = lax.broadcasted_iota(jnp.int32, (ROWS, 2 * ROWS), 0)
+    query_at = lax.broadcasted_iota(jnp.int32, (ROWS, 2 * ROWS), 1) % ROWS
     pick = lax.broadcasted_iota(jnp.int32, (8, LANES), 1) // HEAD_DIM
     pick = (pick == lax.broadcasted_iota(jnp.int32, (8, LANES), 0)).astype(FLOAT)
 
@@ -138,9 +142,18 @@
         start = jnp.where(core == i // per_half, 0, half) + (i % per_half) * ROWS
         return pl.ds(pl.multiple_of(start, ROWS), ROWS)
 
+    def side_by_side(ref, i):
+        return jnp.concatenate([ref[0:1, i * ROWS : (i + 1) * ROWS], ref[1:2, i * ROWS : (i + 1) * ROWS]], 1)
+
     for i in range(blocks):
-        product = do_ref[place(i), :].astype(FLOAT) * o_ref[place(i), :].astype(FLOAT)
+        grads = do_ref[place(i), :].astype(FLOAT)
+        queries = q_ref[place(i), :].astype(FLOAT) * SCALE
+        product = grads * o_ref[place(i), :].astype(FLOAT)
         inner[:, i * ROWS : (i + 1) * ROWS] = dot_nt(pick, product, precision=lax.Precision.HIGHEST)
+        q_two[i, :ROWS] = jnp.where(first, queries, 0.0).astype(BRAIN)
+        q_two[i, ROWS:] = jnp.where(first, 0.0, queries).astype(BRAIN)
+        do_two[i, :ROWS] = jnp.where(first, grads, 0.0).astype(BRAIN)
+        do_two[i, ROWS:] = jnp.where(first, 0.0, grads).astype(BRAIN)
     dq_sum[...] = jnp.zeros_like(dq_sum)
 
     for j in range(blocks):
@@ -148,37 +161,26 @@
             hook(j)
         keys = k_ref[place(j), :]
         values = v_ref[place(j), :]
-        dk_sum[...] = jnp.zeros_like(dk_sum)
-        dv_sum[...] = jnp.zeros_like(dv_sum)
-
-        def query_step(i, carry, j=j, keys=keys, values=values):
-            rows = pl.ds(pl.multiple_of(i * ROWS, ROWS), ROWS)
-            queries = q_ref[place(i), :].astype(FLOAT) * SCALE
-            grads = do_ref[place(i), :].astype(FLOAT)
-            dead = jnp.logical_and(key_at + j * ROWS >= real, key_at + j * ROWS < half)
-            keep = jnp.logical_and(key_at + j * ROWS <= query_at + i * ROWS, jnp.logical_not(dead))
-            dqs = []
-            dk = dk_sum[...]
-            dv = dv_sum[...]
-            for head in range(2):
-                mine = first if head == 0 else jnp.logical_not(first)
-                q_m = jnp.where(mine, queries, 0.0).astype(BRAIN)
-                do_m = jnp.where(mine, grads, 0.0).astype(BRAIN)
-                s = dot_nt(keys, q_m)
-                p = jnp.where(keep, jnp.exp(s - lse_ref[0, head : head + 1, rows]), 0.0)
-                dp = dot_nt(values, do_m)
-                ds = (p * (dp - inner[head : head + 1, rows])).astype(BRAIN)
-                dv = dv + dot_nn(p.astype(BRAIN), do_m)
-                dk = dk + dot_nn(ds, q_m)
-                dqs.append(dot_tn(ds, keys))
-            dk_sum[...] = dk
-            dv_sum[...] = dv
-            dq_sum[rows, :] += jnp.where(first, dqs[0], dqs[1])
-            return carry
-
-        lax.fori_loop(j, blocks, query_step, 0)
-        dk_ref[place(j), :] = dk_sum[...].astype(BRAIN)
-        dv_ref[place(j), :] = dv_sum[...].astype(BRAIN)
+        dk = dv = None
+        for i in range(j, blocks):
+            rows = pl.ds(i * ROWS, ROWS)
+            q_m, do_m = q_two[i], do_two[i]
+            s = dot_nt(keys, q_m) - side_by_side(lse_ref.at[0], i)
+            if i == j:
+                s = jnp.where(key_at <= query_at, s, NEGATIVE)
+            elif j == per_half - 1:
+                s = jnp.where(key_at < real - j * ROWS, s, NEGATIVE)
+            p = jnp.exp(s)
+            dp = dot_nt(values, do_m)
+            ds = (p * (dp - side_by_side(inner, i))).astype(BRAIN)
+            dv_term = dot_nn(p.astype(BRAIN), do_m)
+            dk_term = dot_nn(ds, q_m)
+            dk = dk_term if dk is None else dk + dk_term
+            dv = dv_term if dv is None else dv + dv_term
+            dq = dot_tn(ds, keys)
+            dq_sum[rows, :] += jnp.where(first, dq[:ROWS], dq[ROWS:])
+        dk_ref[place(j), :] = dk.astype(BRAIN)
+        dv_ref[place(j), :] = dv.astype(BRAIN)
 
     for i in range(blocks):
         dq_ref[place(i), :] = (dq_sum[i * ROWS : (i + 1) * ROWS, :] * SCALE).astype(BRAIN)
@@ -195,9 +197,9 @@
         out_specs=[spec] * 3,
         scratch_shapes=[
             pltpu.VMEM((rows, LANES), FLOAT),
-            pltpu.VMEM((ROWS, LANES), FLOAT),
-            pltpu.VMEM((ROWS, LANES), FLOAT),
             pltpu.VMEM((8, rows), FLOAT),
+            pltpu.VMEM((rows // ROWS, 2 * ROWS, LANES), BRAIN),
+            pltpu.VMEM((rows // ROWS, 2 * ROWS, LANES), BRAIN),
         ],
         out_shape=[jax.ShapeDtypeStruct((rows, width), BRAIN)] * 3,
         compiler_params=pltpu.CompilerParams(vmem_limit_bytes=48 * 2**20),
@@ -210,7 +212,7 @@
 
 ORDERS = ("zxy", "zyx", "xyz")
 TICKS = 5
-SUM_TIME = 1.6
+SUM_TIME = 3.3
 
 
 def whereabouts():
@@ -653,10 +655,10 @@
 
 def sum_kernel(slots, count, real, *refs):
     terms, refs = refs[:count], refs[count:]
-    home, block, q, k, v, do, o, h, w_q, w_k, w_v, x0, dx1, lse, gains, vectors = refs[:16]
-    refs = refs[16:]
-    outs, (home_out, frames_out, block_out, vectors_out) = refs[: count + 3], refs[count + 3 : count + 7]
-    refs = refs[count + 7 :]
+    home, q, k, v, do, o, h, w_q, w_k, w_v, x0, dx1, lse, gains, vectors = refs[:15]
+    refs = refs[15:]
+    outs, (home_out, frames_out, vectors_out) = refs[: count + 3], refs[count + 3 : count + 6]
+    refs = refs[count + 6 :]
     lands = len([1 for _, _, sizes in slots for kind, order in enumerate(ORDERS) if sizes[kind] and order != "xyz"])
     landings, refs = refs[:lands], refs[lands:]
     send, recv, local, cross_send, cross_recv, cross_local, v_send, v_recv, h_send, h_recv, loads = refs[:11]
@@ -676,17 +678,15 @@
     early = [n for n, slot in enumerate(slots) if slot[0] < count]
     late = [n for n, slot in enumerate(slots) if slot[0] >= count]
     home_start, home_finish = crossing.prepare(home, home_out)
-    block_start, block_finish = crossing.prepare(block, block_out)
     frames_start, frames_finish = crossing.prepare(far, frames_out)
     greet(c, y, up, down, x, True)
     for n in early:
         run_events(chains[n][0])
-    block_start()
     home_start()
 
     work = tiles * (tiles + 1) // 2
     times = [p + sum(tiles - i for i in range(j)) / work for p in range(pairs) for j in range(tiles)]
-    times += [pairs + 0.5 * i for i in range(1, 5)]
+    times += [pairs + 0.9 * i for i in range(1, 5)]
     spots = {}
     for number, tick, part in sum_order(len(early)):
         due = part * SUM_TIME * pairs
@@ -697,7 +697,7 @@
         for number, tick in spots.get(spot, []):
             run_events(chains[number][tick])
 
-    def attention(pair_in, dq_sum, dk_sum, dv_sum, inner):
+    def attention(pair_in, *held):
         def load(p, i):
             lanes = pl.ds(pl.multiple_of(p * LANES, LANES), LANES)
             slot = lax.rem(p, 2)
@@ -727,7 +727,7 @@
             slot = lax.rem(p, 2)
             attend_back_kernel(
                 half, real, *(pair_in.at[slot, i] for i in range(5)), lse.at[pl.ds(p, 1)],
-                *(grads.at[i, every, lanes] for i in range(3)), dq_sum, dk_sum, dv_sum, inner, hook=hook,
+                *(grads.at[i, every, lanes] for i in range(3)), *held, hook=hook,
             )
             return carry
 
@@ -735,8 +735,8 @@
 
     pl.run_scoped(
         attention,
-        pltpu.VMEM((2, 5, rows, LANES), BRAIN), pltpu.VMEM((rows, LANES), FLOAT),
-        pltpu.VMEM((ROWS, LANES), FLOAT), pltpu.VMEM((ROWS, LANES), FLOAT), pltpu.VMEM((8, rows), FLOAT),
+        pltpu.VMEM((2, 5, rows, LANES), BRAIN), pltpu.VMEM((rows, LANES), FLOAT), pltpu.VMEM((8, rows), FLOAT),
+        pltpu.VMEM((tiles, 2 * ROWS, LANES), BRAIN), pltpu.VMEM((tiles, 2 * ROWS, LANES), BRAIN),
     )
 
     def exchange(part):
@@ -853,25 +853,22 @@
     z_down.start()
     z_up.wait()
     z_more.start()
-    for number, tick in spots.get(len(times), []):
+    rest = spots.get(len(times), []) + [(n, tick) for n in late for tick in range(1, TICKS + 1)]
+    for number, tick in sorted(rest, key=lambda event: (event[1], event[0])):
         run_events(chains[number][tick])
-    for tick in range(1, TICKS + 1):
-        for n in late:
-            run_events(chains[n][tick])
     z_down.wait()
     z_more.wait()
     vectors_out[...] = (held[6] + held[7]) + (held[8] + held[9])
     home_finish()
-    block_finish()
     frames_finish()
 
 
-def sum_gradients(terms, home, block, attention, h, weights, x0, dx1, lse, gains, vectors, real, slots):
+def sum_gradients(terms, home, attention, h, weights, x0, dx1, lse, gains, vectors, real, slots):
     count = len(terms)
     rows, share = attention[0].shape
     half, width = x0.shape
     size = terms[0].shape[3]
-    crossings = 3 * len(slots) + 3
+    crossings = 3 * len(slots) + 2
     dma = pltpu.SemaphoreType.DMA
     vmem = pl.BlockSpec(memory_space=pltpu.VMEM)
     landings = sum_landings(slots, size)
@@ -879,11 +876,11 @@
     most = [max(sizes[kind] for _, _, sizes in slots) for kind in range(2)]
     results = pl.pallas_call(
         functools.partial(sum_kernel, slots, count, real),
-        in_specs=[ANY] * (count + 13) + [vmem] * 3,
-        out_specs=[ANY] * (count + 6) + [vmem] + [ANY] * len(landings),
+        in_specs=[ANY] * (count + 12) + [vmem] * 3,
+        out_specs=[ANY] * (count + 5) + [vmem] + [ANY] * len(landings),
         out_shape=[jax.ShapeDtypeStruct((size, n), BRAIN) for n in widths]
         + [jax.ShapeDtypeStruct(home.shape, BRAIN), jax.ShapeDtypeStruct(x0.shape, BRAIN)]
-        + [jax.ShapeDtypeStruct(block.shape, BRAIN), jax.ShapeDtypeStruct(vectors.shape, FLOAT)]
+        + [jax.ShapeDtypeStruct(vectors.shape, FLOAT)]
         + landings,
         scratch_shapes=[
             dma((len(slots), 3, 5)), dma((len(slots), 3, 5)), dma((len(slots), 3, 4)),
@@ -899,17 +896,16 @@
             collective_id=3, has_side_effects=True, vmem_limit_bytes=58 * 2**20
         ),
         name="sum_gradients",
-    )(*terms, home, block, *attention, h, *weights, x0, dx1, lse, gains, vectors)
-    return results[: count + 7]
-
-
-def slots_of(widths, six=((1, 4, 1), (0, 4, 2), (1, 4, 1)), eight=(1, 5, 2), last=None):
+    )(*terms, home, *attention, h, *weights, x0, dx1, lse, gains, vectors)
+    return results[: count + 6]
+
+
+def slots_of(widths, six=((2, 3, 1), (2, 3, 1), (3, 2, 1)), eight=(3, 3, 2)):
     slots = []
     for which, width in enumerate(widths):
         tiles = width // LANES
-        ways = last if last and which >= len(widths) - 3 else six
         if tiles == 6:
-            slots.append((which, 0, tuple(LANES * n for n in ways[len(slots) % len(ways)])))
+            slots.append((which, 0, tuple(LANES * n for n in six[len(slots) % len(six)])))
         elif tiles % 8 == 0:
             for at in range(0, tiles, 8):
                 slots.append((which, at * LANES, tuple(LANES * n for n in eight)))
@@ -1047,11 +1043,9 @@
     dy = (2.0 * tokens_all / token_count) * valid * deviation
 
     dyb = both(dy.astype(BRAIN))
-    cut = hidden - share
-    fo_grad = dot_tn(dyb, g[:, :cut]).astype(BRAIN)
+    fo_grad = dot_tn(dyb, g).astype(BRAIN)
     dyb, fo_grad = lax.optimization_barrier((dyb, fo_grad))
     fo_grad = lax.psum_scatter(fo_grad, CHIPS, scatter_dimension=0, tiled=True)
-    fo_rest = dot_tn(dyb, g[:, cut:]).astype(BRAIN)
     du = (slope.astype(FLOAT) * dot_nn(dyb, w_fo)).astype(BRAIN)
     fi_grad = dot_tn(h3, du).astype(BRAIN)
     term, gain3, bias3 = norm_back(x2, gains[4], summed(du, w_fi))
@@ -1078,13 +1072,11 @@
     zero = jnp.zeros((width,), FLOAT)
     vectors = jnp.stack([zero, zero, gain2, bias2, gain3, bias3])
     vectors = jnp.concatenate([vectors, jnp.full((2, width), error)], 0)
-    grads = [fi_grad, fo_rest, co_grad, cq_grad, ck_grad, cv_grad, so_grad]
+    grads = [fi_grad, co_grad, cq_grad, ck_grad, cv_grad, so_grad]
     if fits:
-        slots = slots_of(
-            [v.shape[1] for v in grads] + [w_q.shape[1]] * 3, six=((1, 4, 1), (1, 3, 2)), eight=(1, 5, 2), last=((0, 4, 2),)
-        )
-        *grads, home, frames, fo_grad, vectors = sum_gradients(
-            [by_chip(v) for v in grads], home, fo_grad, (q1, k1, v1, do1, o1), h1,
+        slots = slots_of([v.shape[1] for v in grads] + [share] * 3, six=((2, 2, 2),))
+        *grads, home, frames, vectors = sum_gradients(
+            [by_chip(v) for v in grads], home, (q1, k1, v1, do1, o1), h1,
             [by_chip(v) for v in (w_q, w_k, w_v)], x_own, dx1, lse1, gains, vectors, real, slots,
         )
     else:
@@ -1095,13 +1087,12 @@
         frames = swap_clip((dx1 + term).astype(BRAIN))
         grads += [dot_tn(h1, d).astype(BRAIN) for d in (dq1, dk1, dv1)]
         grads = [swap_clip(lax.psum_scatter(v, CHIPS, scatter_dimension=0, tiled=True)) for v in grads]
-        home, fo_grad = swap_clip(home), swap_clip(fo_grad)
+        home = swap_clip(home)
         vectors = lax.psum(vectors.at[:2].set(jnp.stack([gain1, bias1])), ("z", "x", "c", "y"))
     layer_out = home[:real][None]
     inputs_grad = frames[None].astype(FLOAT)[:, :real]
-    fo_grad, *grads = (v.astype(FLOAT) for v in (fo_grad, *grads))
-    fi_grad, fo_rest, co_grad, cq_grad, ck_grad, cv_grad, so_grad, q_grad, k_grad, v_grad = grads
-    fo_grad = jnp.concatenate([fo_grad.T, fo_rest.T], 0)
+    fi_grad, co_grad, cq_grad, ck_grad, cv_grad, so_grad, q_grad, k_grad, v_grad = (v.astype(FLOAT) for v in grads)
+    fo_grad = jnp.where(at_core == at_y, fo_grad, swap_others(fo_grad)).astype(FLOAT).T
     loss = vectors[6, 0] / (width * token_count)
     mine = block // 2
     place = (lax.axis_index(("z", "x", "c")) * 2 + at_y) * mine

time: 1120 us -> 1060 us (0.946)
  Pallas kernels: 678 us -> 626 us
  matrix products: 236 us -> 218 us
    pallas_call x1, Pallas kernels: 321 us -> 294 us  [gather(): pl.pallas_call(functools.partial(gather_kernel, slots, count, real), out_...]
    pallas_call x1, Pallas kernels: 357 us -> 331 us  [sum_gradients(): pl.pallas_call(functools.partial(sum_kernel, slots, count, real), in_spec...]
    reduce_scatter x1, waiting for transfers between devices: 21.8 us -> 0.01 us  [on_device(): fo_grad = lax.psum_scatter(fo_grad, CHIPS, scatter_dimension=0, tiled=True)]
    dot_general x12, matrix products: 91.8 us -> 78.1 us  [dot_nt(): lax.dot_general(a, b, (((1,), (1,)), ((), ())), preferred_element_type=FL...]
    dot_general x8 -> x7, matrix products: 70.3 us -> 65.4 us  [dot_tn(): lax.dot_general(a, b, (((0,), (0,)), ((), ())), preferred_element_type=FL...]
  transfers between devices with their start and end apart: 15 -> 16, of which waited for: 9 -> 10; matrix products, arithmetic and copies ran while one was open for 15% -> 15% of each run, Pallas kernels for 0% -> 32%
where the time goes in v3:
time: 1060 us; the launch traced here: 1050 us
  Pallas kernels  626 us (59%)
  matrix products  218 us (21%)
  waiting for transfers between devices  86.3 us (8%)
  other arithmetic  43 us (4%)
  local copies, waits for them, and re-layouts  32.6 us (3%)
  between operations  21.5 us (2%)
  starting transfers between devices  18.1 us (2%)
    pallas_call x1, Pallas kernels, sum_gradients(): pl.pallas_call(functools.partial(sum_kernel, slots, count, real), in_spec...  331 us
    pallas_call x1, Pallas kernels, gather(): pl.pallas_call(functools.partial(gather_kernel, slots, count, real), out_...  294 us
    dot_general x12, matrix products, dot_nt(): lax.dot_general(a, b, (((1,), (1,)), ((), ())), preferred_element_type=FL...  78.1 us
    dot_general x7, matrix products, dot_nn(): lax.dot_general(a, b, (((1,), (0,)), ((), ())), preferred_element_type=FL...  69.5 us
    dot_general x7, matrix products, dot_tn(): lax.dot_general(a, b, (((0,), (0,)), ((), ())), preferred_element_type=FL...  65.4 us
    all_gather x1, waiting for transfers between devices, on_device(): w_fo = lax.all_gather(feed_rows, CHIPS, axis=0, tiled=True)  49.8 us
    ppermute x12, waiting for transfers between devices, swap_core(): return lax.ppermute(v, 'c', [(0, 1), (1, 0)])  27.2 us
  transfers between devices with their start and end apart: 16, of which 10 were waited for; matrix products, arithmetic and copies ran while one was open for 15% of the time, Pallas kernels for 32%

profile of v3, /device:TPU:1, one launch (start us, length us, event | category | flops | bytes accessed | tf_op | source)
XLA Modules:
  0.0 1045.4 jit_solution(9657873628446741167)
XLA Ops:
  18.3 294.2 %gather.1 = (bf16[4,2,2,96,128]{4,3,2,1,0:T(8,128)(2,1)}, bf16[4,2,2,96,768]{4,3,2,1,0:T(8,128)(2,1)}, bf16[4,2,2,96,768]{4,3,2,1,0:T(8,128)(2,1)}, bf16[4,2,2,9...) custom-call(bf16[96,128]{1,0:T(8,128)(2,1)} %pad.16.refs_0_, ...), custom_call_target="tpu_custom_call" | custom-call | tf_op jit(solution)/shard_map/gather/pallas_call | solution.py:470
  312.5 5.6 convolution_convert_fusion.13
  318.1 5.7 collective-permute-start
  328.3 5.5 fusion.58
  342.0 7.0 convolution_convert_fusion.12
  371.8 21.1 %multiply_convert_fusion.1 = (bf16[1536,3072]{1,0:T(8,128)(2,1)}, f32[1536,3072]{1,0:T(8,128)}) fusion(bf16[1536,3072]{1,0:T(8,128)(2,1)S(1)} %bitcast.177, bf16[768,1536]{1,0:T(8,128)(2,1)S(1)} %collective-permute-done.3, bf16[768,1536]{1,0:T(8,128)(2,1)S(1)} %add_convert_fusion), kind=kOutput, calls=%fused_computation.7 | convolution fusion | flops 14528544768 | bytes 42467328 | tf_op jit(solution)/shard_map/dot_general | solution.py:53
  393.0 49.8 %all-gather.2.cloned.1.call-done = bf16[1536,3072]{1,0:T(8,128)(2,1)} async-done(((bf16[96,3072]{1,0:T(8,128)(2,1)}), bf16[1536,3072]{1,0:T(8,128)(2,1)}) %all-gather.2.cloned.1.call-update) | async-done | bytes 9437200 | tf_op jit(solution)/shard_map/all_gather | solution.py:1025
  442.8 12.7 %fusion.17 = bf16[768,1536]{1,0:T(8,128)(2,1)} fusion(bf16[1536,3072]{1,0:T(8,128)(2,1)} %all-gather.2.cloned.1.call-done, bf16[1536,3072]{1,0:T(8,128)(2,1)} %get-tuple-element.191), kind=kOutput, calls=%fused_computation.70 | convolution fusion | flops 7248936960 | bytes 16515072 | tf_op jit(solution)/shard_map/dot_general | solution.py:49
  461.8 14.5 %fusion.6 = (f32[]{:T(128)}, f32[768,1536]{1,0:T(8,128)S(1)}) fusion(f32[768]{0:T(1024)S(1)} %get-tuple-element.158, bf16[768,1664]{1,0:T(8,128)(2,1)S(1)} %copy-done.4, f32[768,1536]{1,0:T(8,128)} %copy-done.2, bf16[768,1536]{1,0:T(8,128)(2,1)} %collective-permute-done.5, bf16[1536,3072]{1,0:T(8,128)(2,1)} %all-gather.2.cloned.1.call-done, ...), kind=kOutput, calls=%fused_computation.14 | convolution fusion | flops 7257194496 | bytes 28314628 | tf_op jit(solution)/shard_map/dot_general | solution.py:49
  484.7 17.8 %convolution_convert_fusion.1 = bf16[1536,3072]{1,0:T(8,128)(2,1)} fusion(bf16[1536,3072]{1,0:T(8,128)(2,1)S(1)} %copy-done.53, bf16[768,1536]{1,0:T(8,128)(2,1)S(1)} %collective-permute-done.6, bf16[768,1536]{1,0:T(8,128)(2,1)S(1)} %multiply_convert_fusion.4), kind=kOutput, calls=%fused_computation.10 | convolution fusion | flops 14509670400 | bytes 23592960 | tf_op jit(solution)/shard_map/dot_general | solution.py:57
  505.4 25.7 %multiply_convert_fusion = bf16[1536,3072]{1,0:T(8,128)(2,1)} fusion(f32[1536,3072]{1,0:T(8,128)} %get-tuple-element.192, bf16[1536,1536]{1,0:T(8,128)(2,1)S(1)} %pad_maximum_fusion.2, bf16[1536,3072]{1,0:T(8,128)(2,1)} %all-gather.2.cloned.1.call-done), kind=kOutput, calls=%fused_computation.6 | convolution fusion | flops 14552137728 | bytes 42467328 | tf_op jit(solution)/shard_map/dot_general | solution.py:53
  531.1 11.5 %fusion.20 = bf16[768,1536]{1,0:T(8,128)(2,1)S(1)} fusion(bf16[1536,3072]{1,0:T(8,128)(2,1)} %bitcast.173, bf16[1536,3072]{1,0:T(8,128)(2,1)} %multiply_convert_fusion), kind=kOutput, calls=%fused_computation.71 | convolution fusion | flops 7248936960 | bytes 16515072 | tf_op jit(solution)/shard_map/dot_general | solution.py:49
  543.1 4.3 collective-permute-done.7
  547.4 14.7 %multiply_reduce_fusion = (f32[1536]{0:T(1024)S(1)}, f32[768]{0:T(1024)S(1)}, f32[768]{0:T(1024)S(1)}, f32[1536]{0:T(1024)S(1)}, f32[768,1536]{1,0:T(8,128)}) fusion(f32[768,1536]{1,0:T(8,128)S(1)} %bitcast.126, f32[768]{0:T(1024)S(1)} %copy-done.48, f32[768]{0:T(1024)S(1)} %copy-done.44, bf16[768,1536]{1,0:T(8,128)(2,1)} %collective-permute-done.7, ...), kind=kOutput, calls=%fused_computation.28 | convolution fusion | flops 7260728832 | bytes 25982976 | tf_op jit(solution)/shard_map/dot_general | solution.py:49
  562.1 7.1 fusion.53
  574.2 6.6 convolution_convert_fusion.8
  589.0 20.6 %convolution_convert_fusion = bf16[1536,3072]{1,0:T(8,128)(2,1)} fusion(bf16[1536,3072]{1,0:T(8,128)(2,1)} %multiply_convert_fusion, bf16[768,1536]{1,0:T(8,128)(2,1)} %copy-done.52, bf16[768,1536]{1,0:T(8,128)(2,1)S(1)} %copy-done.17), kind=kOutput, calls=%fused_computation.9 | convolution fusion | flops 14509670400 | bytes 23592960 | tf_op jit(solution)/shard_map/dot_general | solution.py:57
  622.7 7.7 convolution_convert_fusion.9
  630.4 7.7 convolution_convert_fusion.7
  649.3 7.9 convolution_convert_fusion.2.refs_10_
  657.2 7.1 convolution_convert_fusion.3
  664.4 331.4 %sum_gradients.1 = (bf16[96,3072]{1,0:T(8,128)(2,1)}, bf16[96,768]{1,0:T(8,128)(2,1)}, bf16[96,768]{1,0:T(8,128)(2,1)}, bf16[96,768]{1,0:T(8,128)(2,1)}, bf16[96...) custom-call(bf16[4,2,2,96,3072]{4,3,2,1,0:T(8,128)(2,1)} %bitcast.13, ...), custom_call_target="tpu_custom_call" | custom-call | tf_op jit(solution)/shard_map/sum_gradients/pallas_call | solution.py:877
  1011.8 9.3 copy.69
  1028.2 7.9 collective-permute-done.13
  (252 shorter events, 120.3 us)
Async XLA Ops:
  7.2 435.6 %all-gather.2.cloned.1.call-start = ((), (), s32[]{:S(2)}) async-start(), calls=%async_computation.1 | async-start | bytes 10027008 | tf_op jit(solution)/shard_map/all_gather | solution.py:1025
  318.1 10.2 collective-permute-start
  323.9 700.8 %reduce-scatter.2.cloned.1.call-start = ((), (), s32[]{:S(2)}) async-start(), calls=%async_computation.2 | async-start | bytes 10027008 | tf_op jit(solution)/shard_map/reduce_scatter | solution.py:1048
  324.5 40.0 %copy-start.39 = (f32[1536]{0:T(1024)}, f32[1536]{0:T(1024)S(1)}, u32[]{:S(2)}) copy-start(f32[1536]{0:T(1024)S(1)} %get-tuple-element.160) | copy-start | bytes 18436
  337.1 4.9 collective-permute-start.1
  356.8 4.6 collective-permute-start.2
  365.9 4.5 collective-permute-start.3
  442.8 18.8 %copy-start.4 = (bf16[768,1664]{1,0:T(8,128)(2,1)S(1)}, bf16[768,1664]{1,0:T(8,128)(2,1)}, u32[]{:S(2)}) copy-start(bf16[768,1664]{1,0:T(8,128)(2,1)} %get-tuple-element.66) | copy-start | bytes 7667716
  455.5 6.4 collective-permute-start.5
  458.8 2.1 collective-permute-start.4
  478.8 4.5 collective-permute-start.6
  502.5 44.9 %slice-start.6 = ((s8[4718592]{0:T(1024)(128)(4,1)}), s8[4194304]{0:T(1024)(128)(4,1)S(1)}, s32[]{:S(2)}) async-start(s8[4718592]{0:T(1024)(128)(4,1)} %bitcast.125), calls=%async_computation.9 | async-start | bytes 8388608
  502.5 59.6 %slice-start.8 = ((s8[4718592]{0:T(1024)(128)(4,1)}), s8[4194304]{0:T(1024)(128)(4,1)S(1)}, s32[]{:S(2)}) async-start(s8[4718592]{0:T(1024)(128)(4,1)} %bitcast.127), calls=%async_computation.11 | async-start | bytes 8388608
  505.4 42.0 %slice-start.7 = ((s8[4718592]{0:T(1024)(128)(4,1)}), s8[524288]{0:T(1024)(128)(4,1)S(1)}, s32[]{:S(2)}) async-start(s8[4718592]{0:T(1024)(128)(4,1)} %bitcast.125), calls=%async_computation.10 | async-start | bytes 1048576
  505.4 56.7 %slice-start.9 = ((s8[4718592]{0:T(1024)(128)(4,1)}), s8[524288]{0:T(1024)(128)(4,1)S(1)}, s32[]{:S(2)}) async-start(s8[4718592]{0:T(1024)(128)(4,1)} %bitcast.127), calls=%async_computation.12 | async-start | bytes 1048576
  531.1 16.3 %copy-start.48 = (f32[768]{0:T(1024)S(1)}, f32[768]{0:T(1024)}, u32[]{:S(2)}) copy-start(f32[768]{0:T(1024)} %copy-done.47) | copy-start | bytes 9220
  542.7 4.7 collective-permute-start.7
  569.3 4.9 collective-permute-start.8
  588.7 20.9 %copy-start.13 = (bf16[1536,768]{0,1:T(8,128)(2,1)S(1)}, bf16[1536,768]{0,1:T(8,128)(2,1)}, u32[]{:S(2)}) copy-start(bf16[1536,768]{0,1:T(8,128)(2,1)} %copy-done.12) | copy-start | bytes 7077892
  588.7 25.6 %collective-permute-start.9 = (bf16[768,1536]{1,0:T(8,128)(2,1)}, bf16[768,1536]{1,0:T(8,128)(2,1)S(1)}, u32[]{:S(2)}, u32[]{:S(2)}) collective-permute-start(bf16[768,1536]{1,0:T(8,128)(2,1)} %convolution_convert_fusion.4), channel_id=1, source_target_pairs={{0,2},{2,0},{1,3},{3,1},{4,6},{6,4},{5,7},{7,5},{8,10},{10,8},{9,1... | collective-permute-start | bytes 7077896 | tf_op jit(solution)/shard_map/ppermute | solution.py:25
  614.2 26.2 %collective-permute-start.11 = (bf16[64,768]{1,0:T(8,128)(2,1)S(1)}, bf16[64,768]{1,0:T(8,128)(2,1)S(1)}, u32[]{:S(2)}, u32[]{:S(2)}) collective-permute-start(bf16[64,768]{1,0:T(8,128)(2,1)S(1)} %broadcast_select_fusion), channel_id=1, source_target_pairs={{0,2},{2,0},{1,3},{3,1},{4,6},{6,4},{5,7},{7,5},{8,10},{10,8},{9,1... | collective-permute-start | bytes 294920 | tf_op jit(solution)/shard_map/ppermute | solution.py:25
  622.2 27.1 %collective-permute-start.10 = (bf16[768,1536]{1,0:T(8,128)(2,1)S(1)}, bf16[768,1536]{1,0:T(8,128)(2,1)}, u32[]{:S(2)}, u32[]{:S(2)}) collective-permute-start(bf16[768,1536]{1,0:T(8,128)(2,1)S(1)} %get-tuple-element.166), channel_id=1, source_target_pairs={{0,2},{2,0},{1,3},{3,1},{4,6},{6,4},{5,7},{7,5},{8,10},{10,8},{9,1... | collective-permute-start | bytes 7077896 | tf_op jit(solution)/shard_map/ppermute | solution.py:25
  640.4 6.8 collective-permute-start.12
  1024.6 11.5 %collective-permute-start.13 = (bf16[96,3072]{1,0:T(8,128)(2,1)}, bf16[96,3072]{1,0:T(8,128)(2,1)S(1)}, u32[]{:S(2)}, u32[]{:S(2)}) collective-permute-start(bf16[96,3072]{1,0:T(8,128)(2,1)} %reduce-scatter.2.cloned.1.call-done), channel_id=1, source_target_pairs={{1,2},{2,1},{5,6},{6,5},{9,10},{10,9},{13,14},{14,13},{17,18},{18,... | collective-permute-start | bytes 1769480 | tf_op jit(solution)/shard_map/ppermute | solution.py:33
  (61 other events, 372.7 us)
Sparse Core Ops, SparseCore 0:
  324.0 118.7 all-gather.1
  569.8 209.5 reduce-scatter.1

commit v4 on v3

--- a/solution.py
+++ b/solution.py
@@ -31,6 +31,10 @@
 
 def swap_others(v):
     return lax.ppermute(v, ("c", "y"), [(1, 2), (2, 1)])
+
+
+def swap_weight(v):
+    return jnp.where(lax.axis_index("c") == lax.axis_index("y"), v, swap_others(v))
 
 
 def ring_fit():
@@ -212,7 +216,7 @@
 
 ORDERS = ("zxy", "zyx", "xyz")
 TICKS = 5
-SUM_TIME = 3.3
+SUM_TIME = 2.2
 
 
 def whereabouts():
@@ -359,11 +363,11 @@
 
 
 def gather_kernel(slots, count, real, *refs):
-    blocks, (frames, text, target, block) = refs[:count], refs[count : count + 4]
-    refs = refs[count + 4 :]
-    weights, (own_out, text_out, target_out, block_out) = refs[:count], refs[count : count + 4]
-    gains_ref, h_ref, q_ref, k_ref, v_ref, o_ref, lse_ref = refs[count + 4 : count + 11]
-    send, recv, cross_send, cross_recv, cross_local, core_send, core_recv, loads, tiny, both, held = refs[count + 11 :]
+    blocks, (frames, text, target) = refs[:count], refs[count : count + 3]
+    refs = refs[count + 3 :]
+    weights, (own_out, text_out, target_out) = refs[:count], refs[count : count + 3]
+    gains_ref, h_ref, q_ref, k_ref, v_ref, o_ref, lse_ref = refs[count + 3 : count + 10]
+    send, recv, cross_send, cross_recv, cross_local, core_send, core_recv, loads, tiny, both, held = refs[count + 10 :]
     rows, width = h_ref.shape
     half = rows // 2
     pairs = q_ref.shape[1] // LANES
@@ -373,7 +377,7 @@
     chains = gather_events(where, slots, weights, send, recv)
     starts = list(bring_own(crossing, where, slots, chains, blocks, weights))
     frames_start, frames_finish = crossing.prepare(frames, both.at[0])
-    moves = [crossing.prepare(*pair) for pair in ((text, text_out), (block, block_out), (target, target_out))]
+    moves = [crossing.prepare(*pair) for pair in ((text, text_out), (target, target_out))]
     sibling = pltpu.make_async_remote_copy(
         src_ref=both.at[0], dst_ref=both.at[1], send_sem=core_send, recv_sem=core_recv,
         device_id={"c": 1 - c}, device_id_type=MESH,
@@ -457,12 +461,12 @@
         finish()
 
 
-def gather(blocks, frames, text, target, block, real, slots):
+def gather(blocks, frames, text, target, real, slots):
     count = len(blocks)
     rows, width = 2 * frames.shape[0], frames.shape[1]
     share = blocks[1].shape[1]
     pairs = share // LANES
-    crossings = count + 4
+    crossings = count + 3
     dma = pltpu.SemaphoreType.DMA
     vmem = pl.BlockSpec(memory_space=pltpu.VMEM)
     heads = jax.ShapeDtypeStruct((rows, share), BRAIN)
@@ -471,12 +475,12 @@
         functools.partial(gather_kernel, slots, count, real),
         out_shape=[
             *gathered,
-            *[jax.ShapeDtypeStruct(v.shape, v.dtype) for v in (frames, text, target, block)],
+            *[jax.ShapeDtypeStruct(v.shape, v.dtype) for v in (frames, text, target)],
             jax.ShapeDtypeStruct((8, width), FLOAT), jax.ShapeDtypeStruct((rows, width), BRAIN),
             heads, heads, heads, heads, jax.ShapeDtypeStruct((pairs, 8, rows), FLOAT),
         ],
-        in_specs=[ANY] * (count + 4),
-        out_specs=[ANY] * (count + 4) + [vmem] * 7,
+        in_specs=[ANY] * (count + 3),
+        out_specs=[ANY] * (count + 3) + [vmem] * 7,
         scratch_shapes=[
             dma((len(slots), 3, 5)), dma((len(slots), 3, 5)),
             dma((crossings,)), dma((crossings,)), dma((crossings,)), dma, dma, dma((5,)),
@@ -487,7 +491,7 @@
             collective_id=1, has_side_effects=True, vmem_limit_bytes=56 * 2**20
         ),
         name="gather",
-    )(*blocks, frames, text, target, block)
+    )(*blocks, frames, text, target)
 
 
 def plus(*terms):
@@ -986,9 +990,9 @@
     digits = jnp.where((jnp.arange(block) == 0)[:, None], digits[None, :], jnp.zeros((), BRAIN))
     tiny = jnp.pad(jnp.concatenate([jnp.stack(tiny, 1), digits], 1), ((0, 0), (0, LANES - 8)))
     weights = [
-        tiny, self_query, self_key, self_value, self_out.T, cross_query, cross_key, cross_value, cross_out.T, feed_in
+        tiny, self_query, self_key, self_value, self_out.T, cross_query, cross_key, cross_value, cross_out.T
     ]
-    feed_rows = feed_out.T
+    wide = [swap_weight(v) for v in (feed_in, feed_out.T)]
 
     def both(own):
         return jnp.concatenate([own, swap_core(own)], 0)
@@ -1006,23 +1010,24 @@
     target = padded(jnp.concatenate([teacher[0], flags], 1))
     if fits:
         slots = slots_of([v.shape[1] for v in weights])
-        *weights, x_own, text, target, feed_rows, gains, h1, q1, k1, v1, o1, lse1 = gather(
-            weights, frames, text_states[0], target, feed_rows, real, slots
+        frames, *wide = lax.optimization_barrier((frames, *wide))
+        *weights, x_own, text, target, gains, h1, q1, k1, v1, o1, lse1 = gather(
+            weights, frames, text_states[0], target, real, slots
         )
         weights = [joined(v) for v in weights]
     else:
         weights = [lax.all_gather(swap_clip(v), CHIPS, axis=0, tiled=True) for v in weights]
-        x_own, text, target, feed_rows = (swap_clip(v) for v in (frames, text_states[0], target, feed_rows))
+        x_own, text, target = (swap_clip(v) for v in (frames, text_states[0], target))
         gains = weights[0].T.astype(FLOAT)
         x_all = jnp.concatenate([x_own, swap_core(x_own)], 0)
         h1 = normalize(x_all.astype(FLOAT), gains[0], gains[1]).astype(BRAIN)
         q1, k1, v1 = (dot_nn(h1, w).astype(BRAIN) for w in weights[1:4])
         o1, lse1 = attend_self(q1, k1, v1, real)
-    tiny, w_q, w_k, w_v, w_so, w_cq, w_ck, w_cv, w_co, w_fi = weights
+    tiny, w_q, w_k, w_v, w_so, w_cq, w_ck, w_cv, w_co = weights
+    w_fi, w_fo = (lax.all_gather(v, CHIPS, axis=0, tiled=True) for v in wide)
     counted = jnp.sum(tiny[:, 6:8].astype(FLOAT), 0)
     counted = counted[0] * 64.0 + counted[1]
     token_count = counted + swap_core(counted)
-    w_fo = lax.all_gather(feed_rows, CHIPS, axis=0, tiled=True)
     valid = target[:, width : width + 1].astype(FLOAT)
     target = target[:, :width].astype(FLOAT)
     x0 = x_own.astype(FLOAT)
@@ -1048,6 +1053,7 @@
     fo_grad = lax.psum_scatter(fo_grad, CHIPS, scatter_dimension=0, tiled=True)
     du = (slope.astype(FLOAT) * dot_nn(dyb, w_fo)).astype(BRAIN)
     fi_grad = dot_tn(h3, du).astype(BRAIN)
+    fi_grad = lax.psum_scatter(fi_grad, CHIPS, scatter_dimension=0, tiled=True)
     term, gain3, bias3 = norm_back(x2, gains[4], summed(du, w_fi))
     dx2 = dy + term
     dx2b = both(dx2.astype(BRAIN))
@@ -1072,7 +1078,7 @@
     zero = jnp.zeros((width,), FLOAT)
     vectors = jnp.stack([zero, zero, gain2, bias2, gain3, bias3])
     vectors = jnp.concatenate([vectors, jnp.full((2, width), error)], 0)
-    grads = [fi_grad, co_grad, cq_grad, ck_grad, cv_grad, so_grad]
+    grads = [co_grad, cq_grad, ck_grad, cv_grad, so_grad]
     if fits:
         slots = slots_of([v.shape[1] for v in grads] + [share] * 3, six=((2, 2, 2),))
         *grads, home, frames, vectors = sum_gradients(
@@ -1091,8 +1097,8 @@
         vectors = lax.psum(vectors.at[:2].set(jnp.stack([gain1, bias1])), ("z", "x", "c", "y"))
     layer_out = home[:real][None]
     inputs_grad = frames[None].astype(FLOAT)[:, :real]
-    fi_grad, co_grad, cq_grad, ck_grad, cv_grad, so_grad, q_grad, k_grad, v_grad = (v.astype(FLOAT) for v in grads)
-    fo_grad = jnp.where(at_core == at_y, fo_grad, swap_others(fo_grad)).astype(FLOAT).T
+    co_grad, cq_grad, ck_grad, cv_grad, so_grad, q_grad, k_grad, v_grad = (v.astype(FLOAT) for v in grads)
+    fi_grad, fo_grad = swap_weight(fi_grad).astype(FLOAT), swap_weight(fo_grad).astype(FLOAT).T
     loss = vectors[6, 0] / (width * token_count)
     mine = block // 2
     place = (lax.axis_index(("z", "x", "c")) * 2 + at_y) * mine

time: 1060 us -> 1010 us (0.953)
  Pallas kernels: 626 us -> 553 us
  matrix products: 218 us -> 238 us
  starting transfers between devices: 18.1 us -> 30.3 us
    pallas_call x1, Pallas kernels: 331 us -> 275 us  [sum_gradients(): pl.pallas_call(functools.partial(sum_kernel, slots, count, real), in_spec...]
    dot_general x12, matrix products: 78.1 us -> 94.5 us  [dot_nt(): lax.dot_general(a, b, (((1,), (1,)), ((), ())), preferred_element_type=FL...]
    pallas_call x1, Pallas kernels: 294 us -> 278 us  [gather(): pl.pallas_call(functools.partial(gather_kernel, slots, count, real), out_...]
    all_gather x1 -> x2, waiting for transfers between devices: 49.8 us -> 37.5 us  [on_device(): w_fi, w_fo = (lax.all_gather(v, CHIPS, axis=0, tiled=True) for v in wide)]
  transfers between devices with their start and end apart: 16 -> 21, of which waited for: 10 -> 11; matrix products, arithmetic and copies ran while one was open for 15% -> 26% of each run, Pallas kernels for 32% -> 55%
where the time goes in v4:
time: 1010 us; the launch traced here: 1000 us
  Pallas kernels  553 us (55%)
  matrix products  238 us (24%)
  waiting for transfers between devices  77.5 us (8%)
  other arithmetic  49.8 us (5%)
  local copies, waits for them, and re-layouts  32.9 us (3%)
  starting transfers between devices  30.3 us (3%)
  between operations  21.7 us (2%)
    pallas_call x1, Pallas kernels, gather(): pl.pallas_call(functools.partial(gather_kernel, slots, count, real), out_...  278 us
    pallas_call x1, Pallas kernels, sum_gradients(): pl.pallas_call(functools.partial(sum_kernel, slots, count, real), in_spec...  275 us
    dot_general x12, matrix products, dot_nt(): lax.dot_general(a, b, (((1,), (1,)), ((), ())), preferred_element_type=FL...  94.5 us
    dot_general x7, matrix products, dot_nn(): lax.dot_general(a, b, (((1,), (0,)), ((), ())), preferred_element_type=FL...  70.6 us
    dot_general x7, matrix products, dot_tn(): lax.dot_general(a, b, (((0,), (0,)), ((), ())), preferred_element_type=FL...  61.6 us
    all_gather x2, waiting for transfers between devices, on_device(): w_fi, w_fo = (lax.all_gather(v, CHIPS, axis=0, tiled=True) for v in wide)  37.5 us
    ppermute x12, waiting for transfers between devices, swap_core(): return lax.ppermute(v, 'c', [(0, 1), (1, 0)])  23.3 us
  transfers between devices with their start and end apart: 21, of which 11 were waited for; matrix products, arithmetic and copies ran while one was open for 26% of the time, Pallas kernels for 55%

profile of v4, /device:TPU:1, one launch (start us, length us, event | category | flops | bytes accessed | tf_op | source)
XLA Modules:
  0.0 1003.3 jit_solution(2030020089002911665)
XLA Ops:
  34.6 278.2 %gather.1 = (bf16[4,2,2,96,128]{4,3,2,1,0:T(8,128)(2,1)}, bf16[4,2,2,96,768]{4,3,2,1,0:T(8,128)(2,1)}, bf16[4,2,2,96,768]{4,3,2,1,0:T(8,128)(2,1)}, bf16[4,2,2,9...) custom-call(bf16[96,128]{1,0:T(8,128)(2,1)} %pad.16.refs_0_, ...), custom_call_target="tpu_custom_call" | custom-call | tf_op jit(solution)/shard_map/gather/pallas_call | solution.py:474
  312.8 5.6 convolution_convert_fusion.13
  318.4 7.2 collective-permute-start.3
  330.1 5.4 fusion.58
  343.7 7.0 convolution_convert_fusion.12
  356.3 13.5 %convolution_convert_fusion.10 = bf16[768,1536]{1,0:T(8,128)(2,1)S(1)} fusion(bf16[768,768]{0,1:T(8,128)(2,1)S(1)} %bitcast.154, bf16[1536,768]{1,0:T(8,128)(2,1)S(1)} %bitcast.175), kind=kOutput, calls=%fused_computation.66 | convolution fusion | flops 1813118976 | bytes 5898240 | tf_op jit(solution)/shard_map/dot_general | solution.py:53
  383.6 24.1 %multiply_convert_fusion.1 = (bf16[1536,3072]{1,0:T(8,128)(2,1)}, f32[1536,3072]{1,0:T(8,128)}) fusion(bf16[1536,3072]{1,0:T(8,128)(2,1)} %all-gather.3.cloned.1.call-done, bf16[768,1536]{1,0:T(8,128)(2,1)} %collective-permute-done.6, bf16[768,1536]{1,0:T(8,128)(2,1)S(1)} %add_convert_fusion), kind=kOutput, calls=%fused_computation.7 | convolution fusion | flops 14528544768 | bytes 42467328 | tf_op jit(solution)/shard_map/dot_general | solution.py:57
  407.7 37.5 %all-gather.5.cloned.1.call-done = bf16[1536,3072]{1,0:T(8,128)(2,1)} async-done(((bf16[96,3072]{1,0:T(8,128)(2,1)}), bf16[1536,3072]{1,0:T(8,128)(2,1)}) %all-gather.5.cloned.1.call-update) | async-done | bytes 9437200 | tf_op jit(solution)/shard_map/all_gather | solution.py:1027
  445.2 12.7 %fusion.17 = bf16[768,1536]{1,0:T(8,128)(2,1)} fusion(bf16[1536,3072]{1,0:T(8,128)(2,1)} %all-gather.5.cloned.1.call-done, bf16[1536,3072]{1,0:T(8,128)(2,1)} %get-tuple-element.191), kind=kOutput, calls=%fused_computation.70 | convolution fusion | flops 7248936960 | bytes 16515072 | tf_op jit(solution)/shard_map/dot_general | solution.py:53
  464.2 14.5 %fusion.6 = (f32[]{:T(128)}, f32[768,1536]{1,0:T(8,128)S(1)}) fusion(f32[768]{0:T(1024)S(1)} %get-tuple-element.158, bf16[768,1664]{1,0:T(8,128)(2,1)S(1)} %copy-done.4, f32[768,1536]{1,0:T(8,128)} %copy-done.2, bf16[768,1536]{1,0:T(8,128)(2,1)} %collective-permute-done.7, bf16[1536,3072]{1,0:T(8,128)(2,1)} %all-gather.5.cloned.1.call-done, ...), kind=kOutput, calls=%fused_computation.14 | convolution fusion | flops 7257194496 | bytes 28314628 | tf_op jit(solution)/shard_map/dot_general | solution.py:53
  487.1 17.8 %convolution_convert_fusion.1 = bf16[1536,3072]{1,0:T(8,128)(2,1)} fusion(bf16[1536,3072]{1,0:T(8,128)(2,1)S(1)} %copy-done.70, bf16[768,1536]{1,0:T(8,128)(2,1)S(1)} %collective-permute-done.8, bf16[768,1536]{1,0:T(8,128)(2,1)S(1)} %multiply_convert_fusion.4), kind=kOutput, calls=%fused_computation.10 | convolution fusion | flops 14509670400 | bytes 23592960 | tf_op jit(solution)/shard_map/dot_general | solution.py:61
  509.8 25.2 %multiply_convert_fusion = bf16[1536,3072]{1,0:T(8,128)(2,1)S(1)} fusion(f32[1536,3072]{1,0:T(8,128)} %get-tuple-element.192, bf16[1536,1536]{1,0:T(8,128)(2,1)} %pad_maximum_fusion.2, bf16[1536,3072]{1,0:T(8,128)(2,1)} %all-gather.5.cloned.1.call-done), kind=kOutput, calls=%fused_computation.6 | convolution fusion | flops 14552137728 | bytes 42467328 | tf_op jit(solution)/shard_map/dot_general | solution.py:57
  535.1 14.8 %fusion.20 = bf16[768,1536]{1,0:T(8,128)(2,1)} fusion(bf16[1536,3072]{1,0:T(8,128)(2,1)} %all-gather.3.cloned.1.call-done, bf16[1536,3072]{1,0:T(8,128)(2,1)S(1)} %multiply_convert_fusion), kind=kOutput, calls=%fused_computation.71 | convolution fusion | flops 7248936960 | bytes 16515072 | tf_op jit(solution)/shard_map/dot_general | solution.py:53
  550.2 19.1 %convolution_convert_fusion = bf16[1536,3072]{1,0:T(8,128)(2,1)} fusion(bf16[1536,3072]{1,0:T(8,128)(2,1)S(1)} %multiply_convert_fusion, bf16[768,1536]{1,0:T(8,128)(2,1)} %collective-permute-done.6, bf16[768,1536]{1,0:T(8,128)(2,1)S(1)} %copy-done.25), kind=kOutput, calls=%fused_computation.9 | convolution fusion | flops 14509670400 | bytes 23592960 | tf_op jit(solution)/shard_map/dot_general | solution.py:61
  570.0 15.2 %multiply_reduce_fusion = (f32[1536]{0:T(1024)S(1)}, f32[768]{0:T(1024)S(1)}, f32[768]{0:T(1024)S(1)}, f32[1536]{0:T(1024)S(1)}, f32[768,1536]{1,0:T(8,128)S(1)}) fusion(f32[768,1536]{1,0:T(8,128)} %copy-done.2, f32[768]{0:T(1024)S(1)} %copy-done.56, f32[768]{0:T(1024)S(1)} %copy-done.52, bf16[768,1536]{1,0:T(8,128)(2,1)} %collective-permute-done.9, ...), kind=kOutput, calls=%fused_computation.28 | convolution fusion | flops 7260728832 | bytes 25982976 | tf_op jit(solution)/shard_map/dot_general | solution.py:53
  585.3 8.8 fusion.53
  598.7 5.4 convolution_convert_fusion.8
  624.0 5.3 multiply_reduce_fusion.1
  634.4 5.4 convolution_convert_fusion.9
  639.8 7.8 convolution_convert_fusion.7
  658.0 7.8 convolution_convert_fusion.2.refs_9_
  665.7 7.0 convolution_convert_fusion.3
  672.7 275.1 %sum_gradients.1 = (bf16[96,768]{1,0:T(8,128)(2,1)}, bf16[96,768]{1,0:T(8,128)(2,1)}, bf16[96,768]{1,0:T(8,128)(2,1)}, bf16[96,768]{1,0:T(8,128)(2,1)}, bf16[96,...) custom-call(bf16[4,2,2,96,768]{4,3,2,1,0:T(8,128)(2,1)} %bitcast.138, ...), custom_call_target="tpu_custom_call" | custom-call | tf_op jit(solution)/shard_map/sum_gradients/pallas_call | solution.py:881
  963.4 9.3 copy.69
  (290 shorter events, 151.8 us)
Async XLA Ops:
  7.3 376.3 %all-gather.3.cloned.1.call-start = ((), (), s32[]{:S(2)}) async-start(), calls=%async_computation.2 | async-start | bytes 10027008 | tf_op jit(solution)/shard_map/all_gather | solution.py:1027
  7.3 12.7 %collective-permute-start.1 = (bf16[96,3072]{1,0:T(8,128)(2,1)}, bf16[96,3072]{1,0:T(8,128)(2,1)}, u32[]{:S(2)}, u32[]{:S(2)}) collective-permute-start(bf16[96,3072]{1,0:T(8,128)(2,1)} %bitcast.158), channel_id=1, source_target_pairs={{1,2},{2,1},{5,6},{6,5},{9,10},{10,9},{13,14},{14,13},{17,18},{18,... | collective-permute-start | bytes 1769480 | tf_op jit(solution)/shard_map/ppermute | solution.py:33
  12.1 14.2 %collective-permute-start = (bf16[96,3072]{1,0:T(8,128)(2,1)}, bf16[96,3072]{1,0:T(8,128)(2,1)}, u32[]{:S(2)}, u32[]{:S(2)}) collective-permute-start(bf16[96,3072]{1,0:T(8,128)(2,1)} %param.38), channel_id=1, source_target_pairs={{1,2},{2,1},{5,6},{6,5},{9,10},{10,9},{13,14},{14,13},{17,18},{18,... | collective-permute-start | bytes 1769480 | tf_op jit(solution)/shard_map/ppermute | solution.py:33
  28.3 416.9 %all-gather.5.cloned.1.call-start = ((), (), s32[]{:S(2)}) async-start(), calls=%async_computation.3 | async-start | bytes 10027008 | tf_op jit(solution)/shard_map/all_gather | solution.py:1027
  318.4 11.7 %collective-permute-start.3 = (bf16[768,1536]{1,0:T(8,128)(2,1)}, bf16[768,1536]{1,0:T(8,128)(2,1)}, u32[]{:S(2)}, u32[]{:S(2)}) collective-permute-start(bf16[768,1536]{1,0:T(8,128)(2,1)} %convolution_convert_fusion.13), channel_id=1, source_target_pairs={{0,2},{2,0},{1,3},{3,1},{4,6},{6,4},{5,7},{7,5},{8,10},{10,8},{9,1... | collective-permute-start | bytes 7077896 | tf_op jit(solution)/shard_map/ppermute | solution.py:25
  325.6 650.6 %reduce-scatter.5.cloned.1.call-start = ((), (), s32[]{:S(2)}) async-start(), calls=%async_computation.5 | async-start | bytes 10027008 | tf_op jit(solution)/shard_map/reduce_scatter | solution.py:1053
  326.0 51.4 %copy-start.47 = (f32[1536]{0:T(1024)}, f32[1536]{0:T(1024)S(1)}, u32[]{:S(2)}) copy-start(f32[1536]{0:T(1024)S(1)} %get-tuple-element.161) | copy-start | bytes 18436
  338.8 4.9 collective-permute-start.4
  369.9 4.6 collective-permute-start.5
  377.4 30.2 %copy-start.55 = (f32[768]{0:T(1024)}, f32[768]{0:T(1024)S(1)}, u32[]{:S(2)}) copy-start(f32[768]{0:T(1024)S(1)} %add_rsqrt_fusion) | copy-start | bytes 9220
  379.0 28.7 %copy-start.24 = (bf16[768,1536]{1,0:T(8,128)(2,1)}, bf16[768,1536]{1,0:T(8,128)(2,1)S(1)}, u32[]{:S(2)}) copy-start(bf16[768,1536]{1,0:T(8,128)(2,1)S(1)} %add_convert_fusion) | copy-start | bytes 7077892
  379.0 4.7 collective-permute-start.6
  457.9 6.3 collective-permute-start.7
  461.2 2.1 collective-permute-start.2
  481.2 4.5 collective-permute-start.8
  509.7 470.5 %reduce-scatter.3.cloned.1.call-start = ((), (), s32[]{:S(2)}) async-start(), calls=%async_computation.4 | async-start | bytes 10027008 | tf_op jit(solution)/shard_map/reduce_scatter | solution.py:1056
  549.9 19.5 %collective-permute-start.9 = (bf16[768,1536]{1,0:T(8,128)(2,1)}, bf16[768,1536]{1,0:T(8,128)(2,1)}, u32[]{:S(2)}, u32[]{:S(2)}) collective-permute-start(bf16[768,1536]{1,0:T(8,128)(2,1)} %fusion.20), channel_id=1, source_target_pairs={{0,2},{2,0},{1,3},{3,1},{4,6},{6,4},{5,7},{7,5},{8,10},{10,8},{9,1... | collective-permute-start | bytes 7077896 | tf_op jit(solution)/shard_map/ppermute | solution.py:25
  594.1 4.6 collective-permute-start.10
  613.9 10.1 %collective-permute-start.11 = (bf16[768,1536]{1,0:T(8,128)(2,1)}, bf16[768,1536]{1,0:T(8,128)(2,1)}, u32[]{:S(2)}, u32[]{:S(2)}) collective-permute-start(bf16[768,1536]{1,0:T(8,128)(2,1)} %convolution_convert_fusion.4), channel_id=1, source_target_pairs={{0,2},{2,0},{1,3},{3,1},{4,6},{6,4},{5,7},{7,5},{8,10},{10,8},{9,1... | collective-permute-start | bytes 7077896 | tf_op jit(solution)/shard_map/ppermute | solution.py:25
  623.5 26.4 %collective-permute-start.13 = (bf16[64,768]{1,0:T(8,128)(2,1)S(1)}, bf16[64,768]{1,0:T(8,128)(2,1)S(1)}, u32[]{:S(2)}, u32[]{:S(2)}) collective-permute-start(bf16[64,768]{1,0:T(8,128)(2,1)S(1)} %broadcast_select_fusion.2), channel_id=1, source_target_pairs={{0,2},{2,0},{1,3},{3,1},{4,6},{6,4},{5,7},{7,5},{8,10},{10,8},{9,1... | collective-permute-start | bytes 294920 | tf_op jit(solution)/shard_map/ppermute | solution.py:25
  634.3 23.7 %collective-permute-start.12 = (bf16[768,1536]{1,0:T(8,128)(2,1)S(1)}, bf16[768,1536]{1,0:T(8,128)(2,1)}, u32[]{:S(2)}, u32[]{:S(2)}) collective-permute-start(bf16[768,1536]{1,0:T(8,128)(2,1)S(1)} %get-tuple-element.166), channel_id=1, source_target_pairs={{0,2},{2,0},{1,3},{3,1},{4,6},{6,4},{5,7},{7,5},{8,10},{10,8},{9,1... | collective-permute-start | bytes 7077896 | tf_op jit(solution)/shard_map/ppermute | solution.py:25
  649.9 6.0 collective-permute-start.14
  976.2 11.5 %collective-permute-start.16 = (bf16[96,3072]{1,0:T(8,128)(2,1)}, bf16[96,3072]{1,0:T(8,128)(2,1)S(1)}, u32[]{:S(2)}, u32[]{:S(2)}) collective-permute-start(bf16[96,3072]{1,0:T(8,128)(2,1)} %reduce-scatter.5.cloned.1.call-done), channel_id=1, source_target_pairs={{1,2},{2,1},{5,6},{6,5},{9,10},{10,9},{13,14},{14,13},{17,18},{18,... | collective-permute-start | bytes 1769480 | tf_op jit(solution)/shard_map/ppermute | solution.py:33
  980.2 13.9 %collective-permute-start.15 = (bf16[96,3072]{1,0:T(8,128)(2,1)}, bf16[96,3072]{1,0:T(8,128)(2,1)S(1)}, u32[]{:S(2)}, u32[]{:S(2)}) collective-permute-start(bf16[96,3072]{1,0:T(8,128)(2,1)} %reduce-scatter.3.cloned.1.call-done), channel_id=1, source_target_pairs={{1,2},{2,1},{5,6},{6,5},{9,10},{10,9},{13,14},{14,13},{17,18},{18,... | collective-permute-start | bytes 1769480 | tf_op jit(solution)/shard_map/ppermute | solution.py:33
  (79 other events, 716.3 us)
Sparse Core Ops, SparseCore 0:
  28.4 180.6 all-gather.2
  325.8 119.3 all-gather.4
  509.9 167.9 reduce-scatter.4
  684.4 271.7 reduce-scatter.2

commit v5 on v4

--- a/solution.py
+++ b/solution.py
@@ -363,11 +363,11 @@
 
 
 def gather_kernel(slots, count, real, *refs):
-    blocks, (frames, text, target) = refs[:count], refs[count : count + 3]
-    refs = refs[count + 3 :]
-    weights, (own_out, text_out, target_out) = refs[:count], refs[count : count + 3]
-    gains_ref, h_ref, q_ref, k_ref, v_ref, o_ref, lse_ref = refs[count + 3 : count + 10]
-    send, recv, cross_send, cross_recv, cross_local, core_send, core_recv, loads, tiny, both, held = refs[count + 10 :]
+    blocks, (frames, text) = refs[:count], refs[count : count + 2]
+    refs = refs[count + 2 :]
+    weights, (own_out, text_out) = refs[:count], refs[count : count + 2]
+    gains_ref, h_ref, q_ref, k_ref, v_ref, o_ref, lse_ref = refs[count + 2 : count + 9]
+    send, recv, cross_send, cross_recv, cross_local, core_send, core_recv, loads, tiny, both, held = refs[count + 9 :]
     rows, width = h_ref.shape
     half = rows // 2
     pairs = q_ref.shape[1] // LANES
@@ -377,7 +377,7 @@
     chains = gather_events(where, slots, weights, send, recv)
     starts = list(bring_own(crossing, where, slots, chains, blocks, weights))
     frames_start, frames_finish = crossing.prepare(frames, both.at[0])
-    moves = [crossing.prepare(*pair) for pair in ((text, text_out), (target, target_out))]
+    text_start, text_finish = crossing.prepare(text, text_out)
     sibling = pltpu.make_async_remote_copy(
         src_ref=both.at[0], dst_ref=both.at[1], send_sem=core_send, recv_sem=core_recv,
         device_id={"c": 1 - c}, device_id_type=MESH,
@@ -394,17 +394,15 @@
                 run_events(chains[number][stage])
 
     greet(c, y, up, down, x, True)
-    for start in starts[:NEEDED_FIRST]:
-        start()
-    frames_start()
-    for start in starts[NEEDED_FIRST:]:
-        start()
-    for start, _ in moves:
+    for start in starts:
         start()
     ready = NEEDED_FIRST + TICKS - 1
     for at in range(ready):
         tick(at)
-        if at == 3:
+        if at == 2:
+            frames_start()
+            text_start()
+        if at == 5:
             frames_finish()
             sibling.start()
             keep.start()
@@ -457,16 +455,15 @@
     for ticks in chains[NEEDED_FIRST:]:
         run_events(ticks[TICKS - 1])
     keep.wait()
-    for _, finish in moves:
-        finish()
-
-
-def gather(blocks, frames, text, target, real, slots):
+    text_finish()
+
+
+def gather(blocks, frames, text, real, slots):
     count = len(blocks)
     rows, width = 2 * frames.shape[0], frames.shape[1]
     share = blocks[1].shape[1]
     pairs = share // LANES
-    crossings = count + 3
+    crossings = count + 2
     dma = pltpu.SemaphoreType.DMA
     vmem = pl.BlockSpec(memory_space=pltpu.VMEM)
     heads = jax.ShapeDtypeStruct((rows, share), BRAIN)
@@ -475,12 +472,12 @@
         functools.partial(gather_kernel, slots, count, real),
         out_shape=[
             *gathered,
-            *[jax.ShapeDtypeStruct(v.shape, v.dtype) for v in (frames, text, target)],
+            *[jax.ShapeDtypeStruct(v.shape, v.dtype) for v in (frames, text)],
             jax.ShapeDtypeStruct((8, width), FLOAT), jax.ShapeDtypeStruct((rows, width), BRAIN),
             heads, heads, heads, heads, jax.ShapeDtypeStruct((pairs, 8, rows), FLOAT),
         ],
-        in_specs=[ANY] * (count + 3),
-        out_specs=[ANY] * (count + 3) + [vmem] * 7,
+        in_specs=[ANY] * (count + 2),
+        out_specs=[ANY] * (count + 2) + [vmem] * 7,
         scratch_shapes=[
             dma((len(slots), 3, 5)), dma((len(slots), 3, 5)),
             dma((crossings,)), dma((crossings,)), dma((crossings,)), dma, dma, dma((5,)),
@@ -491,7 +488,7 @@
             collective_id=1, has_side_effects=True, vmem_limit_bytes=56 * 2**20
         ),
         name="gather",
-    )(*blocks, frames, text, target)
+    )(*blocks, frames, text)
 
 
 def plus(*terms):
@@ -659,10 +656,10 @@
 
 def sum_kernel(slots, count, real, *refs):
     terms, refs = refs[:count], refs[count:]
-    home, q, k, v, do, o, h, w_q, w_k, w_v, x0, dx1, lse, gains, vectors = refs[:15]
-    refs = refs[15:]
-    outs, (home_out, frames_out, vectors_out) = refs[: count + 3], refs[count + 3 : count + 6]
-    refs = refs[count + 6 :]
+    q, k, v, do, o, h, w_q, w_k, w_v, x0, dx1, lse, gains, vectors = refs[:14]
+    refs = refs[14:]
+    outs, (frames_out, vectors_out) = refs[: count + 3], refs[count + 3 : count + 5]
+    refs = refs[count + 5 :]
     lands = len([1 for _, _, sizes in slots for kind, order in enumerate(ORDERS) if sizes[kind] and order != "xyz"])
     landings, refs = refs[:lands], refs[lands:]
     send, recv, local, cross_send, cross_recv, cross_local, v_send, v_recv, h_send, h_recv, loads = refs[:11]
@@ -681,12 +678,10 @@
     chains = sum_events(where, slots, all_terms, outs, landings, refs[22:], pads, crossing, send, recv, local)
     early = [n for n, slot in enumerate(slots) if slot[0] < count]
     late = [n for n, slot in enumerate(slots) if slot[0] >= count]
-    home_start, home_finish = crossing.prepare(home, home_out)
     frames_start, frames_finish = crossing.prepare(far, frames_out)
     greet(c, y, up, down, x, True)
     for n in early:
         run_events(chains[n][0])
-    home_start()
 
     work = tiles * (tiles + 1) // 2
     times = [p + sum(tiles - i for i in range(j)) / work for p in range(pairs) for j in range(tiles)]
@@ -863,16 +858,15 @@
     z_down.wait()
     z_more.wait()
     vectors_out[...] = (held[6] + held[7]) + (held[8] + held[9])
-    home_finish()
     frames_finish()
 
 
-def sum_gradients(terms, home, attention, h, weights, x0, dx1, lse, gains, vectors, real, slots):
+def sum_gradients(terms, attention, h, weights, x0, dx1, lse, gains, vectors, real, slots):
     count = len(terms)
     rows, share = attention[0].shape
     half, width = x0.shape
     size = terms[0].shape[3]
-    crossings = 3 * len(slots) + 2
+    crossings = 3 * len(slots) + 1
     dma = pltpu.SemaphoreType.DMA
     vmem = pl.BlockSpec(memory_space=pltpu.VMEM)
     landings = sum_landings(slots, size)
@@ -880,10 +874,10 @@
     most = [max(sizes[kind] for _, _, sizes in slots) for kind in range(2)]
     results = pl.pallas_call(
         functools.partial(sum_kernel, slots, count, real),
-        in_specs=[ANY] * (count + 12) + [vmem] * 3,
-        out_specs=[ANY] * (count + 5) + [vmem] + [ANY] * len(landings),
+        in_specs=[ANY] * (count + 11) + [vmem] * 3,
+        out_specs=[ANY] * (count + 4) + [vmem] + [ANY] * len(landings),
         out_shape=[jax.ShapeDtypeStruct((size, n), BRAIN) for n in widths]
-        + [jax.ShapeDtypeStruct(home.shape, BRAIN), jax.ShapeDtypeStruct(x0.shape, BRAIN)]
+        + [jax.ShapeDtypeStruct(x0.shape, BRAIN)]
         + [jax.ShapeDtypeStruct(vectors.shape, FLOAT)]
         + landings,
         scratch_shapes=[
@@ -900,8 +894,8 @@
             collective_id=3, has_side_effects=True, vmem_limit_bytes=58 * 2**20
         ),
         name="sum_gradients",
-    )(*terms, home, *attention, h, *weights, x0, dx1, lse, gains, vectors)
-    return results[: count + 6]
+    )(*terms, *attention, h, *weights, x0, dx1, lse, gains, vectors)
+    return results[: count + 5]
 
 
 def slots_of(widths, six=((2, 3, 1), (2, 3, 1), (3, 2, 1)), eight=(3, 3, 2)):
@@ -1009,15 +1003,15 @@
     flags = jnp.pad(valid_frames[0][:, None].astype(BRAIN), ((0, 0), (0, LANES - 1)))
     target = padded(jnp.concatenate([teacher[0], flags], 1))
     if fits:
-        slots = slots_of([v.shape[1] for v in weights])
+        slots = slots_of([v.shape[1] for v in weights], six=((2, 3, 1), (1, 3, 2)))
         frames, *wide = lax.optimization_barrier((frames, *wide))
-        *weights, x_own, text, target, gains, h1, q1, k1, v1, o1, lse1 = gather(
-            weights, frames, text_states[0], target, real, slots
+        *weights, x_own, text, gains, h1, q1, k1, v1, o1, lse1 = gather(
+            weights, frames, text_states[0], real, slots
         )
         weights = [joined(v) for v in weights]
     else:
         weights = [lax.all_gather(swap_clip(v), CHIPS, axis=0, tiled=True) for v in weights]
-        x_own, text, target = (swap_clip(v) for v in (frames, text_states[0], target))
+        x_own, text = (swap_clip(v) for v in (frames, text_states[0]))
         gains = weights[0].T.astype(FLOAT)
         x_all = jnp.concatenate([x_own, swap_core(x_own)], 0)
         h1 = normalize(x_all.astype(FLOAT), gains[0], gains[1]).astype(BRAIN)
@@ -1028,6 +1022,8 @@
     counted = jnp.sum(tiny[:, 6:8].astype(FLOAT), 0)
     counted = counted[0] * 64.0 + counted[1]
     token_count = counted + swap_core(counted)
+    target, x_own = lax.optimization_barrier((target, x_own))
+    target = swap_weight(target)
     valid = target[:, width : width + 1].astype(FLOAT)
     target = target[:, :width].astype(FLOAT)
     x0 = x_own.astype(FLOAT)
@@ -1041,7 +1037,7 @@
     h3 = both(normalize(x2, gains[4], gains[5]).astype(BRAIN))
     g, slope = gelu_pair(dot_nn(h3, w_fi))
     y = x2 + summed(g, w_fo)
-    home = y.astype(BRAIN)
+    home = swap_weight(y.astype(BRAIN))
     deviation = y - target
     error = jnp.sum(valid * deviation * deviation)
     tokens_all = real * lax.axis_size(("z", "x", "c", "y"))
@@ -1081,8 +1077,8 @@
     grads = [co_grad, cq_grad, ck_grad, cv_grad, so_grad]
     if fits:
         slots = slots_of([v.shape[1] for v in grads] + [share] * 3, six=((2, 2, 2),))
-        *grads, home, frames, vectors = sum_gradients(
-            [by_chip(v) for v in grads], home, (q1, k1, v1, do1, o1), h1,
+        *grads, frames, vectors = sum_gradients(
+            [by_chip(v) for v in grads], (q1, k1, v1, do1, o1), h1,
             [by_chip(v) for v in (w_q, w_k, w_v)], x_own, dx1, lse1, gains, vectors, real, slots,
         )
     else:
@@ -1093,7 +1089,6 @@
         frames = swap_clip((dx1 + term).astype(BRAIN))
         grads += [dot_tn(h1, d).astype(BRAIN) for d in (dq1, dk1, dv1)]
         grads = [swap_clip(lax.psum_scatter(v, CHIPS, scatter_dimension=0, tiled=True)) for v in grads]
-        home = swap_clip(home)
         vectors = lax.psum(vectors.at[:2].set(jnp.stack([gain1, bias1])), ("z", "x", "c", "y"))
     layer_out = home[:real][None]
     inputs_grad = frames[None].astype(FLOAT)[:, :real]

time: 1010 us -> 1030 us (1.020)
  waiting for transfers between devices: 77.5 us -> 114 us
  Pallas kernels: 553 us -> 535 us
    ppermute x4 -> x6, waiting for transfers between devices: 16.6 us -> 40.6 us  [swap_others(): return lax.ppermute(v, ('c', 'y'), [(1, 2), (2, 1)])]
    all_gather x2, waiting for transfers between devices: 37.5 us -> 56.8 us  [on_device(): w_fi, w_fo = (lax.all_gather(v, CHIPS, axis=0, tiled=True) for v in wide)]
    pallas_call x1, Pallas kernels: 278 us -> 267 us  [gather(): pl.pallas_call(functools.partial(gather_kernel, slots, count, real), out_...]
  transfers between devices with their start and end apart: 21 -> 23, of which waited for: 11 -> 13; matrix products, arithmetic and copies ran while one was open for 26% -> 26% of each run, Pallas kernels for 55% -> 52%
where the time goes in v5:
time: 1030 us; the launch traced here: 1020 us
  Pallas kernels  535 us (52%)
  matrix products  236 us (23%)
  waiting for transfers between devices  114 us (11%)
  other arithmetic  54.4 us (5%)
  local copies, waits for them, and re-layouts  32.3 us (3%)
  starting transfers between devices  27.9 us (3%)
  between operations  21.7 us (2%)
    pallas_call x1, Pallas kernels, sum_gradients(): pl.pallas_call(functools.partial(sum_kernel, slots, count, real), in_spec...  268 us
    pallas_call x1, Pallas kernels, gather(): pl.pallas_call(functools.partial(gather_kernel, slots, count, real), out_...  267 us
    dot_general x12, matrix products, dot_nt(): lax.dot_general(a, b, (((1,), (1,)), ((), ())), preferred_element_type=FL...  92.6 us
    dot_general x7, matrix products, dot_nn(): lax.dot_general(a, b, (((1,), (0,)), ((), ())), preferred_element_type=FL...  72.8 us
    dot_general x7, matrix products, dot_tn(): lax.dot_general(a, b, (((0,), (0,)), ((), ())), preferred_element_type=FL...  63.5 us
    all_gather x2, waiting for transfers between devices, on_device(): w_fi, w_fo = (lax.all_gather(v, CHIPS, axis=0, tiled=True) for v in wide)  56.8 us
    ppermute x6, waiting for transfers between devices, swap_others(): return lax.ppermute(v, ('c', 'y'), [(1, 2), (2, 1)])  40.6 us
    unnamed x165, local copies, waits for them, and re-layouts  21.5 us
  transfers between devices with their start and end apart: 23, of which 13 were waited for; matrix products, arithmetic and copies ran while one was open for 26% of the time, Pallas kernels for 52%

profile of v5, /device:TPU:1, one launch (start us, length us, event | category | flops | bytes accessed | tf_op | source)
XLA Modules:
  0.0 1021.7 jit_solution(3709286126761077660)
XLA Ops:
  20.6 5.4 collective-permute-done
  31.3 267.1 %gather.1 = (bf16[4,2,2,96,128]{4,3,2,1,0:T(8,128)(2,1)}, bf16[4,2,2,96,768]{4,3,2,1,0:T(8,128)(2,1)}, bf16[4,2,2,96,768]{4,3,2,1,0:T(8,128)(2,1)}, bf16[4,2,2,9...) custom-call(bf16[96,128]{1,0:T(8,128)(2,1)} %pad.16.refs_0_, ...), custom_call_target="tpu_custom_call" | custom-call | tf_op jit(solution)/shard_map/gather/pallas_call | solution.py:471
  298.4 5.6 convolution_convert_fusion.13
  323.4 7.0 convolution_convert_fusion.12
  336.3 12.9 %convolution_convert_fusion.10 = bf16[768,1536]{1,0:T(8,128)(2,1)S(1)} fusion(bf16[768,768]{0,1:T(8,128)(2,1)S(1)} %bitcast.156, bf16[1536,768]{1,0:T(8,128)(2,1)S(1)} %bitcast.177), kind=kOutput, calls=%fused_computation.66 | convolution fusion | flops 1813118976 | bytes 5898240 | tf_op jit(solution)/shard_map/dot_general | solution.py:53
  363.0 23.9 %multiply_convert_fusion.1 = (bf16[1536,3072]{1,0:T(8,128)(2,1)}, f32[1536,3072]{1,0:T(8,128)}) fusion(bf16[1536,3072]{1,0:T(8,128)(2,1)} %all-gather.3.cloned.1.call-done, bf16[768,1536]{1,0:T(8,128)(2,1)} %collective-permute-done.7, bf16[768,1536]{1,0:T(8,128)(2,1)} %copy-done.20), kind=kOutput, calls=%fused_computation.7 | convolution fusion | flops 14528544768 | bytes 42467328 | tf_op jit(solution)/shard_map/dot_general | solution.py:57
  386.9 56.8 %all-gather.5.cloned.1.call-done = bf16[1536,3072]{1,0:T(8,128)(2,1)} async-done(((bf16[96,3072]{1,0:T(8,128)(2,1)}), bf16[1536,3072]{1,0:T(8,128)(2,1)}) %all-gather.5.cloned.1.call-update) | async-done | bytes 9437200 | tf_op jit(solution)/shard_map/all_gather | solution.py:1021
  443.7 12.6 %fusion.17 = bf16[768,1536]{1,0:T(8,128)(2,1)} fusion(bf16[1536,3072]{1,0:T(8,128)(2,1)} %all-gather.5.cloned.1.call-done, bf16[1536,3072]{1,0:T(8,128)(2,1)} %get-tuple-element.191), kind=kOutput, calls=%fused_computation.70 | convolution fusion | flops 7248936960 | bytes 16515072 | tf_op jit(solution)/shard_map/dot_general | solution.py:53
  464.7 14.2 %fusion.53 = (bf16[768,1536]{1,0:T(8,128)(2,1)}, f32[768,1536]{1,0:T(8,128)S(1)}) fusion(f32[768,1536]{1,0:T(8,128)} %copy-done.2, bf16[768,1536]{1,0:T(8,128)(2,1)} %collective-permute-done.8, bf16[1536,3072]{1,0:T(8,128)(2,1)} %all-gather.5.cloned.1.call-done, bf16[1536,3072]{1,0:T(8,128)(2,1)} %get-tuple-element.191), kind=kOutput, calls=%fused_computation.140 | convolution fusion | flops 7252475904 | bytes 28311552 | tf_op jit(solution)/shard_map/dot_general | solution.py:53
  487.8 19.4 %convolution_convert_fusion.1 = bf16[1536,3072]{1,0:T(8,128)(2,1)} fusion(bf16[1536,3072]{1,0:T(8,128)(2,1)} %get-tuple-element.191, bf16[768,1536]{1,0:T(8,128)(2,1)S(1)} %collective-permute-done.9, bf16[768,1536]{1,0:T(8,128)(2,1)S(1)} %multiply_convert_fusion.4), kind=kOutput, calls=%fused_computation.10 | convolution fusion | flops 14509670400 | bytes 23592960 | tf_op jit(solution)/shard_map/dot_general | solution.py:61
  512.0 25.3 %multiply_convert_fusion = bf16[1536,3072]{1,0:T(8,128)(2,1)S(1)} fusion(f32[1536,3072]{1,0:T(8,128)} %get-tuple-element.192, bf16[1536,1536]{1,0:T(8,128)(2,1)} %pad_maximum_fusion.2, bf16[1536,3072]{1,0:T(8,128)(2,1)} %all-gather.5.cloned.1.call-done), kind=kOutput, calls=%fused_computation.6 | convolution fusion | flops 14552137728 | bytes 42467328 | tf_op jit(solution)/shard_map/dot_general | solution.py:57
  537.3 14.8 %fusion.20 = bf16[768,1536]{1,0:T(8,128)(2,1)} fusion(bf16[1536,3072]{1,0:T(8,128)(2,1)} %all-gather.3.cloned.1.call-done, bf16[1536,3072]{1,0:T(8,128)(2,1)S(1)} %multiply_convert_fusion), kind=kOutput, calls=%fused_computation.71 | convolution fusion | flops 7248936960 | bytes 16515072 | tf_op jit(solution)/shard_map/dot_general | solution.py:53
  552.4 19.1 %convolution_convert_fusion = bf16[1536,3072]{1,0:T(8,128)(2,1)} fusion(bf16[1536,3072]{1,0:T(8,128)(2,1)S(1)} %multiply_convert_fusion, bf16[768,1536]{1,0:T(8,128)(2,1)} %collective-permute-done.7, bf16[768,1536]{1,0:T(8,128)(2,1)S(1)} %copy-done.21), kind=kOutput, calls=%fused_computation.9 | convolution fusion | flops 14509670400 | bytes 23592960 | tf_op jit(solution)/shard_map/dot_general | solution.py:61
  572.2 15.2 %multiply_reduce_fusion = (f32[1536]{0:T(1024)S(1)}, f32[768]{0:T(1024)S(1)}, f32[768]{0:T(1024)S(1)}, f32[1536]{0:T(1024)S(1)}, f32[768,1536]{1,0:T(8,128)S(1)}) fusion(f32[768,1536]{1,0:T(8,128)} %copy-done.2, f32[768]{0:T(1024)S(1)} %copy-done.53, f32[768]{0:T(1024)S(1)} %copy-done.49, bf16[768,1536]{1,0:T(8,128)(2,1)} %collective-permute-done.10, ...), kind=kOutput, calls=%fused_computation.28 | convolution fusion | flops 7260728832 | bytes 25982976 | tf_op jit(solution)/shard_map/dot_general | solution.py:53
  587.5 8.5 fusion.55
  600.6 5.5 convolution_convert_fusion.8
  615.5 23.4 %collective-permute-done.14 = bf16[768,1536]{1,0:T(8,128)(2,1)} collective-permute-done((bf16[768,1536]{1,0:T(8,128)(2,1)}, bf16[768,1536]{1,0:T(8,128)(2,1)}, u32[]{:S(2)}, u32[]{:S(2)}) %collective-permute-start.14) | collective-permute-done | bytes 2359328 | tf_op jit(solution)/shard_map/ppermute | solution.py:33
  650.2 5.6 multiply_reduce_fusion.1
  655.9 5.5 fusion.54
  666.5 7.7 convolution_convert_fusion.7
  684.6 8.5 convolution_convert_fusion.2.refs_8_
  693.0 7.7 convolution_convert_fusion.3
  700.8 267.8 %sum_gradients.1 = (bf16[96,768]{1,0:T(8,128)(2,1)}, bf16[96,768]{1,0:T(8,128)(2,1)}, bf16[96,768]{1,0:T(8,128)(2,1)}, bf16[96,768]{1,0:T(8,128)(2,1)}, bf16[96,...) custom-call(bf16[4,2,2,96,768]{4,3,2,1,0:T(8,128)(2,1)} %bitcast.144, ...), custom_call_target="tpu_custom_call" | custom-call | tf_op jit(solution)/shard_map/sum_gradients/pallas_call | solution.py:875
  984.1 9.2 copy.69
  (296 shorter events, 151.5 us)
Async XLA Ops:
  7.3 355.7 %all-gather.3.cloned.1.call-start = ((), (), s32[]{:S(2)}) async-start(), calls=%async_computation.2 | async-start | bytes 10027008 | tf_op jit(solution)/shard_map/all_gather | solution.py:1021
  7.3 12.4 %collective-permute-start.1 = (bf16[96,3072]{1,0:T(8,128)(2,1)}, bf16[96,3072]{1,0:T(8,128)(2,1)S(1)}, u32[]{:S(2)}, u32[]{:S(2)}) collective-permute-start(bf16[96,3072]{1,0:T(8,128)(2,1)} %bitcast.160), channel_id=1, source_target_pairs={{1,2},{2,1},{5,6},{6,5},{9,10},{10,9},{13,14},{14,13},{17,18},{18,... | collective-permute-start | bytes 1769480 | tf_op jit(solution)/shard_map/ppermute | solution.py:33
  12.0 14.1 %collective-permute-start = (bf16[96,3072]{1,0:T(8,128)(2,1)}, bf16[96,3072]{1,0:T(8,128)(2,1)S(1)}, u32[]{:S(2)}, u32[]{:S(2)}) collective-permute-start(bf16[96,3072]{1,0:T(8,128)(2,1)} %param.38), channel_id=1, source_target_pairs={{1,2},{2,1},{5,6},{6,5},{9,10},{10,9},{13,14},{14,13},{17,18},{18,... | collective-permute-start | bytes 1769480 | tf_op jit(solution)/shard_map/ppermute | solution.py:33
  27.0 416.7 %all-gather.5.cloned.1.call-start = ((), (), s32[]{:S(2)}) async-start(), calls=%async_computation.3 | async-start | bytes 10027008 | tf_op jit(solution)/shard_map/all_gather | solution.py:1021
  304.0 6.9 collective-permute-start.4
  306.7 688.0 %reduce-scatter.5.cloned.1.call-start = ((), (), s32[]{:S(2)}) async-start(), calls=%async_computation.5 | async-start | bytes 10027008 | tf_op jit(solution)/shard_map/reduce_scatter | solution.py:1049
  307.4 51.3 %copy-start.4 = (bf16[768,1664]{1,0:T(8,128)(2,1)}, bf16[768,1664]{1,0:T(8,128)(2,1)S(1)}, u32[]{:S(2)}) copy-start(bf16[768,1664]{1,0:T(8,128)(2,1)S(1)} %pad.19) | copy-start | bytes 7667716
  318.5 4.9 collective-permute-start.5
  349.3 4.6 collective-permute-start.6
  358.4 4.7 collective-permute-start.7
  358.7 103.3 %collective-permute-start.3 = (bf16[768,1664]{1,0:T(8,128)(2,1)S(1)}, bf16[768,1664]{1,0:T(8,128)(2,1)}, u32[]{:S(2)}, u32[]{:S(2)}) collective-permute-start(bf16[768,1664]{1,0:T(8,128)(2,1)S(1)} %pad.19), channel_id=1, source_target_pairs={{1,2},{2,1},{5,6},{6,5},{9,10},{10,9},{13,14},{14,13},{17,18},{18,... | collective-permute-start | bytes 7667720 | tf_op jit(solution)/shard_map/ppermute | solution.py:33
  456.2 8.5 collective-permute-start.8
  459.3 2.1 collective-permute-start.2
  481.8 4.6 collective-permute-start.9
  512.0 486.7 %reduce-scatter.3.cloned.1.call-start = ((), (), s32[]{:S(2)}) async-start(), calls=%async_computation.4 | async-start | bytes 10027008 | tf_op jit(solution)/shard_map/reduce_scatter | solution.py:1052
  552.1 19.5 %collective-permute-start.10 = (bf16[768,1536]{1,0:T(8,128)(2,1)}, bf16[768,1536]{1,0:T(8,128)(2,1)}, u32[]{:S(2)}, u32[]{:S(2)}) collective-permute-start(bf16[768,1536]{1,0:T(8,128)(2,1)} %fusion.20), channel_id=1, source_target_pairs={{0,2},{2,0},{1,3},{3,1},{4,6},{6,4},{5,7},{7,5},{8,10},{10,8},{9,1... | collective-permute-start | bytes 7077896 | tf_op jit(solution)/shard_map/ppermute | solution.py:25
  596.0 4.5 collective-permute-start.11
  596.4 42.6 %collective-permute-start.14 = (bf16[768,1536]{1,0:T(8,128)(2,1)}, bf16[768,1536]{1,0:T(8,128)(2,1)}, u32[]{:S(2)}, u32[]{:S(2)}) collective-permute-start(bf16[768,1536]{1,0:T(8,128)(2,1)} %get-tuple-element.164), channel_id=1, source_target_pairs={{1,2},{2,1},{5,6},{6,5},{9,10},{10,9},{13,14},{14,13},{17,18},{18,... | collective-permute-start | bytes 7077896 | tf_op jit(solution)/shard_map/ppermute | solution.py:33
  615.2 34.1 %collective-permute-start.12 = (bf16[768,1536]{1,0:T(8,128)(2,1)}, bf16[768,1536]{1,0:T(8,128)(2,1)}, u32[]{:S(2)}, u32[]{:S(2)}) collective-permute-start(bf16[768,1536]{1,0:T(8,128)(2,1)} %convolution_convert_fusion.4), channel_id=1, source_target_pairs={{0,2},{2,0},{1,3},{3,1},{4,6},{6,4},{5,7},{7,5},{8,10},{10,8},{9,1... | collective-permute-start | bytes 7077896 | tf_op jit(solution)/shard_map/ppermute | solution.py:25
  649.2 27.3 %collective-permute-start.15 = (bf16[64,768]{1,0:T(8,128)(2,1)S(1)}, bf16[64,768]{1,0:T(8,128)(2,1)S(1)}, u32[]{:S(2)}, u32[]{:S(2)}) collective-permute-start(bf16[64,768]{1,0:T(8,128)(2,1)S(1)} %broadcast_select_fusion.3), channel_id=1, source_target_pairs={{0,2},{2,0},{1,3},{3,1},{4,6},{6,4},{5,7},{7,5},{8,10},{10,8},{9,1... | collective-permute-start | bytes 294920 | tf_op jit(solution)/shard_map/ppermute | solution.py:25
  661.4 23.2 %collective-permute-start.13 = (bf16[768,1536]{1,0:T(8,128)(2,1)}, bf16[768,1536]{1,0:T(8,128)(2,1)}, u32[]{:S(2)}, u32[]{:S(2)}) collective-permute-start(bf16[768,1536]{1,0:T(8,128)(2,1)} %get-tuple-element.166), channel_id=1, source_target_pairs={{0,2},{2,0},{1,3},{3,1},{4,6},{6,4},{5,7},{7,5},{8,10},{10,8},{9,1... | collective-permute-start | bytes 7077896 | tf_op jit(solution)/shard_map/ppermute | solution.py:25
  676.6 5.9 collective-permute-start.16
  994.7 11.4 %collective-permute-start.18 = (bf16[96,3072]{1,0:T(8,128)(2,1)}, bf16[96,3072]{1,0:T(8,128)(2,1)S(1)}, u32[]{:S(2)}, u32[]{:S(2)}) collective-permute-start(bf16[96,3072]{1,0:T(8,128)(2,1)} %reduce-scatter.5.cloned.1.call-done), channel_id=1, source_target_pairs={{1,2},{2,1},{5,6},{6,5},{9,10},{10,9},{13,14},{14,13},{17,18},{18,... | collective-permute-start | bytes 1769480 | tf_op jit(solution)/shard_map/ppermute | solution.py:33
  998.7 13.8 %collective-permute-start.17 = (bf16[96,3072]{1,0:T(8,128)(2,1)}, bf16[96,3072]{1,0:T(8,128)(2,1)S(1)}, u32[]{:S(2)}, u32[]{:S(2)}) collective-permute-start(bf16[96,3072]{1,0:T(8,128)(2,1)} %reduce-scatter.3.cloned.1.call-done), channel_id=1, source_target_pairs={{1,2},{2,1},{5,6},{6,5},{9,10},{10,9},{13,14},{14,13},{17,18},{18,... | collective-permute-start | bytes 1769480 | tf_op jit(solution)/shard_map/ppermute | solution.py:33
  (81 other events, 745.0 us)
Sparse Core Ops, SparseCore 0:
  27.1 230.8 all-gather.2
  306.8 136.8 all-gather.4
  512.1 169.9 reduce-scatter.4
  688.6 258.0 reduce-scatter.2

commit v6 on v4

--- a/solution.py
+++ b/solution.py
@@ -940,34 +940,74 @@
     return (u * half_erf).astype(BRAIN), (half_erf + u * density).astype(BRAIN)
 
 
-def split_heads(values):
-    return values.reshape(values.shape[0], -1, HEAD_DIM)
-
-
-def merge_heads(values):
-    return values.reshape(values.shape[0], -1)
+def cross_probs(queries, keys, first, head):
+    mine = first if head == 0 else jnp.logical_not(first)
+    masked = jnp.where(mine, queries, 0.0).astype(BRAIN)
+    s = dot_nt(masked, keys)
+    e = jnp.exp(s - jnp.max(s, 1, keepdims=True))
+    return masked, mine, e / jnp.sum(e, 1, keepdims=True)
+
+
+def cross_kernel(q_ref, k_ref, v_ref, o_ref):
+    first = lax.broadcasted_iota(jnp.int32, (2 * ROWS, LANES), 1) < HEAD_DIM
+    for start in range(0, q_ref.shape[0], 2 * ROWS):
+        rows = pl.ds(start, 2 * ROWS)
+        queries = q_ref[rows, :].astype(FLOAT) * SCALE
+        outs = []
+        for head in range(2):
+            _, _, probs = cross_probs(queries, k_ref[...], first, head)
+            outs.append(dot_nn(probs.astype(BRAIN), v_ref[...]))
+        o_ref[rows, :] = jnp.where(first, outs[0], outs[1]).astype(BRAIN)
+
+
+def cross_back_kernel(q_ref, k_ref, v_ref, do_ref, dq_ref, dk_ref, dv_ref):
+    first = lax.broadcasted_iota(jnp.int32, (2 * ROWS, LANES), 1) < HEAD_DIM
+    dk = jnp.zeros(k_ref.shape, FLOAT)
+    dv = jnp.zeros(v_ref.shape, FLOAT)
+    for start in range(0, q_ref.shape[0], 2 * ROWS):
+        rows = pl.ds(start, 2 * ROWS)
+        queries = q_ref[rows, :].astype(FLOAT) * SCALE
+        grads = do_ref[rows, :].astype(FLOAT)
+        dqs = []
+        for head in range(2):
+            q_m, mine, probs = cross_probs(queries, k_ref[...], first, head)
+            do_m = jnp.where(mine, grads, 0.0).astype(BRAIN)
+            dp = dot_nt(do_m, v_ref[...])
+            ds = (probs * (dp - jnp.sum(probs * dp, 1, keepdims=True))).astype(BRAIN)
+            dqs.append(dot_nn(ds, k_ref[...]))
+            dk = dk + dot_tn(ds, q_m)
+            dv = dv + dot_tn(probs.astype(BRAIN), do_m)
+        dq_ref[rows, :] = (jnp.where(first, dqs[0], dqs[1]) * SCALE).astype(BRAIN)
+    dk_ref[...] = dk.astype(BRAIN)
+    dv_ref[...] = dv.astype(BRAIN)
 
 
 def attend_cross(q, k, v):
-    scores = jnp.einsum("qhd,khd->hqk", q, k, preferred_element_type=FLOAT) * SCALE
-    top = jnp.max(scores, -1, keepdims=True)
-    e = jnp.exp(scores - top)
-    total = jnp.sum(e, -1, keepdims=True)
-    probs = e / total
-    out = jnp.einsum("hqk,khd->qhd", probs.astype(BRAIN), v, preferred_element_type=FLOAT)
-    return merge_heads(out).astype(BRAIN), (top + jnp.log(total))[..., 0]
-
-
-def attend_cross_back(q, k, v, do, lse):
-    scores = jnp.einsum("qhd,khd->hqk", q, k, preferred_element_type=FLOAT) * SCALE
-    probs = jnp.exp(scores - lse[..., None])
-    dp = jnp.einsum("qhd,khd->hqk", do, v, preferred_element_type=FLOAT)
-    inner = jnp.sum(probs * dp, -1, keepdims=True)
-    ds = (probs * (dp - inner)).astype(BRAIN)
-    dq = jnp.einsum("hqk,khd->qhd", ds, k, preferred_element_type=FLOAT) * SCALE
-    dk = jnp.einsum("hqk,qhd->khd", ds, q, preferred_element_type=FLOAT) * SCALE
-    dv = jnp.einsum("hqk,qhd->khd", probs.astype(BRAIN), do, preferred_element_type=FLOAT)
-    return tuple(merge_heads(t).astype(BRAIN) for t in (dq, dk, dv))
+    tall = pl.BlockSpec((q.shape[0], LANES), lambda p: (0, p))
+    short = pl.BlockSpec((k.shape[0], LANES), lambda p: (0, p))
+    return pl.pallas_call(
+        cross_kernel,
+        grid=(q.shape[1] // LANES,),
+        in_specs=[tall, short, short],
+        out_specs=tall,
+        out_shape=jax.ShapeDtypeStruct(q.shape, BRAIN),
+        compiler_params=pltpu.CompilerParams(vmem_limit_bytes=32 * 2**20),
+        name="cross",
+    )(q, k, v)
+
+
+def attend_cross_back(q, k, v, do):
+    tall = pl.BlockSpec((q.shape[0], LANES), lambda p: (0, p))
+    short = pl.BlockSpec((k.shape[0], LANES), lambda p: (0, p))
+    return pl.pallas_call(
+        cross_back_kernel,
+        grid=(q.shape[1] // LANES,),
+        in_specs=[tall, short, short, tall],
+        out_specs=[tall, short, short],
+        out_shape=[jax.ShapeDtypeStruct(t.shape, BRAIN) for t in (q, k, v)],
+        compiler_params=pltpu.CompilerParams(vmem_limit_bytes=32 * 2**20),
+        name="cross_back",
+    )(q, k, v, do)
 
 
 def on_device(
@@ -1036,7 +1076,7 @@
     q2 = dot_nn(h2, w_cq).astype(BRAIN)
     k2 = dot_nn(text, w_ck).astype(BRAIN)
     v2 = dot_nn(text, w_cv).astype(BRAIN)
-    o2, lse2 = attend_cross(split_heads(q2), split_heads(k2), split_heads(v2))
+    o2 = attend_cross(q2, k2, v2)
     x2 = x1 + summed(o2, w_co)
     h3 = both(normalize(x2, gains[4], gains[5]).astype(BRAIN))
     g, slope = gelu_pair(dot_nn(h3, w_fi))
@@ -1059,9 +1099,7 @@
     dx2b = both(dx2.astype(BRAIN))
     co_grad = dot_tn(dx2b, o2).astype(BRAIN)
     do2 = dot_nn(dx2b, w_co).astype(BRAIN)
-    dq2, dk2, dv2 = attend_cross_back(
-        split_heads(q2), split_heads(k2), split_heads(v2), split_heads(do2), lse2
-    )
+    dq2, dk2, dv2 = attend_cross_back(q2, k2, v2, do2)
     cq_grad = dot_tn(h2, dq2).astype(BRAIN)
     ck_grad = dot_tn(text, dk2).astype(BRAIN)
     cv_grad = dot_tn(text, dv2).astype(BRAIN)

time: 1010 us -> 1020 us (level)
  Pallas kernels: 553 us -> 586 us
  matrix products: 238 us -> 216 us
    pallas_call x0 -> x2, Pallas kernels: none -> 28.3 us  [the longest x1 19.1 us: attend_cross_back(): pl.pallas_call(cross_back_kernel, grid=(q.shape[1] // LANES,), in_specs=[...]
    dot_general x6 -> x0, matrix products: 11.2 us -> none  [the longest x1 4.01 us: attend_cross_back(): jnp.einsum('hqk,qhd->khd', probs.astype(BRAIN), do, preferred_element_typ...]
    all_gather x2, waiting for transfers between devices: 37.5 us -> 48.7 us  [on_device(): w_fi, w_fo = (lax.all_gather(v, CHIPS, axis=0, tiled=True) for v in wide)]
  transfers between devices with their start and end apart: 21 -> 21, of which waited for: 11 -> 12; matrix products, arithmetic and copies ran while one was open for 26% -> 22% of each run, Pallas kernels for 55% -> 58%
where the time goes in v6:
time: 1020 us; the launch traced here: 1010 us
  Pallas kernels  586 us (57%)
  matrix products  216 us (21%)
  waiting for transfers between devices  87.1 us (9%)
  other arithmetic  40.1 us (4%)
  starting transfers between devices  30.1 us (3%)
  local copies, waits for them, and re-layouts  28.6 us (3%)
  between operations  21.6 us (2%)
    pallas_call x1, Pallas kernels, sum_gradients(): pl.pallas_call(functools.partial(sum_kernel, slots, count, real), in_spec...  280 us
    pallas_call x1, Pallas kernels, gather(): pl.pallas_call(functools.partial(gather_kernel, slots, count, real), out_...  278 us
    dot_general x12, matrix products, dot_nt(): lax.dot_general(a, b, (((1,), (1,)), ((), ())), preferred_element_type=FL...  86.6 us
    dot_general x7, matrix products, dot_nn(): lax.dot_general(a, b, (((1,), (0,)), ((), ())), preferred_element_type=FL...  69.4 us
    dot_general x7, matrix products, dot_tn(): lax.dot_general(a, b, (((0,), (0,)), ((), ())), preferred_element_type=FL...  59.6 us
    all_gather x2, waiting for transfers between devices, on_device(): w_fi, w_fo = (lax.all_gather(v, CHIPS, axis=0, tiled=True) for v in wide)  48.7 us
    ppermute x12, waiting for transfers between devices, swap_core(): return lax.ppermute(v, 'c', [(0, 1), (1, 0)])  21.6 us
  transfers between devices with their start and end apart: 21, of which 12 were waited for; matrix products, arithmetic and copies ran while one was open for 22% of the time, Pallas kernels for 58%

profile of v6, /device:TPU:1, one launch (start us, length us, event | category | flops | bytes accessed | tf_op | source)
XLA Modules:
  0.0 1009.2 jit_solution(15097397281460225814)
XLA Ops:
  34.6 278.1 %gather.1 = (bf16[4,2,2,96,128]{4,3,2,1,0:T(8,128)(2,1)}, bf16[4,2,2,96,768]{4,3,2,1,0:T(8,128)(2,1)}, bf16[4,2,2,96,768]{4,3,2,1,0:T(8,128)(2,1)}, bf16[4,2,2,9...) custom-call(bf16[96,128]{1,0:T(8,128)(2,1)} %pad.16.refs_0_, ...), custom_call_target="tpu_custom_call" | custom-call | tf_op jit(solution)/shard_map/gather/pallas_call | solution.py:474
  312.8 5.6 convolution_convert_fusion.12
  318.4 7.2 collective-permute-start.3
  330.1 5.4 fusion.52
  341.7 5.5 convolution_convert_fusion.11.q_ref
  347.2 9.1 cross.1
  372.1 24.4 %multiply_convert_fusion.1 = (bf16[1536,3072]{1,0:T(8,128)(2,1)}, f32[1536,3072]{1,0:T(8,128)}) fusion(bf16[1536,3072]{1,0:T(8,128)(2,1)} %all-gather.3.cloned.1.call-done, bf16[768,1536]{1,0:T(8,128)(2,1)} %collective-permute-done.6, bf16[768,1536]{1,0:T(8,128)(2,1)S(1)} %add_convert_fusion), kind=kOutput, calls=%fused_computation.7 | convolution fusion | flops 14528544768 | bytes 42467328 | tf_op jit(solution)/shard_map/dot_general | solution.py:57
  396.5 48.7 %all-gather.5.cloned.1.call-done = bf16[1536,3072]{1,0:T(8,128)(2,1)} async-done(((bf16[96,3072]{1,0:T(8,128)(2,1)}), bf16[1536,3072]{1,0:T(8,128)(2,1)}) %all-gather.5.cloned.1.call-update) | async-done | bytes 9437200 | tf_op jit(solution)/shard_map/all_gather | solution.py:1067
  445.2 12.7 %fusion.15 = bf16[768,1536]{1,0:T(8,128)(2,1)} fusion(bf16[1536,3072]{1,0:T(8,128)(2,1)} %all-gather.5.cloned.1.call-done, bf16[1536,3072]{1,0:T(8,128)(2,1)} %get-tuple-element.191), kind=kOutput, calls=%fused_computation.60 | convolution fusion | flops 7248936960 | bytes 16515072 | tf_op jit(solution)/shard_map/dot_general | solution.py:53
  464.1 14.5 %fusion.6 = (f32[]{:T(128)}, f32[768,1536]{1,0:T(8,128)S(1)}) fusion(f32[768]{0:T(1024)S(1)} %get-tuple-element.164, bf16[768,1664]{1,0:T(8,128)(2,1)S(1)} %copy-done.11, f32[768,1536]{1,0:T(8,128)} %copy-done.9, bf16[768,1536]{1,0:T(8,128)(2,1)} %collective-permute-done.7, bf16[1536,3072]{1,0:T(8,128)(2,1)} %all-gather.5.cloned.1.call-done, ...), kind=kOutput, calls=%fused_computation.14 | convolution fusion | flops 7257194496 | bytes 28314628 | tf_op jit(solution)/shard_map/dot_general | solution.py:53
  487.0 17.8 %convolution_convert_fusion.1 = bf16[1536,3072]{1,0:T(8,128)(2,1)} fusion(bf16[1536,3072]{1,0:T(8,128)(2,1)S(1)} %copy-done.70, bf16[768,1536]{1,0:T(8,128)(2,1)S(1)} %collective-permute-done.8, bf16[768,1536]{1,0:T(8,128)(2,1)S(1)} %multiply_convert_fusion.2), kind=kOutput, calls=%fused_computation.10 | convolution fusion | flops 14509670400 | bytes 23592960 | tf_op jit(solution)/shard_map/dot_general | solution.py:61
  509.7 25.2 %multiply_convert_fusion = bf16[1536,3072]{1,0:T(8,128)(2,1)S(1)} fusion(f32[1536,3072]{1,0:T(8,128)} %get-tuple-element.192, bf16[1536,1536]{1,0:T(8,128)(2,1)} %pad_maximum_fusion.2, bf16[1536,3072]{1,0:T(8,128)(2,1)} %all-gather.5.cloned.1.call-done), kind=kOutput, calls=%fused_computation.6 | convolution fusion | flops 14552137728 | bytes 42467328 | tf_op jit(solution)/shard_map/dot_general | solution.py:57
  535.0 14.8 %fusion.18 = bf16[768,1536]{1,0:T(8,128)(2,1)} fusion(bf16[1536,3072]{1,0:T(8,128)(2,1)} %all-gather.3.cloned.1.call-done, bf16[1536,3072]{1,0:T(8,128)(2,1)S(1)} %multiply_convert_fusion), kind=kOutput, calls=%fused_computation.61 | convolution fusion | flops 7248936960 | bytes 16515072 | tf_op jit(solution)/shard_map/dot_general | solution.py:53
  550.1 19.1 %convolution_convert_fusion = bf16[1536,3072]{1,0:T(8,128)(2,1)} fusion(bf16[1536,3072]{1,0:T(8,128)(2,1)S(1)} %multiply_convert_fusion, bf16[768,1536]{1,0:T(8,128)(2,1)} %collective-permute-done.6, bf16[768,1536]{1,0:T(8,128)(2,1)S(1)} %copy-done.24), kind=kOutput, calls=%fused_computation.9 | convolution fusion | flops 14509670400 | bytes 23592960 | tf_op jit(solution)/shard_map/dot_general | solution.py:61
  569.9 15.2 %multiply_reduce_fusion = (f32[1536]{0:T(1024)S(1)}, f32[768]{0:T(1024)S(1)}, f32[768]{0:T(1024)S(1)}, f32[1536]{0:T(1024)S(1)}, f32[768,1536]{1,0:T(8,128)S(1)}) fusion(f32[768,1536]{1,0:T(8,128)} %copy-done.9, f32[768]{0:T(1024)S(1)} %copy-done.52, f32[768]{0:T(1024)S(1)} %copy-done.48, bf16[768,1536]{1,0:T(8,128)(2,1)} %collective-permute-done.9, ...), kind=kOutput, calls=%fused_computation.28 | convolution fusion | flops 7260728832 | bytes 25982976 | tf_op jit(solution)/shard_map/dot_general | solution.py:53
  585.2 9.2 fusion.50
  599.0 5.5 convolution_convert_fusion.8.do_ref
  604.6 19.1 %cross_back.1 = (bf16[1536,768]{1,0:T(8,128)(2,1)S(1)}, bf16[64,768]{1,0:T(8,128)(2,1)S(1)}, bf16[64,768]{1,0:T(8,128)(2,1)S(1)}) custom-call(bf16[1536,768]{1,0:T(8,128)(2,1)S(1)} %copy-done.1, bf16[64,768]{1,0:T(8,128)(2,1)S(1)} %copy-done.7, bf16[64,768]{1,0:T(8,128)(2,1)S(1)} %copy-done.5, bf16[1536,768]{1,0:T(8,128)(2,1)S(1)} %convolution_convert_fusion.8.do_ref), custom_call_target="tpu_custom_call" | custom-call | tf_op jit(solution)/shard_map/cross_back/pallas_call | solution.py:1002
  633.0 5.6 multiply_reduce_fusion.1
  663.9 7.8 convolution_convert_fusion.4.refs_9_
  671.7 7.8 convolution_convert_fusion.5
  679.5 279.7 %sum_gradients.1 = (bf16[96,768]{1,0:T(8,128)(2,1)}, bf16[96,768]{1,0:T(8,128)(2,1)}, bf16[96,768]{1,0:T(8,128)(2,1)}, bf16[96,768]{1,0:T(8,128)(2,1)}, bf16[96,...) custom-call(bf16[4,2,2,96,768]{4,3,2,1,0:T(8,128)(2,1)} %bitcast.100, ...), custom_call_target="tpu_custom_call" | custom-call | tf_op jit(solution)/shard_map/sum_gradients/pallas_call | solution.py:881
  963.8 9.3 copy.57
  994.8 5.2 collective-permute-done.15
  (269 shorter events, 135.1 us)
Async XLA Ops:
  7.3 364.8 %all-gather.3.cloned.1.call-start = ((), (), s32[]{:S(2)}) async-start(), calls=%async_computation.2 | async-start | bytes 10027008 | tf_op jit(solution)/shard_map/all_gather | solution.py:1067
  7.3 12.7 %collective-permute-start.1 = (bf16[96,3072]{1,0:T(8,128)(2,1)}, bf16[96,3072]{1,0:T(8,128)(2,1)}, u32[]{:S(2)}, u32[]{:S(2)}) collective-permute-start(bf16[96,3072]{1,0:T(8,128)(2,1)} %bitcast.105), channel_id=1, source_target_pairs={{1,2},{2,1},{5,6},{6,5},{9,10},{10,9},{13,14},{14,13},{17,18},{18,... | collective-permute-start | bytes 1769480 | tf_op jit(solution)/shard_map/ppermute | solution.py:33
  12.1 14.2 %collective-permute-start = (bf16[96,3072]{1,0:T(8,128)(2,1)}, bf16[96,3072]{1,0:T(8,128)(2,1)}, u32[]{:S(2)}, u32[]{:S(2)}) collective-permute-start(bf16[96,3072]{1,0:T(8,128)(2,1)} %param.38), channel_id=1, source_target_pairs={{1,2},{2,1},{5,6},{6,5},{9,10},{10,9},{13,14},{14,13},{17,18},{18,... | collective-permute-start | bytes 1769480 | tf_op jit(solution)/shard_map/ppermute | solution.py:33
  28.3 416.9 %all-gather.5.cloned.1.call-start = ((), (), s32[]{:S(2)}) async-start(), calls=%async_computation.3 | async-start | bytes 10027008 | tf_op jit(solution)/shard_map/all_gather | solution.py:1067
  318.4 11.7 %collective-permute-start.3 = (bf16[768,1536]{1,0:T(8,128)(2,1)}, bf16[768,1536]{1,0:T(8,128)(2,1)}, u32[]{:S(2)}, u32[]{:S(2)}) collective-permute-start(bf16[768,1536]{1,0:T(8,128)(2,1)} %convolution_convert_fusion.12), channel_id=1, source_target_pairs={{0,2},{2,0},{1,3},{3,1},{4,6},{6,4},{5,7},{7,5},{8,10},{10,8},{9,1... | collective-permute-start | bytes 7077896 | tf_op jit(solution)/shard_map/ppermute | solution.py:25
  325.6 656.6 %reduce-scatter.5.cloned.1.call-start = ((), (), s32[]{:S(2)}) async-start(), calls=%async_computation.5 | async-start | bytes 10027008 | tf_op jit(solution)/shard_map/reduce_scatter | solution.py:1093
  326.1 39.8 %copy-start.43 = (f32[1536]{0:T(1024)}, f32[1536]{0:T(1024)S(1)}, u32[]{:S(2)}) copy-start(f32[1536]{0:T(1024)S(1)} %get-tuple-element.167) | copy-start | bytes 18436
  335.5 27.6 %copy-start.8 = (f32[768,1536]{1,0:T(8,128)}, f32[768,1536]{1,0:T(8,128)S(1)}, u32[]{:S(2)}) copy-start(f32[768,1536]{1,0:T(8,128)S(1)} %get-tuple-element.188) | copy-start | bytes 14155780
  337.0 4.6 collective-permute-start.4
  358.4 4.6 collective-permute-start.5
  367.4 29.1 %copy-start.23 = (bf16[768,1536]{1,0:T(8,128)(2,1)}, bf16[768,1536]{1,0:T(8,128)(2,1)S(1)}, u32[]{:S(2)}) copy-start(bf16[768,1536]{1,0:T(8,128)(2,1)S(1)} %add_convert_fusion) | copy-start | bytes 7077892
  367.4 4.7 collective-permute-start.6
  457.8 6.3 collective-permute-start.7
  461.2 2.0 collective-permute-start.2
  481.0 4.5 collective-permute-start.8
  509.7 477.0 %reduce-scatter.3.cloned.1.call-start = ((), (), s32[]{:S(2)}) async-start(), calls=%async_computation.4 | async-start | bytes 10027008 | tf_op jit(solution)/shard_map/reduce_scatter | solution.py:1096
  549.8 19.5 %collective-permute-start.9 = (bf16[768,1536]{1,0:T(8,128)(2,1)}, bf16[768,1536]{1,0:T(8,128)(2,1)}, u32[]{:S(2)}, u32[]{:S(2)}) collective-permute-start(bf16[768,1536]{1,0:T(8,128)(2,1)} %fusion.18), channel_id=1, source_target_pairs={{0,2},{2,0},{1,3},{3,1},{4,6},{6,4},{5,7},{7,5},{8,10},{10,8},{9,1... | collective-permute-start | bytes 7077896 | tf_op jit(solution)/shard_map/ppermute | solution.py:25
  594.4 4.7 collective-permute-start.10
  627.2 5.8 collective-permute-start.11
  632.8 23.0 %collective-permute-start.13 = (bf16[64,768]{1,0:T(8,128)(2,1)S(1)}, bf16[64,768]{1,0:T(8,128)(2,1)S(1)}, u32[]{:S(2)}, u32[]{:S(2)}) collective-permute-start(bf16[64,768]{1,0:T(8,128)(2,1)S(1)} %broadcast_select_fusion.2), channel_id=1, source_target_pairs={{0,2},{2,0},{1,3},{3,1},{4,6},{6,4},{5,7},{7,5},{8,10},{10,8},{9,1... | collective-permute-start | bytes 294920 | tf_op jit(solution)/shard_map/ppermute | solution.py:25
  642.8 21.1 %collective-permute-start.12 = (bf16[768,1536]{1,0:T(8,128)(2,1)}, bf16[768,1536]{1,0:T(8,128)(2,1)}, u32[]{:S(2)}, u32[]{:S(2)}) collective-permute-start(bf16[768,1536]{1,0:T(8,128)(2,1)} %get-tuple-element.172), channel_id=1, source_target_pairs={{0,2},{2,0},{1,3},{3,1},{4,6},{6,4},{5,7},{7,5},{8,10},{10,8},{9,1... | collective-permute-start | bytes 7077896 | tf_op jit(solution)/shard_map/ppermute | solution.py:25
  655.9 5.9 collective-permute-start.14
  982.2 11.5 %collective-permute-start.16 = (bf16[96,3072]{1,0:T(8,128)(2,1)}, bf16[96,3072]{1,0:T(8,128)(2,1)S(1)}, u32[]{:S(2)}, u32[]{:S(2)}) collective-permute-start(bf16[96,3072]{1,0:T(8,128)(2,1)} %reduce-scatter.5.cloned.1.call-done), channel_id=1, source_target_pairs={{1,2},{2,1},{5,6},{6,5},{9,10},{10,9},{13,14},{14,13},{17,18},{18,... | collective-permute-start | bytes 1769480 | tf_op jit(solution)/shard_map/ppermute | solution.py:33
  986.7 13.3 %collective-permute-start.15 = (bf16[96,3072]{1,0:T(8,128)(2,1)}, bf16[96,3072]{1,0:T(8,128)(2,1)S(1)}, u32[]{:S(2)}, u32[]{:S(2)}) collective-permute-start(bf16[96,3072]{1,0:T(8,128)(2,1)} %reduce-scatter.3.cloned.1.call-done), channel_id=1, source_target_pairs={{1,2},{2,1},{5,6},{6,5},{9,10},{10,9},{13,14},{14,13},{17,18},{18,... | collective-permute-start | bytes 1769480 | tf_op jit(solution)/shard_map/ppermute | solution.py:33
  (75 other events, 765.7 us)
Sparse Core Ops, SparseCore 0:
  28.4 180.6 all-gather.2
  325.7 119.4 all-gather.4
  509.8 167.7 reduce-scatter.4
  684.0 267.8 reduce-scatter.2
